TPU v7x, 256 devices: a whole 4x4x8 slice. The times are simulated.
256 devices in a mesh: stream: 8 (over z_lo, x), span: 32 (over z_hi, y, core).
Axes of the slice: x: 4, y: 4, z: 8 (z_hi: 4, z_lo: 2; z = z_hi * 2 + z_lo), core: 2. Of those that a mesh axis runs over, the one named last changes fastest.
Arguments:
- fields: float32 [1, 96, 384, 1024], P(None, 'stream', 'span'), may hold values from -6 to 6
Outputs:
- coefficients: float32 [1, 96, 384, 1024], P(None, 'stream', 'span')
All inputs are finite; a program needn't handle non-finite values.
Results may differ from a plain program's by a relative error of at most 0.00002.
Values sent between devices are 32-bit elements; how exact they have to be, the bound alone decides.
No kernel may reach another device: no remote copies, remote signals or barrier semaphores. Data moves between devices by JAX's collectives and lax.ppermute only.
A program may use at most 128 MiB of HBM per device.

v0:
```python
import jax
import jax.numpy as jnp
from jax import lax
from jax.sharding import PartitionSpec as P


def with_halo(cells, sides, width):
    for axis, dim in sides:
        count = lax.axis_size(axis)
        head = lax.slice_in_dim(cells, 0, width, axis=dim)
        tail = lax.slice_in_dim(cells, cells.shape[dim] - width, cells.shape[dim], axis=dim)
        cells = jnp.concatenate(
            [
                lax.ppermute(tail, axis, [(i, (i + 1) % count) for i in range(count)]),
                cells,
                lax.ppermute(head, axis, [((i + 1) % count, i) for i in range(count)]),
            ],
            axis=dim,
        )
    return cells


def take(array, axis, start, stop, step=1):
    return lax.slice_in_dim(array, start, stop, step, axis)


def lift_ext(ext, axis):
    pairs = (ext.shape[axis] - 12) // 2
    evens = take(ext, axis, 0, ext.shape[axis], 2)
    odds = take(ext, axis, 1, ext.shape[axis], 2)
    detail = take(odds, axis, 1, pairs + 4) - (
        0.5625 * (take(evens, axis, 1, pairs + 4) + take(evens, axis, 2, pairs + 5))
        - 0.0625 * (take(evens, axis, 0, pairs + 3) + take(evens, axis, 3, pairs + 6))
    )
    smooth = take(evens, axis, 3, pairs + 3) + (
        0.28125 * (take(detail, axis, 1, pairs + 1) + take(detail, axis, 2, pairs + 2))
        - 0.03125 * (take(detail, axis, 0, pairs) + take(detail, axis, 3, pairs + 3))
    )
    kept = take(detail, axis, 2, pairs + 2)
    joined = jnp.stack([smooth, kept], axis + 1)
    shape = list(smooth.shape)
    shape[axis] = 2 * pairs
    return joined.reshape(shape)


def wrap_local(array, axis):
    length = array.shape[axis]
    return jnp.concatenate(
        [take(array, axis, length - 6, length), array, take(array, axis, 0, 6)], axis
    )


def along_lines(items):
    lifted = lift_ext(wrap_local(items, 2), 2)
    return lax.all_to_all(lifted, "span", split_axis=2, concat_axis=3, tiled=True)


def span_lift(array):
    return along_lines(lax.all_to_all(array, "span", split_axis=3, concat_axis=2, tiled=True))


def level(array):
    extended = with_halo(array, (("stream", 1),), 6)
    array = lift_ext(extended, 1)
    array = span_lift(array)
    return lift_ext(wrap_local(array, 3), 3)


def local(fields):
    first = level(fields)
    coarse = level(first[:, ::2, ::2, ::2])
    return first.at[:, ::2, ::2, ::2].set(coarse)


def solution(mesh):
    return jax.shard_map(
        local,
        mesh=mesh,
        in_specs=(P(None, "stream", "span", None),),
        out_specs=P(None, "stream", "span", None),
        check_vma=False,
    )
```

profile of v0, /device:TPU:1, one launch (start us, length us, event | category | flops | bytes accessed | tf_op | source)
XLA Modules:
  0.0 399.1 jit_solution(7347887136343011131)
XLA Ops:
  0.0 1.5 fusion.56
  1.5 2.1 collective-permute-start
  3.6 2.7 collective-permute-start.1
  6.4 4.8 %collective-permute-done = f32[1,6,12,1024]{3,0,2,1:T(1,128)S(1)} collective-permute-done((f32[1,6,12,1024]{3,0,2,1:T(1,128)S(1)}, f32[1,6,12,1024]{3,0,2,1:T(1,128)S(1)}, u32[]{:S(2)}, u32[]{:S(2)}) %collective-permute-start) | collective-permute-done | bytes 294944 | tf_op jit(solution)/shard_map/ppermute | solution.py:14
  15.0 6.4 %copy.132 = f32[1,12,12,1024]{2,1,0,3:T(8,128)} copy(f32[1,12,12,1024]{3,0,2,1:T(1,128)S(1)} %bitcast.81) | data formatting | bytes 1179648 | tf_op jit(solution)/shard_map/reshape | solution.py:43
  21.5 6.4 %reshape.52 = f32[32,1,4608]{2,1,0:T(1,128)S(1)} reshape(f32[1024,1,12,12]{3,2,1,0:T(8,128)} %bitcast.67) | data formatting | bytes 1179648
  27.8 33.1 %all_to_all.72 = f32[32,1,4608]{2,1,0:T(1,128)S(1)} all-to-all(f32[32,1,4608]{2,1,0:T(1,128)S(1)} %reshape.52), channel_id=1, replica_groups=mesh['stream'=8,'span'=32] {'span'}, dimensions={0} | all-to-all | bytes 1179648 | tf_op jit(solution)/shard_map/all_to_all | solution.py:59
  61.5 2.0 reduce.6
  63.5 5.5 %reshape.53 = f32[1024,1,12,12]{3,2,1,0:T(8,128)} reshape(f32[32,4608]{1,0:T(8,128)S(1)} %reduce.6) | data formatting | bytes 1179648
  69.0 7.0 %copy.158 = f32[1,12,12,32,32]{4,3,0,2,1:T(8,128)} copy(f32[1,12,12,32,32]{2,1,4,3,0:T(8,128)} %bitcast.68) | data formatting | bytes 1179648 | tf_op jit(solution)/shard_map/all_to_all | solution.py:59
  76.1 4.1 %copy.134 = f32[1,12,32,12,32]{4,0,3,2,1:T(1,128)S(1)} copy(f32[1,12,32,12,32]{4,2,0,3,1:T(8,128)} %bitcast.76) | data formatting | bytes 1179648 | tf_op jit(solution)/shard_map/all_to_all | solution.py:59
  82.0 10.3 %slice.271 = f32[1,12,198,32]{2,3,1,0:T(8,128)S(1)} slice(f32[1,12,396,32]{2,3,1,0:T(8,128)S(1)} %pad_maximum_fusion), slice={[0:1:1], [0:12:1], [0:396:2], [0:32:1]} | slice | bytes 608256 | tf_op jit(solution)/shard_map/slice | solution.py:24
  92.2 10.5 %slice.273 = f32[1,12,198,32]{2,3,1,0:T(8,128)S(1)} slice(f32[1,12,396,32]{2,3,1,0:T(8,128)S(1)} %pad_maximum_fusion), slice={[0:1:1], [0:12:1], [1:396:2], [0:32:1]} | slice | bytes 608256 | tf_op jit(solution)/shard_map/slice | solution.py:24
  105.0 3.8 copy.163
  108.9 8.2 %reduce.7 = f32[384,12,32]{2,1,0:T(8,128)S(1)} reduce(f32[384,12,1,32]{3,2,1,0:T(1,128)} %bitcast.73, f32[]{:T(128)} %broadcast.16), dimensions={2}, to_apply=%bitcast.65.reduce_sub_computation | reduce | bytes 1179652
  117.1 2.0 reshape.54
  119.1 5.4 %all-to-all-start.1 = ((f32[32,1,4608]{2,1,0:T(1,128)}), f32[32,1,4608]{2,1,0:T(1,128)S(1)}, u32[]{:S(2)}, u32[]{:S(2)}) async-start(f32[32,1,4608]{2,1,0:T(1,128)} %reshape.54), calls=%async_computation.1 | async-start | bytes 1179648 | tf_op jit(solution)/shard_map/all_to_all | solution.py:55
  124.6 19.5 %all-to-all-done.1 = f32[32,1,4608]{2,1,0:T(1,128)S(1)} async-done(((f32[32,1,4608]{2,1,0:T(1,128)}), f32[32,1,4608]{2,1,0:T(1,128)S(1)}, u32[]{:S(2)}, u32[]{:S(2)}) %all-to-all-start.1) | async-done | bytes 589856 | tf_op jit(solution)/shard_map/all_to_all | solution.py:55
  144.1 2.0 reduce.8
  146.1 3.9 reshape.55
  150.0 2.2 copy.140
  153.8 2.8 concatenate.23
  156.7 14.8 %slice.285 = f32[1,12,12,518]{3,0,2,1:T(1,128)S(1)} slice(f32[1,12,12,1036]{3,0,2,1:T(1,128)S(1)} %concatenate.23), slice={[0:1:1], [0:12:1], [0:12:1], [0:1036:2]} | slice | bytes 596736 | tf_op jit(solution)/shard_map/slice | solution.py:24
  171.5 15.1 %slice.287 = f32[1,12,12,518]{3,0,2,1:T(1,128)S(1)} slice(f32[1,12,12,1036]{3,0,2,1:T(1,128)S(1)} %concatenate.23), slice={[0:1:1], [0:12:1], [0:12:1], [1:1036:2]} | slice | bytes 596736 | tf_op jit(solution)/shard_map/slice | solution.py:24
  186.6 3.1 slice_subtract_fusion.1
  189.7 2.5 fusion.18
  192.7 6.5 %copy.143 = f32[1,12,12,512,2]{2,4,3,1,0:T(2,128)} copy(f32[1,12,12,512,2]{3,0,4,2,1:T(1,128)S(1)} %pad_maximum_fusion.3) | data formatting | bytes 1179648 | tf_op jit(solution)/shard_map/stack | solution.py:40
  199.2 11.6 %slice.297 = f32[1,6,6,512]{2,3,1,0:T(8,128)S(1)} slice(f32[1,12,12,1024]{2,3,1,0:T(8,128)} %bitcast.69), slice={[0:1:1], [0:12:2], [0:12:2], [0:1024:2]} | slice | bytes 147456 | tf_op jit(solution)/shard_map/slice | solution.py:71
  211.4 3.6 collective-permute-start.3
  214.9 2.0 collective-permute-done.2
  217.5 3.1 copy.147
  220.5 6.0 %reduce.9 = f32[512,6,6]{2,1,0:T(8,128)S(1)} reduce(f32[512,6,1,6]{3,2,1,0:T(1,128)} %bitcast.78, f32[]{:T(128)} %broadcast.16), dimensions={2}, to_apply=%bitcast.58.reduce_sub_computation | reduce | bytes 147460
  226.5 1.7 reshape.56
  228.2 6.2 %all-to-all-start.2 = ((f32[32,1,576]{2,1,0:T(1,128)}), f32[32,1,576]{2,1,0:T(1,128)S(1)}, u32[]{:S(2)}, u32[]{:S(2)}) async-start(f32[32,1,576]{2,1,0:T(1,128)} %reshape.56), calls=%async_computation.2 | async-start | bytes 163840 | tf_op jit(solution)/shard_map/all_to_all | solution.py:59
  234.8 9.4 %all-to-all-done.2 = f32[32,1,576]{2,1,0:T(1,128)S(1)} async-done(((f32[32,1,576]{2,1,0:T(1,128)}), f32[32,1,576]{2,1,0:T(1,128)S(1)}, u32[]{:S(2)}, u32[]{:S(2)}) %all-to-all-start.2) | async-done | bytes 73760 | tf_op jit(solution)/shard_map/all_to_all | solution.py:59
  245.0 3.6 reshape.57
  248.6 5.7 %bitcast_reduce_fusion = f32[6,6,512]{1,0,2:T(8,128)S(1)} fusion(f32[512,6,1,6]{3,2,1,0:T(1,128)} %reshape.57), kind=kLoop, calls=%fused_computation.116 | loop fusion | bytes 147456 | tf_op jit(solution)/shard_map/all_to_all | solution.py:59
  254.4 1.6 copy.160
  259.1 1.4 slice.314
  261.6 2.1 reduce.11
  264.7 4.2 %all-to-all-start.3 = ((f32[32,1,576]{2,1,0:T(1,128)}), f32[32,1,576]{2,1,0:T(1,128)S(1)}, u32[]{:S(2)}, u32[]{:S(2)}) async-start(f32[32,1,576]{2,1,0:T(1,128)} %reshape.58), calls=%async_computation.3 | async-start | bytes 163840 | tf_op jit(solution)/shard_map/all_to_all | solution.py:55
  268.9 18.0 %copy.142 = f32[1,12,12,512,2]{4,3,2,1,0:T(8,128)} copy(f32[1,12,12,512,2]{3,0,4,2,1:T(1,128)S(1)} %pad_maximum_fusion.3) | data formatting | bytes 1179648 | tf_op jit(solution)/shard_map/stack | solution.py:40
  286.9 26.9 %reshape.39 = f32[147456]{0:T(1024)S(1)} reshape(f32[1,12,12,512,2]{4,3,2,1,0:T(8,128)} %copy.142) | data formatting | bytes 1179648
  316.7 2.6 slice.326
  319.3 2.5 slice.328
  322.8 2.9 copy.157
  325.7 4.3 %reshape.43 = f32[18432]{0:T(1024)S(1)} reshape(f32[1,6,6,256,2]{4,3,2,1,0:T(8,128)} %copy.157) | data formatting | bytes 147456 | tf_op jit(solution)/shard_map/reshape | solution.py:43
  330.0 68.1 %scatter_fusion = f32[147456]{0:T(1024)S(1)} fusion(f32[147456]{0:T(1024)S(1)} %reshape.39, s32[18432]{0:T(1024)S(1)} %reshape.41, f32[18432]{0:T(1024)S(1)} %reshape.43), kind=kCustom, calls=%fused_computation | custom fusion | bytes 294912
  (72 shorter events, 22.5 us)
Async XLA Ops:
  0.0 11.2 %copy-start.1 = (f32[1,12,12,1024]{3,0,2,1:T(1,128)S(1)}, f32[1,12,12,1024]{3,0,2,1:T(1,128)}, u32[]{:S(2)}) copy-start(f32[1,12,12,1024]{3,0,2,1:T(1,128)} %param.1) | copy-start | bytes 1769476
  1.5 9.6 %collective-permute-start = (f32[1,6,12,1024]{3,0,2,1:T(1,128)S(1)}, f32[1,6,12,1024]{3,0,2,1:T(1,128)S(1)}, u32[]{:S(2)}, u32[]{:S(2)}) collective-permute-start(f32[1,6,12,1024]{3,0,2,1:T(1,128)S(1)} %get-tuple-element.14), channel_id=1, source_target_pairs={{0,32},{32,64},{64,96},{96,128},{128,160},{160,192},{192,224},{224... | collective-permute-start | bytes 884744 | tf_op jit(solution)/shard_map/ppermute | solution.py:14
  3.6 8.0 %collective-permute-start.1 = (f32[1,6,12,1024]{3,0,2,1:T(1,128)S(1)}, f32[1,6,12,1024]{3,0,2,1:T(1,128)S(1)}, u32[]{:S(2)}, u32[]{:S(2)}) collective-permute-start(f32[1,6,12,1024]{3,0,2,1:T(1,128)S(1)} %get-tuple-element.13), channel_id=1, source_target_pairs={{32,0},{64,32},{96,64},{128,96},{160,128},{192,160},{224,192},{0,2... | collective-permute-start | bytes 884744 | tf_op jit(solution)/shard_map/ppermute | solution.py:16
  119.1 25.0 %all-to-all-start.1 = ((f32[32,1,4608]{2,1,0:T(1,128)}), f32[32,1,4608]{2,1,0:T(1,128)S(1)}, u32[]{:S(2)}, u32[]{:S(2)}) async-start(f32[32,1,4608]{2,1,0:T(1,128)} %reshape.54), calls=%async_computation.1 | async-start | bytes 1179648 | tf_op jit(solution)/shard_map/all_to_all | solution.py:55
  211.3 5.6 %collective-permute-start.2 = (f32[1,6,6,512]{3,0,2,1:T(1,128)S(1)}, f32[1,6,6,512]{3,0,2,1:T(1,128)S(1)}, u32[]{:S(2)}, u32[]{:S(2)}) collective-permute-start(f32[1,6,6,512]{3,0,2,1:T(1,128)S(1)} %copy.144), channel_id=1, source_target_pairs={{0,32},{32,64},{64,96},{96,128},{128,160},{160,192},{192,224},{224... | collective-permute-start | bytes 221192 | tf_op jit(solution)/shard_map/ppermute | solution.py:14
  211.4 5.6 %collective-permute-start.3 = (f32[1,6,6,512]{3,0,2,1:T(1,128)S(1)}, f32[1,6,6,512]{3,0,2,1:T(1,128)S(1)}, u32[]{:S(2)}, u32[]{:S(2)}) collective-permute-start(f32[1,6,6,512]{3,0,2,1:T(1,128)S(1)} %copy.144), channel_id=1, source_target_pairs={{32,0},{64,32},{96,64},{128,96},{160,128},{192,160},{224,192},{0,2... | collective-permute-start | bytes 221192 | tf_op jit(solution)/shard_map/ppermute | solution.py:16
  226.5 8.1 %copy-start.3 = (s32[3]{0:T(128)S(1)}, s32[3]{0:T(128)}, u32[]{:S(2)}) copy-start(s32[3]{0:T(128)} %constant.1) | copy-start | bytes 40
  226.5 8.2 %copy-start.2 = (s32[3]{0:T(128)S(1)}, s32[3]{0:T(128)}, u32[]{:S(2)}) copy-start(s32[3]{0:T(128)} %constant.4) | copy-start | bytes 40
  228.2 16.0 %all-to-all-start.2 = ((f32[32,1,576]{2,1,0:T(1,128)}), f32[32,1,576]{2,1,0:T(1,128)S(1)}, u32[]{:S(2)}, u32[]{:S(2)}) async-start(f32[32,1,576]{2,1,0:T(1,128)} %reshape.56), calls=%async_computation.2 | async-start | bytes 163840 | tf_op jit(solution)/shard_map/all_to_all | solution.py:59
  264.7 49.1 %all-to-all-start.3 = ((f32[32,1,576]{2,1,0:T(1,128)}), f32[32,1,576]{2,1,0:T(1,128)S(1)}, u32[]{:S(2)}, u32[]{:S(2)}) async-start(f32[32,1,576]{2,1,0:T(1,128)} %reshape.58), calls=%async_computation.3 | async-start | bytes 163840 | tf_op jit(solution)/shard_map/all_to_all | solution.py:55
  398.1 0.8 copy-start
where the time goes:
time: 406 us; the launch traced here: 399 us
  local copies, waits for them, and re-layouts  271 us (67%)
  waiting for transfers between devices  35.7 us (9%)
  other arithmetic  34.2 us (8%)
  blocking collectives  33.1 us (8%)
  starting transfers between devices  24.3 us (6%)
    unnamed x21, local copies, waits for them, and re-layouts  121 us
    slice x18, local copies, waits for them, and re-layouts, take(): return lax.slice_in_dim(array, start, stop, step, axis)  60.2 us
    all_to_all x1, blocking collectives, span_lift(): lax.all_to_all(array, 'span', split_axis=3, concat_axis=2, tiled=True)  33.1 us
    another operation x5, local copies, waits for them, and re-layouts, lift_ext(): joined = jnp.stack([smooth, kept], axis + 1)  28.8 us
    all_to_all x8, local copies, waits for them, and re-layouts, span_lift(): lax.all_to_all(array, 'span', split_axis=3, concat_axis=2, tiled=True)  21.5 us
    all_to_all x2, waiting for transfers between devices, along_lines(): lax.all_to_all(lifted, 'span', split_axis=2, concat_axis=3, tiled=True)  19.5 us
    reshape x5, local copies, waits for them, and re-layouts, lift_ext(): return joined.reshape(shape)  18.2 us
    unnamed x6, other arithmetic  16.5 us
  transfers between devices with their start and end apart: 7, of which 4 were waited for; matrix products, arithmetic and copies ran while one was open for 11% of the time, Pallas kernels for 0%

commit v1 on v0

v1 whole, which is shorter than its diff:
```python
import functools

import jax
import jax.numpy as jnp
from jax import lax
from jax.experimental import pallas as pl
from jax.experimental.pallas import tpu as pltpu
from jax.sharding import PartitionSpec as P

NEAR_D, FAR_D = 0.5625, 0.0625
NEAR_S, FAR_S = 0.28125, 0.03125
PLANES, ROWS, CELLS, LANES = 12, 12, 1024, 128
TILES = CELLS // LANES
PAIRS = ROWS // 2


def total(a, b):
    return b if a is None else a if b is None else a + b


def scaled(factor, a):
    return None if a is None else factor * a


def near_far(near, far, a, b, c, d):
    return total(scaled(near, total(a, b)), scaled(far, total(c, d)))


def lift(left, cells, right):
    pairs = len(cells) // 2
    e = {i: cells[2 * i] for i in range(pairs)}
    o = {i: cells[2 * i + 1] for i in range(pairs)}
    if left is not None:
        o[-2], e[-1], o[-1] = left
    if right is not None:
        e[pairs], o[pairs], e[pairs + 1] = right
    d = {
        j: total(o.get(j), near_far(-NEAR_D, FAR_D, e.get(j), e.get(j + 1), e.get(j - 1), e.get(j + 2)))
        for j in range(-2, pairs + 1)
    }
    s = [
        total(e[i], near_far(NEAR_S, -FAR_S, d[i - 1], d[i], d[i - 2], d[i + 1]))
        for i in range(pairs)
    ]
    return s, [d[i] for i in range(pairs)]


def edge_right(c):
    return [
        total(c[-3], near_far(-NEAR_D, FAR_D, c[-4], None, c[-6], None)),
        c[-2],
        total(c[-1], scaled(FAR_D, c[-4])),
    ]


def edge_left(c):
    return [c[0], total(c[1], scaled(FAR_D, c[4])), c[2]]


def coarse_terms(c):
    zeros = [None] * len(c)
    to_right, _ = lift(edge_right(c), zeros, None)
    to_left, _ = lift(None, zeros, edge_left(c))
    return to_right, to_left


def plus(a, b):
    return [total(x, y) for x, y in zip(a, b)]


def interleaved(s, d):
    return [row for pair in zip(s, d) for row in pair]


def lane(shape):
    return lax.broadcasted_iota(jnp.int32, shape, len(shape) - 1)


def lift_lanes(v, step):
    n = v.shape[-1]
    at = lane(v.shape) & (2 * step - 1)
    roll = lambda x, k: pltpu.roll(x, (k * step) % n, axis=v.ndim - 1)
    d = v - (NEAR_D * (roll(v, 1) + roll(v, -1)) - FAR_D * (roll(v, 3) + roll(v, -3)))
    w = jnp.where(at == step, d, v)
    s = w + (NEAR_S * (roll(w, 1) + roll(w, -1)) - FAR_S * (roll(w, 3) + roll(w, -3)))
    return jnp.where(at == 0, s, w)


def packed(a, b):
    return jnp.where((lane(a.shape) & 1) == 0, a, pltpu.roll(b, 1, axis=b.ndim - 1))


def unpacked_odd(p):
    return pltpu.roll(p, p.shape[-1] - 1, axis=p.ndim - 1)


def cut(t):
    return pl.ds(t * LANES, LANES)


Y_ROWS, Y_FAR, X_ROWS, X_FAR = 56, 16, 56, 8


def span_edges(a_ref, b_ref, t):
    a = [a_ref[t, pl.ds(y, PLANES, stride=16), :] for y in range(ROWS)]
    b = [b_ref[t, pl.ds(y, PAIRS, stride=16), :] for y in range(ROWS)]
    return a, b


def put_rows(ref, start, rows, t):
    for row in rows:
        ref[pl.ds(start, row.shape[0]), cut(t)] = row
        start += row.shape[0]
    return start


def first_kernel(f_ref, a_ref, b_ref, near_ref, other_ref, far_ref):
    odd_core = lax.axis_index("span") % 2 == 1
    for k in range(PAIRS):
        lows = []
        for x in (2 * k, 2 * k + 1):
            a = lift_lanes(f_ref[x], 1)
            lows.append(lift_lanes(a, 2))
            for t in range(TILES):
                a_ref[t, pl.ds(x * 16, ROWS), :] = a[:, t * LANES:(t + 1) * LANES]
        b = packed(*lows)
        for t in range(TILES):
            b_ref[t, pl.ds(k * 16, ROWS), :] = b[:, t * LANES:(t + 1) * LANES]
    for t in range(TILES):
        a, b = span_edges(a_ref, b_ref, t)
        smooth, _ = lift(None, b, None)
        to_right, to_left = coarse_terms(b)
        far_right = edge_right(to_right)
        far_left = edge_left(to_left)
        sends_right = edge_right(a) + edge_right(smooth)
        sends_left = edge_left(a) + edge_left(smooth)
        near = [jnp.where(odd_core, l, r) for l, r in zip(sends_left, sends_right)]
        other = [jnp.where(odd_core, r, l) for l, r in zip(sends_left, sends_right)]
        far_right, far_left = [far_right[0], far_right[2]], [far_left[1], jnp.zeros_like(far_left[1])]
        end = put_rows(near_ref, 0, near, t)
        put_rows(near_ref, end, [jnp.where(odd_core, l, r) for l, r in zip(far_left, far_right)], t)
        put_rows(other_ref, 0, other, t)
        put_rows(far_ref, 0, [jnp.where(odd_core, r, l) for l, r in zip(far_left, far_right)], t)


def fold_kernel(other_ref, near_ref, out_ref):
    odd_core = lax.axis_index("span") % 2 == 1
    out_ref[...] = other_ref[...]
    for t in range(TILES):
        one = near_ref[pl.ds(54, PAIRS), cut(t)]
        two = near_ref[pl.ds(60, PAIRS), cut(t)]
        zero = jnp.zeros_like(one)
        for row, term in ((0, jnp.where(odd_core, one, zero)), (1, jnp.where(odd_core, zero, one)), (2, jnp.where(odd_core, two, zero))):
            at = pl.ds(36 + row * PAIRS, PAIRS)
            out_ref[at, cut(t)] = other_ref[at, cut(t)] + term


def middle_kernel(a_ref, b_ref, near_ref, other_ref, far_ref, ya_ref, yb_ref, right_ref, left_ref, right2_ref, left2_ref, halo_ref):
    odd_core = lax.axis_index("span") % 2 == 1
    for j in range(3):
        near = near_ref[pl.ds(12 * j, PLANES), :]
        other = other_ref[pl.ds(12 * j, PLANES), :]
        left = jnp.where(odd_core, near, other)
        right = jnp.where(odd_core, other, near)
        for side, h in ((0, left), (1, right)):
            low = lift_lanes(h, 2)
            for t in range(TILES):
                halo_ref[t, pl.ds((side * 3 + j) * 32, PLANES), :] = h[:, t * LANES:(t + 1) * LANES]
                halo_ref[t, pl.ds((side * 3 + j) * 32 + 16, PLANES), :] = low[:, t * LANES:(t + 1) * LANES]
    for t in range(TILES):
        a, b = span_edges(a_ref, b_ref, t)
        halo = [halo_ref[t, pl.ds(32 * j, PLANES), :] for j in range(6)]
        smooth, detail = lift(halo[:3], a, halo[3:])
        for c in range(PAIRS):
            ya_ref[t, pl.ds(c, PLANES, stride=16), :] = smooth[c]
            ya_ref[t, pl.ds(8 + c, PLANES, stride=16), :] = detail[c]
        low = [
            packed(halo_ref[t, pl.ds(32 * j + 16, PAIRS, stride=2), :], halo_ref[t, pl.ds(32 * j + 17, PAIRS, stride=2), :])
            for j in range(6)
        ]
        smooth, _ = lift(low[:3], b, low[3:])
        to_right, to_left = coarse_terms(b)
        near = [near_ref[pl.ds(36 + PAIRS * j, PAIRS), cut(t)] for j in range(3)]
        other = [other_ref[pl.ds(36 + PAIRS * j, PAIRS), cut(t)] for j in range(3)]
        far = [far_ref[pl.ds(PAIRS * j, PAIRS), cut(t)] for j in range(2)]
        left = [jnp.where(odd_core, n, o) for n, o in zip(near, other)]
        right = [jnp.where(odd_core, o, n) for n, o in zip(near, other)]
        zero = jnp.zeros_like(far[0])
        left = plus(plus(left, edge_right(to_left)), [jnp.where(odd_core, far[0], zero), None, jnp.where(odd_core, far[1], zero)])
        right = plus(plus(right, edge_left(to_right)), [None, jnp.where(odd_core, zero, far[0]), None])
        smooth, detail = lift(left, smooth, right)
        for c, row in enumerate(interleaved(smooth, detail)):
            yb_ref[t, pl.ds(c, PAIRS, stride=8), :] = row
    for t in range(TILES):
        a, b = stream_planes(ya_ref, yb_ref, t)
        smooth, _ = lift(None, b, None)
        to_right, to_left = coarse_terms(b)
        far_right, far_left = edge_right(to_right), edge_left(to_left)
        for ref, edge in ((right_ref, edge_right), (left_ref, edge_left)):
            end = 0
            for plane in edge(a):
                end = put_rows(ref, end, [plane[0:6], plane[8:14]], t)
            lows = edge(b) + edge(smooth)
            for j in range(3):
                end = put_rows(ref, end, [packed(lows[2 * j], lows[2 * j + 1])[0:6]], t)
        right2_ref[:, cut(t)] = packed(far_right[0], far_right[2])
        left2_ref[:, cut(t)] = far_left[1]


def stream_planes(ya_ref, yb_ref, t):
    a = [ya_ref[t, pl.ds(16 * x, 16), :] for x in range(PLANES)]
    b = []
    for k in range(PAIRS):
        pair = yb_ref[t, pl.ds(8 * k, 8), :]
        b += [pair, unpacked_odd(pair)]
    return a, b


def last_kernel(ya_ref, yb_ref, left_ref, right_ref, left2_ref, right2_ref, out_ref, la_ref, lb_ref, w_ref):
    even = (lane((8, LANES)) & 1) == 0
    for t in range(TILES):
        for side, ref in ((0, left_ref), (1, right_ref)):
            for j in range(3):
                la_ref[t, pl.ds((side * 3 + j) * 16, 6), :] = ref[pl.ds(12 * j, 6), cut(t)]
                la_ref[t, pl.ds((side * 3 + j) * 16 + 8, 6), :] = ref[pl.ds(12 * j + 6, 6), cut(t)]
                lb_ref[t, pl.ds((side * 3 + j) * 8, 6), :] = ref[pl.ds(36 + 6 * j, 6), cut(t)]
        a, b = stream_planes(ya_ref, yb_ref, t)
        halo = [la_ref[t, pl.ds(16 * j, 16), :] for j in range(6)]
        a_smooth, a_detail = lift(halo[:3], a, halo[3:])
        sides = []
        for side in (0, 1):
            pairs = [lb_ref[t, pl.ds((side * 3 + j) * 8, 8), :] for j in range(3)]
            sides.append([x for pair in pairs for x in (pair, unpacked_odd(pair))])
        smooth, _ = lift(sides[0][:3], b, sides[1][:3])
        to_right, to_left = coarse_terms(b)
        far_left = left2_ref[:, cut(t)]
        left = plus(plus(sides[0][3:], edge_right(to_left)), [far_left, None, unpacked_odd(far_left)])
        right = plus(plus(sides[1][3:], edge_left(to_right)), [None, right2_ref[:, cut(t)], None])
        coarse = interleaved(*lift(left, smooth, right))
        for k in range(PAIRS):
            for x, plane in ((2 * k, a_smooth[k]), (2 * k + 1, a_detail[k])):
                low, high = plane[0:8], plane[8:16]
                if x % 2 == 0:
                    low = jnp.where(even, coarse[k], low)
                w_ref[t, pl.ds(16 * x, 8, stride=2), :] = low
                w_ref[t, pl.ds(16 * x + 1, 8, stride=2), :] = high
        for x in range(PLANES):
            out_ref[x, :, t * LANES:(t + 1) * LANES] = w_ref[t, pl.ds(16 * x, ROWS), :]


VMEM = pl.BlockSpec(memory_space=pltpu.VMEM)


def call(kernel, shapes, args, scratch=()):
    return pl.pallas_call(
        kernel,
        out_shape=[jax.ShapeDtypeStruct(s, jnp.float32) for s in shapes],
        in_specs=[VMEM] * len(args),
        out_specs=[VMEM] * len(shapes),
        scratch_shapes=[pltpu.VMEM(s, jnp.float32) for s in scratch],
        compiler_params=pltpu.CompilerParams(vmem_limit_bytes=16 << 20),
    )(*args)


def local(streams, spans, fields):
    def send(message, target):
        pairs = [(s * spans + y, (lambda q: q[0] % streams * spans + q[1] % spans)(target(s, y))) for s in range(streams) for y in range(spans)]
        return lax.ppermute(message, ("stream", "span"), pairs)

    a, b, near, other, far = call(
        first_kernel,
        [(TILES, PLANES * 16, LANES), (TILES, PAIRS * 16, LANES), (72, CELLS), (Y_ROWS, CELLS), (Y_FAR, CELLS)],
        [fields.reshape(PLANES, ROWS, CELLS)],
    )
    near = send(near, lambda s, y: (s, y ^ 1))
    far = send(far, lambda s, y: (s, y + (2 if y % 2 else -2)))
    (other,) = call(fold_kernel, [(Y_ROWS, CELLS)], [other, near])
    other = send(other, lambda s, y: (s, y + (1 if y % 2 else -1)))
    ya, yb, right, left, right2, left2 = call(
        middle_kernel,
        [(TILES, PLANES * 16, LANES), (TILES, PAIRS * 8, LANES), (X_ROWS, CELLS), (X_ROWS, CELLS), (X_FAR, CELLS), (X_FAR, CELLS)],
        [a, b, near, other, far],
        [(TILES, 192, LANES)],
    )
    from_left = send(right, lambda s, y: (s + 1, y))
    from_right = send(left, lambda s, y: (s - 1, y))
    from_left2 = send(right2, lambda s, y: (s + 2, y))
    from_right2 = send(left2, lambda s, y: (s - 2, y))
    (out,) = call(
        last_kernel,
        [(PLANES, ROWS, CELLS)],
        [ya, yb, from_left, from_right, from_left2, from_right2],
        [(TILES, 96, LANES), (TILES, 48, LANES), (TILES, PLANES * 16, LANES)],
    )
    return out.reshape(fields.shape)


def solution(mesh):
    return jax.shard_map(
        functools.partial(local, mesh.shape["stream"], mesh.shape["span"]),
        mesh=mesh,
        in_specs=(P(None, "stream", "span", None),),
        out_specs=P(None, "stream", "span", None),
        check_vma=False,
    )
```

time: 406 us -> 41 us (0.10)
  the two profiles are of different devices: /device:TPU:1 before, /device:TPU:4 now
where the time goes in v1:
time: 41 us; the launch traced here: 40.9 us
  starting transfers between devices  15 us (37%)
  waiting for transfers between devices  14.3 us (35%)
  Pallas kernels  8.86 us (22%)
  local copies, waits for them, and re-layouts  2.61 us (6%)
    ppermute x7, starting transfers between devices, send(): return lax.ppermute(message, ('stream', 'span'), pairs)  15 us
    ppermute x7, waiting for transfers between devices, send(): return lax.ppermute(message, ('stream', 'span'), pairs)  14.3 us
    pallas_call x4, Pallas kernels, call(): pl.pallas_call(kernel, out_shape=[jax.ShapeDtypeStruct(s, jnp.float32) fo...  8.86 us
    reshape x1, local copies, waits for them, and re-layouts, local(): return out.reshape(fields.shape)  1.42 us
    unnamed x1, local copies, waits for them, and re-layouts  1.18 us
  transfers between devices with their start and end apart: 7, of which 4 were waited for; matrix products, arithmetic and copies ran while one was open for 0% of the time, Pallas kernels for 0%

profile of v1, /device:TPU:4, one launch (start us, length us, event | category | flops | bytes accessed | tf_op | source)
XLA Modules:
  0.0 40.9 jit_solution(17415929712982252647)
XLA Ops:
  0.0 1.2 %copy.5 = f32[1,12,12,1024]{3,2,0,1:T(8,128)S(1)} copy(f32[1,12,12,1024]{3,0,2,1:T(1,128)} %param.1) | data formatting | bytes 1179648
  1.2 6.2 %shard_map.17 = (f32[8,192,128]{2,1,0:T(8,128)S(1)}, f32[8,96,128]{2,1,0:T(8,128)S(1)}, f32[72,1024]{1,0:T(8,128)S(1)}, f32[56,1024]{1,0:T(8,128)S(1)}, f32[16,1024]{1,0:T(8,128)S(1)}) custom-call(f32[12,12,1024]{2,1,0:T(8,128)S(1)} %bitcast.5), custom_call_target="tpu_custom_call" | custom-call | tf_op jit(solution)/shard_map/pallas_call | solution.py:255
  7.4 0.1 collective-permute-start
  7.5 1.6 %collective-permute-done.near_ref = f32[72,1024]{1,0:T(8,128)S(1)} collective-permute-done((f32[72,1024]{1,0:T(8,128)S(1)}, f32[72,1024]{1,0:T(8,128)S(1)}, u32[]{:S(2)}, u32[]{:S(2)}) %collective-permute-start) | collective-permute-done | bytes 294944 | tf_op jit(solution)/shard_map/ppermute | solution.py:268
  9.1 8.6 %collective-permute-start.1 = (f32[56,1024]{1,0:T(8,128)S(1)}, f32[56,1024]{1,0:T(8,128)S(1)}, u32[]{:S(2)}, u32[]{:S(2)}) collective-permute-start(f32[56,1024]{1,0:T(8,128)S(1)} %shard_map.18), channel_id=1, source_target_pairs={{0,31},{1,2},{2,1},{3,4},{4,3},{5,6},{6,5},{7,8},{8,7},{9,10},{10,... | collective-permute-start | bytes 688136 | tf_op jit(solution)/shard_map/ppermute | solution.py:268
  17.7 0.7 %collective-permute-start.2 = (f32[16,1024]{1,0:T(8,128)S(1)}, f32[16,1024]{1,0:T(8,128)S(1)}, u32[]{:S(2)}, u32[]{:S(2)}) collective-permute-start(f32[16,1024]{1,0:T(8,128)S(1)} %get-tuple-element.20), channel_id=1, source_target_pairs={{0,30},{1,3},{2,0},{3,5},{4,2},{5,7},{6,4},{7,9},{8,6},{9,11},{10,... | collective-permute-start | bytes 196616 | tf_op jit(solution)/shard_map/ppermute | solution.py:268
  18.4 6.7 %collective-permute-done.2.far_ref = f32[16,1024]{1,0:T(8,128)S(1)} collective-permute-done((f32[16,1024]{1,0:T(8,128)S(1)}, f32[16,1024]{1,0:T(8,128)S(1)}, u32[]{:S(2)}, u32[]{:S(2)}) %collective-permute-start.2) | collective-permute-done | bytes 65568 | tf_op jit(solution)/shard_map/ppermute | solution.py:268
  25.1 0.0 collective-permute-done.1.other_ref
  25.1 2.1 %shard_map.19 = (f32[8,192,128]{2,1,0:T(8,128)S(1)}, f32[8,48,128]{2,1,0:T(8,128)S(1)}, f32[56,1024]{1,0:T(8,128)S(1)}, f32[56,1024]{1,0:T(8,128)S(1)}, f32[8,1024]{1,0:T(8,128)S(1)}, /*index=5*/f32[8,1024]{1,0:T(8,128)S(1)}) custom-call(f32[8,192,128]{2,1,0:T(8,128)S(1)} %get-tuple-element.16.a_ref, f32[8,96,128]{2,1,0:T(8,128)S(1)} %get-tuple-element.17.b_ref, ...), custom_call_target="tpu_custom_call" | custom-call | tf_op jit(solution)/shard_map/pallas_call | solution.py:255
  27.2 1.3 %collective-permute-start.3 = (f32[56,1024]{1,0:T(8,128)S(1)}, f32[56,1024]{1,0:T(8,128)S(1)}, u32[]{:S(2)}, u32[]{:S(2)}) collective-permute-start(f32[56,1024]{1,0:T(8,128)S(1)} %get-tuple-element.23), channel_id=1, source_target_pairs={{0,32},{1,33},{2,34},{3,35},{4,36},{5,37},{6,38},{7,39},{8,40},{9,... | collective-permute-start | bytes 688136 | tf_op jit(solution)/shard_map/ppermute | solution.py:268
  28.5 0.8 %collective-permute-start.4 = (f32[56,1024]{1,0:T(8,128)S(1)}, f32[56,1024]{1,0:T(8,128)S(1)}, u32[]{:S(2)}, u32[]{:S(2)}) collective-permute-start(f32[56,1024]{1,0:T(8,128)S(1)} %get-tuple-element.24), channel_id=1, source_target_pairs={{0,224},{1,225},{2,226},{3,227},{4,228},{5,229},{6,230},{7,231},{8... | collective-permute-start | bytes 688136 | tf_op jit(solution)/shard_map/ppermute | solution.py:268
  29.3 2.5 %collective-permute-start.5 = (f32[8,1024]{1,0:T(8,128)S(1)}, f32[8,1024]{1,0:T(8,128)S(1)}, u32[]{:S(2)}, u32[]{:S(2)}) collective-permute-start(f32[8,1024]{1,0:T(8,128)S(1)} %get-tuple-element.25), channel_id=1, source_target_pairs={{0,64},{1,65},{2,66},{3,67},{4,68},{5,69},{6,70},{7,71},{8,72},{9,... | collective-permute-start | bytes 98312 | tf_op jit(solution)/shard_map/ppermute | solution.py:268
  31.8 1.0 %collective-permute-start.6 = (f32[8,1024]{1,0:T(8,128)S(1)}, f32[8,1024]{1,0:T(8,128)S(1)}, u32[]{:S(2)}, u32[]{:S(2)}) collective-permute-start(f32[8,1024]{1,0:T(8,128)S(1)} %get-tuple-element.26), channel_id=1, source_target_pairs={{0,192},{1,193},{2,194},{3,195},{4,196},{5,197},{6,198},{7,199},{8... | collective-permute-start | bytes 98312 | tf_op jit(solution)/shard_map/ppermute | solution.py:268
  32.8 1.9 %collective-permute-done.5.left2_ref = f32[8,1024]{1,0:T(8,128)S(1)} collective-permute-done((f32[8,1024]{1,0:T(8,128)S(1)}, f32[8,1024]{1,0:T(8,128)S(1)}, u32[]{:S(2)}, u32[]{:S(2)}) %collective-permute-start.5) | collective-permute-done | bytes 32800 | tf_op jit(solution)/shard_map/ppermute | solution.py:268
  34.7 4.2 %collective-permute-done.6.right2_ref = f32[8,1024]{1,0:T(8,128)S(1)} collective-permute-done((f32[8,1024]{1,0:T(8,128)S(1)}, f32[8,1024]{1,0:T(8,128)S(1)}, u32[]{:S(2)}, u32[]{:S(2)}) %collective-permute-start.6) | collective-permute-done | bytes 32800 | tf_op jit(solution)/shard_map/ppermute | solution.py:268
  38.9 0.0 collective-permute-done.3.left_ref
  38.9 0.0 collective-permute-done.4.right_ref
  38.9 0.5 %shard_map.20 = f32[12,12,1024]{2,1,0:T(8,128)S(1)} custom-call(f32[8,192,128]{2,1,0:T(8,128)S(1)} %get-tuple-element.21.ya_ref, f32[8,48,128]{2,1,0:T(8,128)S(1)} %get-tuple-element.22.yb_ref, f32[56,1024]{1,0:T(8,128)S(1)} %collective-permute-done.3.left_ref, f32[56,1024]{1,0:T(8,128)S(1)} %collective-permute-done.4.right_ref, ...), custom_call_target="tpu_custom_call" | custom-call | tf_op jit(solution)/shard_map/pallas_call | solution.py:255
  39.4 1.4 %copy.2 = f32[1,12,12,1024]{3,0,2,1:T(1,128)} copy(f32[1,12,12,1024]{3,2,1,0:T(8,128)S(1)} %bitcast.4) | data formatting | bytes 1179648 | tf_op jit(solution)/shard_map/reshape | solution.py:295
  (1 shorter events, 0.0 us)
Async XLA Ops:
  7.4 1.7 %collective-permute-start = (f32[72,1024]{1,0:T(8,128)S(1)}, f32[72,1024]{1,0:T(8,128)S(1)}, u32[]{:S(2)}, u32[]{:S(2)}) collective-permute-start(f32[72,1024]{1,0:T(8,128)S(1)} %get-tuple-element.18), channel_id=1, source_target_pairs={{0,1},{1,0},{2,3},{3,2},{4,5},{5,4},{6,7},{7,6},{8,9},{9,8},{10,11... | collective-permute-start | bytes 884744 | tf_op jit(solution)/shard_map/ppermute | solution.py:268
  9.1 16.0 %collective-permute-start.1 = (f32[56,1024]{1,0:T(8,128)S(1)}, f32[56,1024]{1,0:T(8,128)S(1)}, u32[]{:S(2)}, u32[]{:S(2)}) collective-permute-start(f32[56,1024]{1,0:T(8,128)S(1)} %shard_map.18), channel_id=1, source_target_pairs={{0,31},{1,2},{2,1},{3,4},{4,3},{5,6},{6,5},{7,8},{8,7},{9,10},{10,... | collective-permute-start | bytes 688136 | tf_op jit(solution)/shard_map/ppermute | solution.py:268
  17.7 7.4 %collective-permute-start.2 = (f32[16,1024]{1,0:T(8,128)S(1)}, f32[16,1024]{1,0:T(8,128)S(1)}, u32[]{:S(2)}, u32[]{:S(2)}) collective-permute-start(f32[16,1024]{1,0:T(8,128)S(1)} %get-tuple-element.20), channel_id=1, source_target_pairs={{0,30},{1,3},{2,0},{3,5},{4,2},{5,7},{6,4},{7,9},{8,6},{9,11},{10,... | collective-permute-start | bytes 196616 | tf_op jit(solution)/shard_map/ppermute | solution.py:268
  27.2 11.7 %collective-permute-start.3 = (f32[56,1024]{1,0:T(8,128)S(1)}, f32[56,1024]{1,0:T(8,128)S(1)}, u32[]{:S(2)}, u32[]{:S(2)}) collective-permute-start(f32[56,1024]{1,0:T(8,128)S(1)} %get-tuple-element.23), channel_id=1, source_target_pairs={{0,32},{1,33},{2,34},{3,35},{4,36},{5,37},{6,38},{7,39},{8,40},{9,... | collective-permute-start | bytes 688136 | tf_op jit(solution)/shard_map/ppermute | solution.py:268
  28.5 10.4 %collective-permute-start.4 = (f32[56,1024]{1,0:T(8,128)S(1)}, f32[56,1024]{1,0:T(8,128)S(1)}, u32[]{:S(2)}, u32[]{:S(2)}) collective-permute-start(f32[56,1024]{1,0:T(8,128)S(1)} %get-tuple-element.24), channel_id=1, source_target_pairs={{0,224},{1,225},{2,226},{3,227},{4,228},{5,229},{6,230},{7,231},{8... | collective-permute-start | bytes 688136 | tf_op jit(solution)/shard_map/ppermute | solution.py:268
  29.3 5.4 %collective-permute-start.5 = (f32[8,1024]{1,0:T(8,128)S(1)}, f32[8,1024]{1,0:T(8,128)S(1)}, u32[]{:S(2)}, u32[]{:S(2)}) collective-permute-start(f32[8,1024]{1,0:T(8,128)S(1)} %get-tuple-element.25), channel_id=1, source_target_pairs={{0,64},{1,65},{2,66},{3,67},{4,68},{5,69},{6,70},{7,71},{8,72},{9,... | collective-permute-start | bytes 98312 | tf_op jit(solution)/shard_map/ppermute | solution.py:268
  31.8 7.1 %collective-permute-start.6 = (f32[8,1024]{1,0:T(8,128)S(1)}, f32[8,1024]{1,0:T(8,128)S(1)}, u32[]{:S(2)}, u32[]{:S(2)}) collective-permute-start(f32[8,1024]{1,0:T(8,128)S(1)} %get-tuple-element.26), channel_id=1, source_target_pairs={{0,192},{1,193},{2,194},{3,195},{4,196},{5,197},{6,198},{7,199},{8... | collective-permute-start | bytes 98312 | tf_op jit(solution)/shard_map/ppermute | solution.py:268

commit v2 on v1

--- a/solution.py
+++ b/solution.py
@@ -2,6 +2,8 @@
 
 import jax
 import jax.numpy as jnp
+import ml_dtypes
+import numpy as np
 from jax import lax
 from jax.experimental import pallas as pl
 from jax.experimental.pallas import tpu as pltpu
@@ -76,22 +78,34 @@
     return lax.broadcasted_iota(jnp.int32, shape, len(shape) - 1)
 
 
-def lift_lanes(v, step):
-    n = v.shape[-1]
-    at = lane(v.shape) & (2 * step - 1)
-    roll = lambda x, k: pltpu.roll(x, (k * step) % n, axis=v.ndim - 1)
-    d = v - (NEAR_D * (roll(v, 1) + roll(v, -1)) - FAR_D * (roll(v, 3) + roll(v, -3)))
-    w = jnp.where(at == step, d, v)
-    s = w + (NEAR_S * (roll(w, 1) + roll(w, -1)) - FAR_S * (roll(w, 3) + roll(w, -3)))
-    return jnp.where(at == 0, s, w)
-
-
-def packed(a, b):
-    return jnp.where((lane(a.shape) & 1) == 0, a, pltpu.roll(b, 1, axis=b.ndim - 1))
-
-
-def unpacked_odd(p):
-    return pltpu.roll(p, p.shape[-1] - 1, axis=p.ndim - 1)
+def band(size, step, first, count):
+    v = np.eye(size)
+    r = lambda k: np.roll(v, k * step, axis=1)
+    at = np.arange(size) % (2 * step)
+    d = v - (NEAR_D * (r(1) + r(-1)) - FAR_D * (r(3) + r(-3)))
+    v = np.where(at == step, d, v)
+    s = v + (NEAR_S * (r(1) + r(-1)) - FAR_S * (r(3) + r(-3)))
+    v = np.where(at == 0, s, v)
+    m = v[:, first:first + step * count:step]
+    held = m.astype(ml_dtypes.bfloat16)
+    assert (held.astype(np.float64) == m).all()
+    return held
+
+
+def parts(v):
+    high = v.astype(jnp.bfloat16)
+    rest = v - high.astype(jnp.float32)
+    mid = rest.astype(jnp.bfloat16)
+    return high, mid, (rest - mid.astype(jnp.float32)).astype(jnp.bfloat16)
+
+
+def window(v, start, count):
+    tiles = [(start + i) % TILES for i in range(count)]
+    return jnp.concatenate([v[:, i * LANES:(i + 1) * LANES] for i in tiles], axis=1)
+
+
+def banded(split, m, start, count):
+    return sum(jnp.dot(window(p, start, count), m, preferred_element_type=jnp.float32) for p in split)
 
 
 def cut(t):
@@ -102,8 +116,8 @@
 
 
 def span_edges(a_ref, b_ref, t):
-    a = [a_ref[t, pl.ds(y, PLANES, stride=16), :] for y in range(ROWS)]
-    b = [b_ref[t, pl.ds(y, PAIRS, stride=16), :] for y in range(ROWS)]
+    a = [a_ref[t, pl.ds(y, PLANES, stride=ROWS), :] for y in range(ROWS)]
+    b = [b_ref[t, pl.ds(y, PAIRS, stride=ROWS), :] for y in range(ROWS)]
     return a, b
 
 
@@ -114,18 +128,22 @@
     return start
 
 
-def first_kernel(f_ref, a_ref, b_ref, near_ref, other_ref, far_ref):
+def first_kernel(f_ref, fine_ref, low_ref, a_ref, b_ref, near_ref, other_ref, far_ref, v_ref):
     odd_core = lax.axis_index("span") % 2 == 1
-    for k in range(PAIRS):
-        lows = []
-        for x in (2 * k, 2 * k + 1):
-            a = lift_lanes(f_ref[x], 1)
-            lows.append(lift_lanes(a, 2))
-            for t in range(TILES):
-                a_ref[t, pl.ds(x * 16, ROWS), :] = a[:, t * LANES:(t + 1) * LANES]
-        b = packed(*lows)
-        for t in range(TILES):
-            b_ref[t, pl.ds(k * 16, ROWS), :] = b[:, t * LANES:(t + 1) * LANES]
+    for x in range(PLANES):
+        v_ref[pl.ds(x * ROWS, ROWS), :] = f_ref[x]
+    split = parts(v_ref[...])
+    for q in range(4):
+        block = banded(split, fine_ref[...], 2 * q - 1, 4)
+        v_ref[:, pl.ds(256 * q, 256)] = block
+        for t in range(2):
+            a_ref[2 * q + t] = block[:, t * LANES:(t + 1) * LANES]
+    split = parts(v_ref[...])
+    for q in range(2):
+        v_ref[:, pl.ds(256 * q, 256)] = banded(split, low_ref[...], 4 * q - 1, 6)
+    for t in range(TILES):
+        for k in range(PAIRS):
+            b_ref[t, pl.ds(k * ROWS, ROWS), :] = v_ref[pl.ds((2 * k + t // 4) * ROWS, ROWS), cut(t % 4)]
     for t in range(TILES):
         a, b = span_edges(a_ref, b_ref, t)
         smooth, _ = lift(None, b, None)
@@ -155,30 +173,30 @@
             out_ref[at, cut(t)] = other_ref[at, cut(t)] + term
 
 
-def middle_kernel(a_ref, b_ref, near_ref, other_ref, far_ref, ya_ref, yb_ref, right_ref, left_ref, right2_ref, left2_ref, halo_ref):
+def middle_kernel(a_ref, b_ref, near_ref, other_ref, far_ref, low_ref, ya_ref, yb_ref, right_ref, left_ref, right2_ref, left2_ref, halo_ref):
     odd_core = lax.axis_index("span") % 2 == 1
-    for j in range(3):
-        near = near_ref[pl.ds(12 * j, PLANES), :]
-        other = other_ref[pl.ds(12 * j, PLANES), :]
-        left = jnp.where(odd_core, near, other)
-        right = jnp.where(odd_core, other, near)
-        for side, h in ((0, left), (1, right)):
-            low = lift_lanes(h, 2)
-            for t in range(TILES):
-                halo_ref[t, pl.ds((side * 3 + j) * 32, PLANES), :] = h[:, t * LANES:(t + 1) * LANES]
-                halo_ref[t, pl.ds((side * 3 + j) * 32 + 16, PLANES), :] = low[:, t * LANES:(t + 1) * LANES]
+    for side, ref in ((0, near_ref), (1, other_ref)):
+        split = parts(ref[pl.ds(0, 48), :])
+        for q in range(2):
+            low = banded(split, low_ref[...], 4 * q - 1, 6)
+            for t in range(2):
+                halo_ref[2 * q + t, pl.ds(side * 48, 48), :] = low[:, t * LANES:(t + 1) * LANES]
     for t in range(TILES):
         a, b = span_edges(a_ref, b_ref, t)
-        halo = [halo_ref[t, pl.ds(32 * j, PLANES), :] for j in range(6)]
-        smooth, detail = lift(halo[:3], a, halo[3:])
+        near = [near_ref[pl.ds(PLANES * j, PLANES), cut(t)] for j in range(3)]
+        other = [other_ref[pl.ds(PLANES * j, PLANES), cut(t)] for j in range(3)]
+        left = [jnp.where(odd_core, n, o) for n, o in zip(near, other)]
+        right = [jnp.where(odd_core, o, n) for n, o in zip(near, other)]
+        smooth, detail = lift(left, a, right)
         for c in range(PAIRS):
             ya_ref[t, pl.ds(c, PLANES, stride=16), :] = smooth[c]
             ya_ref[t, pl.ds(8 + c, PLANES, stride=16), :] = detail[c]
-        low = [
-            packed(halo_ref[t, pl.ds(32 * j + 16, PAIRS, stride=2), :], halo_ref[t, pl.ds(32 * j + 17, PAIRS, stride=2), :])
-            for j in range(6)
-        ]
-        smooth, _ = lift(low[:3], b, low[3:])
+        near, other = (
+            [halo_ref[t % 4, pl.ds(48 * side + PLANES * j + t // 4, PAIRS, stride=2), :] for j in range(3)] for side in (0, 1)
+        )
+        left = [jnp.where(odd_core, n, o) for n, o in zip(near, other)]
+        right = [jnp.where(odd_core, o, n) for n, o in zip(near, other)]
+        smooth, _ = lift(left, b, right)
         to_right, to_left = coarse_terms(b)
         near = [near_ref[pl.ds(36 + PAIRS * j, PAIRS), cut(t)] for j in range(3)]
         other = [other_ref[pl.ds(36 + PAIRS * j, PAIRS), cut(t)] for j in range(3)]
@@ -192,56 +210,66 @@
         for c, row in enumerate(interleaved(smooth, detail)):
             yb_ref[t, pl.ds(c, PAIRS, stride=8), :] = row
     for t in range(TILES):
-        a, b = stream_planes(ya_ref, yb_ref, t)
+        a = stream_planes(ya_ref, t)
+        for ref, edge in ((right_ref, edge_right), (left_ref, edge_left)):
+            end = 0
+            for plane in edge(a):
+                end = put_rows(ref, end, [plane[0:6], plane[8:14]], t)
+    for t in range(4):
+        b = low_planes(yb_ref, t)
         smooth, _ = lift(None, b, None)
         to_right, to_left = coarse_terms(b)
         far_right, far_left = edge_right(to_right), edge_left(to_left)
         for ref, edge in ((right_ref, edge_right), (left_ref, edge_left)):
-            end = 0
-            for plane in edge(a):
-                end = put_rows(ref, end, [plane[0:6], plane[8:14]], t)
-            lows = edge(b) + edge(smooth)
+            for half, planes in ((0, edge(b)), (4, edge(smooth))):
+                put_rows(ref, 36, [plane[0:6] for plane in planes], t + half)
+        right2_ref[:, cut(t)] = far_right[0]
+        right2_ref[:, cut(t + 4)] = far_right[2]
+        left2_ref[:, cut(t)] = far_left[1]
+
+
+def stream_planes(ya_ref, t):
+    return [ya_ref[t, pl.ds(16 * x, 16), :] for x in range(PLANES)]
+
+
+def low_planes(yb_ref, t):
+    return [yb_ref[t + 4 * odd, pl.ds(8 * k, 8), :] for k in range(PAIRS) for odd in (0, 1)]
+
+
+def last_kernel(ya_ref, yb_ref, left_ref, right_ref, left2_ref, right2_ref, spread_ref, out_ref, la_ref, lb_ref, w_ref, c_ref):
+    even = (lane((8, LANES)) & 1) == 0
+    for t in range(4):
+        b = low_planes(yb_ref, t)
+        for side, ref in ((0, left_ref), (1, right_ref)):
             for j in range(3):
-                end = put_rows(ref, end, [packed(lows[2 * j], lows[2 * j + 1])[0:6]], t)
-        right2_ref[:, cut(t)] = packed(far_right[0], far_right[2])
-        left2_ref[:, cut(t)] = far_left[1]
-
-
-def stream_planes(ya_ref, yb_ref, t):
-    a = [ya_ref[t, pl.ds(16 * x, 16), :] for x in range(PLANES)]
-    b = []
-    for k in range(PAIRS):
-        pair = yb_ref[t, pl.ds(8 * k, 8), :]
-        b += [pair, unpacked_odd(pair)]
-    return a, b
-
-
-def last_kernel(ya_ref, yb_ref, left_ref, right_ref, left2_ref, right2_ref, out_ref, la_ref, lb_ref, w_ref):
-    even = (lane((8, LANES)) & 1) == 0
+                for half in (0, 1):
+                    lb_ref[t, pl.ds((side * 6 + half * 3 + j) * 8, 6), :] = ref[pl.ds(36 + 6 * j, 6), cut(t + 4 * half)]
+        halo = [lb_ref[t, pl.ds(8 * j, 8), :] for j in range(12)]
+        smooth, _ = lift(halo[0:3], b, halo[6:9])
+        to_right, to_left = coarse_terms(b)
+        left = plus(plus(halo[3:6], edge_right(to_left)), [left2_ref[:, cut(t)], None, left2_ref[:, cut(t + 4)]])
+        right = plus(plus(halo[9:12], edge_left(to_right)), [None, right2_ref[:, cut(t)], None])
+        for k, plane in enumerate(interleaved(*lift(left, smooth, right))):
+            c_ref[pl.ds(8 * k, 8), cut(t)] = plane
+    split = parts(c_ref[...])
     for t in range(TILES):
         for side, ref in ((0, left_ref), (1, right_ref)):
             for j in range(3):
                 la_ref[t, pl.ds((side * 3 + j) * 16, 6), :] = ref[pl.ds(12 * j, 6), cut(t)]
                 la_ref[t, pl.ds((side * 3 + j) * 16 + 8, 6), :] = ref[pl.ds(12 * j + 6, 6), cut(t)]
-                lb_ref[t, pl.ds((side * 3 + j) * 8, 6), :] = ref[pl.ds(36 + 6 * j, 6), cut(t)]
-        a, b = stream_planes(ya_ref, yb_ref, t)
+        if t % 2 == 0:
+            spread = sum(
+                jnp.dot(p[:, t * 64:t * 64 + LANES], spread_ref[...], preferred_element_type=jnp.float32) for p in split
+            )
+        coarse = spread[:, (t % 2) * LANES:(t % 2 + 1) * LANES]
+        a = stream_planes(ya_ref, t)
         halo = [la_ref[t, pl.ds(16 * j, 16), :] for j in range(6)]
         a_smooth, a_detail = lift(halo[:3], a, halo[3:])
-        sides = []
-        for side in (0, 1):
-            pairs = [lb_ref[t, pl.ds((side * 3 + j) * 8, 8), :] for j in range(3)]
-            sides.append([x for pair in pairs for x in (pair, unpacked_odd(pair))])
-        smooth, _ = lift(sides[0][:3], b, sides[1][:3])
-        to_right, to_left = coarse_terms(b)
-        far_left = left2_ref[:, cut(t)]
-        left = plus(plus(sides[0][3:], edge_right(to_left)), [far_left, None, unpacked_odd(far_left)])
-        right = plus(plus(sides[1][3:], edge_left(to_right)), [None, right2_ref[:, cut(t)], None])
-        coarse = interleaved(*lift(left, smooth, right))
         for k in range(PAIRS):
             for x, plane in ((2 * k, a_smooth[k]), (2 * k + 1, a_detail[k])):
                 low, high = plane[0:8], plane[8:16]
                 if x % 2 == 0:
-                    low = jnp.where(even, coarse[k], low)
+                    low = jnp.where(even, coarse[8 * k:8 * k + 8], low)
                 w_ref[t, pl.ds(16 * x, 8, stride=2), :] = low
                 w_ref[t, pl.ds(16 * x + 1, 8, stride=2), :] = high
         for x in range(PLANES):
@@ -267,10 +295,13 @@
         pairs = [(s * spans + y, (lambda q: q[0] % streams * spans + q[1] % spans)(target(s, y))) for s in range(streams) for y in range(spans)]
         return lax.ppermute(message, ("stream", "span"), pairs)
 
+    fine, low = jnp.asarray(band(512, 1, 128, 256)), jnp.asarray(band(768, 2, 128, 256))
+    spread = jnp.asarray(np.repeat(np.eye(LANES), 2, axis=1) * (np.arange(2 * LANES) % 2 == 0), jnp.bfloat16)
     a, b, near, other, far = call(
         first_kernel,
-        [(TILES, PLANES * 16, LANES), (TILES, PAIRS * 16, LANES), (72, CELLS), (Y_ROWS, CELLS), (Y_FAR, CELLS)],
-        [fields.reshape(PLANES, ROWS, CELLS)],
+        [(TILES, PLANES * ROWS, LANES), (TILES, PAIRS * ROWS, LANES), (72, CELLS), (Y_ROWS, CELLS), (Y_FAR, CELLS)],
+        [fields.reshape(PLANES, ROWS, CELLS), fine, low],
+        [(PLANES * ROWS, CELLS)],
     )
     near = send(near, lambda s, y: (s, y ^ 1))
     far = send(far, lambda s, y: (s, y + (2 if y % 2 else -2)))
@@ -279,8 +310,8 @@
     ya, yb, right, left, right2, left2 = call(
         middle_kernel,
         [(TILES, PLANES * 16, LANES), (TILES, PAIRS * 8, LANES), (X_ROWS, CELLS), (X_ROWS, CELLS), (X_FAR, CELLS), (X_FAR, CELLS)],
-        [a, b, near, other, far],
-        [(TILES, 192, LANES)],
+        [a, b, near, other, far, low],
+        [(4, 96, LANES)],
     )
     from_left = send(right, lambda s, y: (s + 1, y))
     from_right = send(left, lambda s, y: (s - 1, y))
@@ -289,8 +320,8 @@
     (out,) = call(
         last_kernel,
         [(PLANES, ROWS, CELLS)],
-        [ya, yb, from_left, from_right, from_left2, from_right2],
-        [(TILES, 96, LANES), (TILES, 48, LANES), (TILES, PLANES * 16, LANES)],
+        [ya, yb, from_left, from_right, from_left2, from_right2, spread],
+        [(TILES, 96, LANES), (4, 96, LANES), (TILES, PLANES * 16, LANES), (48, CELLS // 2)],
     )
     return out.reshape(fields.shape)
 

time: 41 us -> 35.5 us (0.87)
  Pallas kernels: 8.86 us -> 3.36 us
    pallas_call x4, Pallas kernels: 8.86 us -> 3.36 us  [call(): pl.pallas_call(kernel, out_shape=[jax.ShapeDtypeStruct(s, jnp.float32) fo...]
    unnamed x1 -> x7, local copies, waits for them, and re-layouts: 1.18 us -> 1.26 us
where the time goes in v2:
time: 35.5 us
  starting transfers between devices  15 us (42%)
  waiting for transfers between devices  14.3 us (40%)
  Pallas kernels  3.36 us (9%)
  local copies, waits for them, and re-layouts  2.68 us (8%)
    ppermute x7, starting transfers between devices, send(): return lax.ppermute(message, ('stream', 'span'), pairs)  15 us
    ppermute x7, waiting for transfers between devices, send(): return lax.ppermute(message, ('stream', 'span'), pairs)  14.3 us
    pallas_call x4, Pallas kernels, call(): pl.pallas_call(kernel, out_shape=[jax.ShapeDtypeStruct(s, jnp.float32) fo...  3.36 us
    reshape x1, local copies, waits for them, and re-layouts, local(): return out.reshape(fields.shape)  1.42 us
    unnamed x7, local copies, waits for them, and re-layouts  1.26 us
  transfers between devices with their start and end apart: 7, of which 4 were waited for; matrix products, arithmetic and copies ran while one was open for 0% of the time, Pallas kernels for 0%

profile of v2, /device:TPU:4, one launch (start us, length us, event | category | flops | bytes accessed | tf_op | source)
XLA Modules:
  0.0 35.5 jit_solution(11887925538306945827)
XLA Ops:
  0.0 0.0 copy-start
  0.0 0.0 copy-start.1
  0.0 1.2 %copy.8 = f32[1,12,12,1024]{3,2,0,1:T(8,128)S(1)} copy(f32[1,12,12,1024]{3,0,2,1:T(1,128)} %param.4) | data formatting | bytes 1179648
  1.3 0.0 copy-done
  1.3 0.0 copy-done.1
  1.3 1.3 %shard_map.46 = (f32[8,144,128]{2,1,0:T(8,128)S(1)}, f32[8,72,128]{2,1,0:T(8,128)S(1)}, f32[72,1024]{1,0:T(8,128)S(1)}, f32[56,1024]{1,0:T(8,128)S(1)}, f32[16,1024]{1,0:T(8,128)S(1)}) custom-call(f32[12,12,1024]{2,1,0:T(8,128)S(1)} %bitcast.5, bf16[512,256]{1,0:T(8,128)(2,1)S(1)} %copy-done.1, bf16[768,256]{1,0:T(8,128)(2,1)S(1)} %copy-done), custom_call_target="tpu_custom_call" | custom-call | tf_op jit(solution)/shard_map/pallas_call | solution.py:283
  2.6 0.1 collective-permute-start
  2.7 1.6 %collective-permute-done.near_ref = f32[72,1024]{1,0:T(8,128)S(1)} collective-permute-done((f32[72,1024]{1,0:T(8,128)S(1)}, f32[72,1024]{1,0:T(8,128)S(1)}, u32[]{:S(2)}, u32[]{:S(2)}) %collective-permute-start) | collective-permute-done | bytes 294944 | tf_op jit(solution)/shard_map/ppermute | solution.py:296
  4.3 8.6 %collective-permute-start.1 = (f32[56,1024]{1,0:T(8,128)S(1)}, f32[56,1024]{1,0:T(8,128)S(1)}, u32[]{:S(2)}, u32[]{:S(2)}) collective-permute-start(f32[56,1024]{1,0:T(8,128)S(1)} %shard_map.47), channel_id=1, source_target_pairs={{0,31},{1,2},{2,1},{3,4},{4,3},{5,6},{6,5},{7,8},{8,7},{9,10},{10,... | collective-permute-start | bytes 688136 | tf_op jit(solution)/shard_map/ppermute | solution.py:296
  12.9 0.7 %collective-permute-start.2 = (f32[16,1024]{1,0:T(8,128)S(1)}, f32[16,1024]{1,0:T(8,128)S(1)}, u32[]{:S(2)}, u32[]{:S(2)}) collective-permute-start(f32[16,1024]{1,0:T(8,128)S(1)} %get-tuple-element.20), channel_id=1, source_target_pairs={{0,30},{1,3},{2,0},{3,5},{4,2},{5,7},{6,4},{7,9},{8,6},{9,11},{10,... | collective-permute-start | bytes 196616 | tf_op jit(solution)/shard_map/ppermute | solution.py:296
  13.6 6.7 %collective-permute-done.2.far_ref = f32[16,1024]{1,0:T(8,128)S(1)} collective-permute-done((f32[16,1024]{1,0:T(8,128)S(1)}, f32[16,1024]{1,0:T(8,128)S(1)}, u32[]{:S(2)}, u32[]{:S(2)}) %collective-permute-start.2) | collective-permute-done | bytes 65568 | tf_op jit(solution)/shard_map/ppermute | solution.py:296
  20.3 0.0 collective-permute-done.1.other_ref
  20.3 0.0 copy-start.2
  20.3 1.5 %shard_map.48 = (f32[8,192,128]{2,1,0:T(8,128)S(1)}, f32[8,48,128]{2,1,0:T(8,128)S(1)}, f32[56,1024]{1,0:T(8,128)S(1)}, f32[56,1024]{1,0:T(8,128)S(1)}, f32[8,1024]{1,0:T(8,128)S(1)}, /*index=5*/f32[8,1024]{1,0:T(8,128)S(1)}) custom-call(f32[8,144,128]{2,1,0:T(8,128)S(1)} %get-tuple-element.16.a_ref, f32[8,72,128]{2,1,0:T(8,128)S(1)} %get-tuple-element.17.b_ref, ...), custom_call_target="tpu_custom_call" | custom-call | tf_op jit(solution)/shard_map/pallas_call | solution.py:283
  21.8 1.3 %collective-permute-start.3 = (f32[56,1024]{1,0:T(8,128)S(1)}, f32[56,1024]{1,0:T(8,128)S(1)}, u32[]{:S(2)}, u32[]{:S(2)}) collective-permute-start(f32[56,1024]{1,0:T(8,128)S(1)} %get-tuple-element.23), channel_id=1, source_target_pairs={{0,32},{1,33},{2,34},{3,35},{4,36},{5,37},{6,38},{7,39},{8,40},{9,... | collective-permute-start | bytes 688136 | tf_op jit(solution)/shard_map/ppermute | solution.py:296
  23.1 0.8 %collective-permute-start.4 = (f32[56,1024]{1,0:T(8,128)S(1)}, f32[56,1024]{1,0:T(8,128)S(1)}, u32[]{:S(2)}, u32[]{:S(2)}) collective-permute-start(f32[56,1024]{1,0:T(8,128)S(1)} %get-tuple-element.24), channel_id=1, source_target_pairs={{0,224},{1,225},{2,226},{3,227},{4,228},{5,229},{6,230},{7,231},{8... | collective-permute-start | bytes 688136 | tf_op jit(solution)/shard_map/ppermute | solution.py:296
  23.9 2.5 %collective-permute-start.5 = (f32[8,1024]{1,0:T(8,128)S(1)}, f32[8,1024]{1,0:T(8,128)S(1)}, u32[]{:S(2)}, u32[]{:S(2)}) collective-permute-start(f32[8,1024]{1,0:T(8,128)S(1)} %get-tuple-element.25), channel_id=1, source_target_pairs={{0,64},{1,65},{2,66},{3,67},{4,68},{5,69},{6,70},{7,71},{8,72},{9,... | collective-permute-start | bytes 98312 | tf_op jit(solution)/shard_map/ppermute | solution.py:296
  26.5 1.0 %collective-permute-start.6 = (f32[8,1024]{1,0:T(8,128)S(1)}, f32[8,1024]{1,0:T(8,128)S(1)}, u32[]{:S(2)}, u32[]{:S(2)}) collective-permute-start(f32[8,1024]{1,0:T(8,128)S(1)} %get-tuple-element.26), channel_id=1, source_target_pairs={{0,192},{1,193},{2,194},{3,195},{4,196},{5,197},{6,198},{7,199},{8... | collective-permute-start | bytes 98312 | tf_op jit(solution)/shard_map/ppermute | solution.py:296
  27.5 1.9 %collective-permute-done.5.left2_ref = f32[8,1024]{1,0:T(8,128)S(1)} collective-permute-done((f32[8,1024]{1,0:T(8,128)S(1)}, f32[8,1024]{1,0:T(8,128)S(1)}, u32[]{:S(2)}, u32[]{:S(2)}) %collective-permute-start.5) | collective-permute-done | bytes 32800 | tf_op jit(solution)/shard_map/ppermute | solution.py:296
  29.4 4.2 %collective-permute-done.6.right2_ref = f32[8,1024]{1,0:T(8,128)S(1)} collective-permute-done((f32[8,1024]{1,0:T(8,128)S(1)}, f32[8,1024]{1,0:T(8,128)S(1)}, u32[]{:S(2)}, u32[]{:S(2)}) %collective-permute-start.6) | collective-permute-done | bytes 32800 | tf_op jit(solution)/shard_map/ppermute | solution.py:296
  33.6 0.0 collective-permute-done.3.left_ref
  33.6 0.0 collective-permute-done.4.right_ref
  33.6 0.0 copy-done.2
  33.6 0.5 %shard_map.49 = f32[12,12,1024]{2,1,0:T(8,128)S(1)} custom-call(f32[8,192,128]{2,1,0:T(8,128)S(1)} %get-tuple-element.21.ya_ref, f32[8,48,128]{2,1,0:T(8,128)S(1)} %get-tuple-element.22.yb_ref, f32[56,1024]{1,0:T(8,128)S(1)} %collective-permute-done.3.left_ref, f32[56,1024]{1,0:T(8,128)S(1)} %collective-permute-done.4.right_ref, ...), custom_call_target="tpu_custom_call" | custom-call | tf_op jit(solution)/shard_map/pallas_call | solution.py:283
  34.0 1.4 %copy.5 = f32[1,12,12,1024]{3,0,2,1:T(1,128)} copy(f32[1,12,12,1024]{3,2,1,0:T(8,128)S(1)} %bitcast.4) | data formatting | bytes 1179648 | tf_op jit(solution)/shard_map/reshape | solution.py:326
  (1 shorter events, 0.0 us)
Async XLA Ops:
  0.0 1.3 %copy-start = (bf16[768,256]{1,0:T(8,128)(2,1)S(1)}, bf16[768,256]{1,0:T(8,128)(2,1)}, u32[]{:S(2)}) copy-start(bf16[768,256]{1,0:T(8,128)(2,1)} %constant.7.clone.low_ref) | copy-start | bytes 1179652
  0.0 1.3 %copy-start.1 = (bf16[512,256]{1,0:T(8,128)(2,1)S(1)}, bf16[512,256]{1,0:T(8,128)(2,1)}, u32[]{:S(2)}) copy-start(bf16[512,256]{1,0:T(8,128)(2,1)} %constant.6.clone.fine_ref) | copy-start | bytes 786436
  2.6 1.7 %collective-permute-start = (f32[72,1024]{1,0:T(8,128)S(1)}, f32[72,1024]{1,0:T(8,128)S(1)}, u32[]{:S(2)}, u32[]{:S(2)}) collective-permute-start(f32[72,1024]{1,0:T(8,128)S(1)} %get-tuple-element.18), channel_id=1, source_target_pairs={{0,1},{1,0},{2,3},{3,2},{4,5},{5,4},{6,7},{7,6},{8,9},{9,8},{10,11... | collective-permute-start | bytes 884744 | tf_op jit(solution)/shard_map/ppermute | solution.py:296
  4.3 16.0 %collective-permute-start.1 = (f32[56,1024]{1,0:T(8,128)S(1)}, f32[56,1024]{1,0:T(8,128)S(1)}, u32[]{:S(2)}, u32[]{:S(2)}) collective-permute-start(f32[56,1024]{1,0:T(8,128)S(1)} %shard_map.47), channel_id=1, source_target_pairs={{0,31},{1,2},{2,1},{3,4},{4,3},{5,6},{6,5},{7,8},{8,7},{9,10},{10,... | collective-permute-start | bytes 688136 | tf_op jit(solution)/shard_map/ppermute | solution.py:296
  12.9 7.4 %collective-permute-start.2 = (f32[16,1024]{1,0:T(8,128)S(1)}, f32[16,1024]{1,0:T(8,128)S(1)}, u32[]{:S(2)}, u32[]{:S(2)}) collective-permute-start(f32[16,1024]{1,0:T(8,128)S(1)} %get-tuple-element.20), channel_id=1, source_target_pairs={{0,30},{1,3},{2,0},{3,5},{4,2},{5,7},{6,4},{7,9},{8,6},{9,11},{10,... | collective-permute-start | bytes 196616 | tf_op jit(solution)/shard_map/ppermute | solution.py:296
  20.3 13.3 %copy-start.2 = (bf16[128,256]{1,0:T(8,128)(2,1)S(1)}, bf16[128,256]{1,0:T(8,128)(2,1)}, u32[]{:S(2)}) copy-start(bf16[128,256]{1,0:T(8,128)(2,1)} %constant.8.clone.spread_ref) | copy-start | bytes 196612
  21.8 11.7 %collective-permute-start.3 = (f32[56,1024]{1,0:T(8,128)S(1)}, f32[56,1024]{1,0:T(8,128)S(1)}, u32[]{:S(2)}, u32[]{:S(2)}) collective-permute-start(f32[56,1024]{1,0:T(8,128)S(1)} %get-tuple-element.23), channel_id=1, source_target_pairs={{0,32},{1,33},{2,34},{3,35},{4,36},{5,37},{6,38},{7,39},{8,40},{9,... | collective-permute-start | bytes 688136 | tf_op jit(solution)/shard_map/ppermute | solution.py:296
  23.1 10.4 %collective-permute-start.4 = (f32[56,1024]{1,0:T(8,128)S(1)}, f32[56,1024]{1,0:T(8,128)S(1)}, u32[]{:S(2)}, u32[]{:S(2)}) collective-permute-start(f32[56,1024]{1,0:T(8,128)S(1)} %get-tuple-element.24), channel_id=1, source_target_pairs={{0,224},{1,225},{2,226},{3,227},{4,228},{5,229},{6,230},{7,231},{8... | collective-permute-start | bytes 688136 | tf_op jit(solution)/shard_map/ppermute | solution.py:296
  23.9 5.4 %collective-permute-start.5 = (f32[8,1024]{1,0:T(8,128)S(1)}, f32[8,1024]{1,0:T(8,128)S(1)}, u32[]{:S(2)}, u32[]{:S(2)}) collective-permute-start(f32[8,1024]{1,0:T(8,128)S(1)} %get-tuple-element.25), channel_id=1, source_target_pairs={{0,64},{1,65},{2,66},{3,67},{4,68},{5,69},{6,70},{7,71},{8,72},{9,... | collective-permute-start | bytes 98312 | tf_op jit(solution)/shard_map/ppermute | solution.py:296
  26.5 7.1 %collective-permute-start.6 = (f32[8,1024]{1,0:T(8,128)S(1)}, f32[8,1024]{1,0:T(8,128)S(1)}, u32[]{:S(2)}, u32[]{:S(2)}) collective-permute-start(f32[8,1024]{1,0:T(8,128)S(1)} %get-tuple-element.26), channel_id=1, source_target_pairs={{0,192},{1,193},{2,194},{3,195},{4,196},{5,197},{6,198},{7,199},{8... | collective-permute-start | bytes 98312 | tf_op jit(solution)/shard_map/ppermute | solution.py:296

commit v3 on v2

v3 whole, which is shorter than its diff:
```python
import functools

import jax
import jax.numpy as jnp
import ml_dtypes
import numpy as np
from jax import lax
from jax.experimental import pallas as pl
from jax.experimental.pallas import tpu as pltpu
from jax.sharding import PartitionSpec as P

NEAR_D, FAR_D = 0.5625, 0.0625
NEAR_S, FAR_S = 0.28125, 0.03125
PLANES, ROWS, CELLS, LANES = 12, 12, 1024, 128
TILES = CELLS // LANES
PAIRS = ROWS // 2


def total(a, b):
    return b if a is None else a if b is None else a + b


def scaled(factor, a):
    return None if a is None else factor * a


def near_far(near, far, a, b, c, d):
    return total(scaled(near, total(a, b)), scaled(far, total(c, d)))


def lift(left, cells, right):
    pairs = len(cells) // 2
    e = {i: cells[2 * i] for i in range(pairs)}
    o = {i: cells[2 * i + 1] for i in range(pairs)}
    if left is not None:
        o[-2], e[-1], o[-1] = left
    if right is not None:
        e[pairs], o[pairs], e[pairs + 1] = right
    d = {
        j: total(o.get(j), near_far(-NEAR_D, FAR_D, e.get(j), e.get(j + 1), e.get(j - 1), e.get(j + 2)))
        for j in range(-2, pairs + 1)
    }
    s = [
        total(e[i], near_far(NEAR_S, -FAR_S, d[i - 1], d[i], d[i - 2], d[i + 1]))
        for i in range(pairs)
    ]
    return s, [d[i] for i in range(pairs)]


def edge_right(c):
    return [
        total(c[-3], near_far(-NEAR_D, FAR_D, c[-4], None, c[-6], None)),
        c[-2],
        total(c[-1], scaled(FAR_D, c[-4])),
    ]


def edge_left(c):
    return [c[0], total(c[1], scaled(FAR_D, c[4])), c[2]]


def coarse_terms(c):
    zeros = [None] * len(c)
    to_right, _ = lift(edge_right(c), zeros, None)
    to_left, _ = lift(None, zeros, edge_left(c))
    return to_right, to_left


def plus(a, b):
    return [total(x, y) for x, y in zip(a, b)]


def interleaved(s, d):
    return [row for pair in zip(s, d) for row in pair]


def lane(shape):
    return lax.broadcasted_iota(jnp.int32, shape, len(shape) - 1)


def band(size, step, first, count):
    v = np.eye(size)
    r = lambda k: np.roll(v, k * step, axis=1)
    at = np.arange(size) % (2 * step)
    d = v - (NEAR_D * (r(1) + r(-1)) - FAR_D * (r(3) + r(-3)))
    v = np.where(at == step, d, v)
    s = v + (NEAR_S * (r(1) + r(-1)) - FAR_S * (r(3) + r(-3)))
    v = np.where(at == 0, s, v)
    m = v[:, first:first + step * count:step]
    held = m.astype(ml_dtypes.bfloat16)
    assert (held.astype(np.float64) == m).all()
    return held


def parts(v):
    high = v.astype(jnp.bfloat16)
    rest = v - high.astype(jnp.float32)
    mid = rest.astype(jnp.bfloat16)
    return high, mid, (rest - mid.astype(jnp.float32)).astype(jnp.bfloat16)


def banded(tiles, m, start, count):
    chosen = [tiles[(start + i) % TILES] for i in range(count)]
    return sum(
        jnp.dot(jnp.concatenate(p, axis=1), m, preferred_element_type=jnp.float32) for p in zip(*chosen)
    )


def cut(t):
    return pl.ds(t * LANES, LANES)


NEAR, EDGE, Y_FAR, X_FAR = 66, 54, 12, 6


def at(count, t, start, size):
    return pl.ds(t * count + start, size)


def span_edges(a_ref, b_ref, t):
    a = [a_ref[t, pl.ds(y, PLANES, stride=ROWS), :] for y in range(ROWS)]
    b = [b_ref[t, pl.ds(y, PAIRS, stride=ROWS), :] for y in range(ROWS)]
    return a, b


def put_rows(ref, start, rows, t):
    count = ref.shape[0] // TILES
    for row in rows:
        ref[at(count, t, start, row.shape[0]), :] = row
        start += row.shape[0]
    return start


def get_rows(ref, start, size, number, t):
    count = ref.shape[0] // TILES
    return [ref[at(count, t, start + size * j, size), :] for j in range(number)]


def choose(odd, a, b):
    return [jnp.where(odd, x, y) for x, y in zip(a, b)]


def first_kernel(f_ref, fine_ref, low_ref, a_ref, b_ref, near_ref, other_ref, far_ref, in_ref, v_ref, sems):
    odd_core = lax.axis_index("span") % 2 == 1
    copies = []
    for g in range(4):
        rows = pl.ds(3 * g * ROWS * TILES, 3 * ROWS * TILES)
        copies.append(pltpu.make_async_copy(f_ref.at[rows], in_ref.at[rows], sems.at[g]))
        copies[-1].start()
    for copy in copies:
        copy.wait()
    tiles = [parts(in_ref[pl.ds(t, PLANES * ROWS, stride=TILES), :]) for t in range(TILES)]
    for q in range(4):
        block = banded(tiles, fine_ref[...], 2 * q - 1, 4)
        for t in range(2):
            a_ref[2 * q + t] = block[:, t * LANES:(t + 1) * LANES]
    tiles = [parts(a_ref[t]) for t in range(TILES)]
    for q in range(2):
        v_ref[:, pl.ds(256 * q, 256)] = banded(tiles, low_ref[...], 4 * q - 1, 6)
    for t in range(TILES):
        for k in range(PAIRS):
            b_ref[t, pl.ds(k * ROWS, ROWS), :] = v_ref[pl.ds((2 * k + t // 4) * ROWS, ROWS), cut(t % 4)]
    for t in range(TILES):
        a, b = span_edges(a_ref, b_ref, t)
        smooth, _ = lift(None, b, None)
        to_right, to_left = coarse_terms(b)
        far_right, far_left = edge_right(to_right), edge_left(to_left)
        far_right, far_left = [far_right[0], far_right[2]], [far_left[1], jnp.zeros_like(far_left[1])]
        right = edge_right(a) + edge_right(smooth)
        left = edge_left(a) + edge_left(smooth)
        put_rows(near_ref, 0, choose(odd_core, left + far_left, right + far_right), t)
        put_rows(other_ref, 0, choose(odd_core, right, left), t)
        put_rows(far_ref, 0, choose(odd_core, far_right, far_left), t)


def fold_kernel(other_ref, near_ref, out_ref):
    odd_core = lax.axis_index("span") % 2 == 1
    out_ref[...] = other_ref[...]
    for t in range(TILES):
        one, two = get_rows(near_ref, EDGE, PAIRS, 2, t)
        zero = jnp.zeros_like(one)
        terms = choose(odd_core, [one, zero, two], [zero, one, zero])
        put_rows(out_ref, 36, plus(get_rows(other_ref, 36, PAIRS, 3, t), terms), t)


def middle_kernel(a_ref, b_ref, near_ref, other_ref, far_ref, low_ref, ya_ref, yb_ref, xnear_ref, xother_ref, xfar_ref, xfar2_ref, halo_ref):
    odd_core = lax.axis_index("span") % 2 == 1
    odd_x = lax.axis_index("stream") % 2 == 1
    odd_pair = lax.axis_index("stream") // 2 % 2 == 1
    for side, ref in ((0, near_ref), (1, other_ref)):
        tiles = [parts(get_rows(ref, 0, 48, 1, t)[0]) for t in range(TILES)]
        for q in range(2):
            low = banded(tiles, low_ref[...], 4 * q - 1, 6)
            for t in range(2):
                halo_ref[2 * q + t, pl.ds(side * 48, 48), :] = low[:, t * LANES:(t + 1) * LANES]
    for t in range(TILES):
        a, b = span_edges(a_ref, b_ref, t)
        near, other = (get_rows(ref, 0, PLANES, 3, t) for ref in (near_ref, other_ref))
        smooth, detail = lift(choose(odd_core, near, other), a, choose(odd_core, other, near))
        for c in range(PAIRS):
            ya_ref[t, pl.ds(c, PLANES, stride=16), :] = smooth[c]
            ya_ref[t, pl.ds(8 + c, PLANES, stride=16), :] = detail[c]
        near, other = (
            [halo_ref[t % 4, pl.ds(48 * side + PLANES * j + t // 4, PAIRS, stride=2), :] for j in range(3)] for side in (0, 1)
        )
        smooth, _ = lift(choose(odd_core, near, other), b, choose(odd_core, other, near))
        to_right, to_left = coarse_terms(b)
        near, other = (get_rows(ref, 36, PAIRS, 3, t) for ref in (near_ref, other_ref))
        one, two = get_rows(far_ref, 0, PAIRS, 2, t)
        zero = jnp.zeros_like(one)
        left = plus(choose(odd_core, near, other), choose(odd_core, [one, zero, two], [zero, zero, zero]))
        right = plus(choose(odd_core, other, near), choose(odd_core, [zero, zero, zero], [zero, one, zero]))
        smooth, detail = lift(plus(left, edge_right(to_left)), smooth, plus(right, edge_left(to_right)))
        for c, row in enumerate(interleaved(smooth, detail)):
            yb_ref[t, pl.ds(c, PAIRS, stride=8), :] = row
    for t in range(TILES):
        a = stream_planes(ya_ref, t)
        right, left = edge_right(a), edge_left(a)
        for ref, planes in ((xnear_ref, choose(odd_x, left, right)), (xother_ref, choose(odd_x, right, left))):
            put_rows(ref, 0, [half for plane in planes for half in (plane[0:6], plane[8:14])], t)
    for t in range(4):
        b = low_planes(yb_ref, t)
        smooth, _ = lift(None, b, None)
        to_right, to_left = coarse_terms(b)
        for half, planes in ((0, b), (4, smooth)):
            right, left = edge_right(planes), edge_left(planes)
            put_rows(xnear_ref, 36, [plane[0:6] for plane in choose(odd_x, left, right)], t + half)
            put_rows(xother_ref, 36, [plane[0:6] for plane in choose(odd_x, right, left)], t + half)
        far_right, far_left = edge_right(to_right), edge_left(to_left)
        far_right, far_left = [far_right[0], far_right[2]], [far_left[1], jnp.zeros_like(far_left[1])]
        for half in (0, 1):
            put_rows(xfar_ref, 0, [choose(odd_pair, far_left, far_right)[half][0:6]], t + 4 * half)
            put_rows(xfar2_ref, 0, [choose(odd_pair, far_right, far_left)[half][0:6]], t + 4 * half)


def stream_planes(ya_ref, t):
    return [ya_ref[t, pl.ds(16 * x, 16), :] for x in range(PLANES)]


def low_planes(yb_ref, t):
    return [yb_ref[t + 4 * odd, pl.ds(8 * k, 8), :] for k in range(PAIRS) for odd in (0, 1)]


def last_kernel(ya_ref, yb_ref, xnear_ref, xother_ref, xfar_ref, xfar2_ref, spread_ref, out_ref, la_ref, lb_ref, c_ref, o_ref, sems):
    odd_x = lax.axis_index("stream") % 2 == 1
    odd_pair = lax.axis_index("stream") // 2 % 2 == 1
    even = (lane((8, LANES)) & 1) == 0
    for t in range(4):
        b = low_planes(yb_ref, t)
        near, other = (get_rows(ref, 36, 6, 3, t) + get_rows(ref, 36, 6, 3, t + 4) for ref in (xnear_ref, xother_ref))
        far, far2 = (get_rows(ref, 0, 6, 1, t) + get_rows(ref, 0, 6, 1, t + 4) for ref in (xfar_ref, xfar2_ref))
        rows = choose(odd_x, near, other) + choose(odd_x, other, near)
        rows += choose(odd_pair, far, far2) + choose(odd_pair, far2, far)[:1]
        for j, row in enumerate(rows):
            lb_ref[t, pl.ds(8 * j, 6), :] = row
        halo = [lb_ref[t, pl.ds(8 * j, 8), :] for j in range(15)]
        smooth, _ = lift(halo[0:3], b, halo[6:9])
        to_right, to_left = coarse_terms(b)
        left = plus(plus(halo[3:6], edge_right(to_left)), [halo[12], None, halo[13]])
        right = plus(plus(halo[9:12], edge_left(to_right)), [None, halo[14], None])
        for k, plane in enumerate(interleaved(*lift(left, smooth, right))):
            c_ref[pl.ds(8 * k, 8), cut(t)] = plane
    split = parts(c_ref[...])
    for t in range(TILES):
        near, other = (get_rows(ref, 0, 6, 6, t) for ref in (xnear_ref, xother_ref))
        for j, row in enumerate(choose(odd_x, near, other) + choose(odd_x, other, near)):
            la_ref[t, pl.ds(8 * j, 6), :] = row
        if t % 2 == 0:
            spread = sum(
                jnp.dot(p[:, t * 64:t * 64 + LANES], spread_ref[...], preferred_element_type=jnp.float32) for p in split
            )
        coarse = spread[:, (t % 2) * LANES:(t % 2 + 1) * LANES]
        a = stream_planes(ya_ref, t)
        halo = [la_ref[t, pl.ds(16 * j, 16), :] for j in range(6)]
        a_smooth, a_detail = lift(halo[:3], a, halo[3:])
        for k in range(PAIRS):
            for x, plane in ((2 * k, a_smooth[k]), (2 * k + 1, a_detail[k])):
                low, high = plane[0:8], plane[8:16]
                if x % 2 == 0:
                    low = jnp.where(even, coarse[8 * k:8 * k + 8], low)
                row = x * ROWS * TILES + t
                o_ref[pl.ds(row, PAIRS, stride=2 * TILES), :] = low[0:6]
                o_ref[pl.ds(row + TILES, PAIRS, stride=2 * TILES), :] = high[0:6]
    copies = []
    for g in range(4):
        rows = pl.ds(3 * g * ROWS * TILES, 3 * ROWS * TILES)
        copies.append(pltpu.make_async_copy(o_ref.at[rows], out_ref.at[rows], sems.at[g]))
        copies[-1].start()
    for copy in copies:
        copy.wait()


VMEM = pl.BlockSpec(memory_space=pltpu.VMEM)
HBM = pl.BlockSpec(memory_space=pltpu.HBM)


def call(kernel, shapes, args, scratch=(), sems=0, ins=VMEM, outs=VMEM):
    return pl.pallas_call(
        kernel,
        out_shape=[jax.ShapeDtypeStruct(s, jnp.float32) for s in shapes],
        in_specs=[ins] + [VMEM] * (len(args) - 1),
        out_specs=[outs] + [VMEM] * (len(shapes) - 1),
        scratch_shapes=[pltpu.VMEM(s, jnp.float32) for s in scratch] + [pltpu.SemaphoreType.DMA((sems,))] * (sems > 0),
        compiler_params=pltpu.CompilerParams(vmem_limit_bytes=16 << 20),
    )(*args)


def message(count):
    return (TILES * count, LANES)


def local(streams, spans, fields):
    def send(rows, target):
        pairs = [(s * spans + y, (lambda q: q[0] % streams * spans + q[1] % spans)(target(s, y))) for s in range(streams) for y in range(spans)]
        return lax.ppermute(rows, ("stream", "span"), pairs)

    fine, low = jnp.asarray(band(512, 1, 128, 256)), jnp.asarray(band(768, 2, 128, 256))
    spread = jnp.asarray(np.repeat(np.eye(LANES), 2, axis=1) * (np.arange(2 * LANES) % 2 == 0), jnp.bfloat16)
    block = (PLANES * ROWS * TILES, LANES)
    a, b, near, other, far = call(
        first_kernel,
        [(TILES, PLANES * ROWS, LANES), (TILES, PAIRS * ROWS, LANES), message(NEAR), message(EDGE), message(Y_FAR)],
        [fields.reshape(block), fine, low],
        [block, (PLANES * ROWS, CELLS)],
        sems=4,
        ins=HBM,
    )
    near = send(near, lambda s, y: (s, y ^ 1))
    far = send(far, lambda s, y: (s, y + (2 if y % 2 else -2)))
    (other,) = call(fold_kernel, [message(EDGE)], [other, near])
    other = send(other, lambda s, y: (s, y + (1 if y % 2 else -1)))
    ya, yb, xnear, xother, xfar, xfar2 = call(
        middle_kernel,
        [(TILES, PLANES * 16, LANES), (TILES, PAIRS * 8, LANES), message(EDGE), message(EDGE), message(X_FAR), message(X_FAR)],
        [a, b, near, other, far, low],
        [(4, 96, LANES)],
    )
    xnear = send(xnear, lambda s, y: (s ^ 1, y))
    xother = send(xother, lambda s, y: (s + (1 if s % 2 else -1), y))
    xfar = send(xfar, lambda s, y: (s + (-2 if s // 2 % 2 else 2), y))
    xfar2 = send(xfar2, lambda s, y: (s + (2 if s // 2 % 2 else -2), y))
    (out,) = call(
        last_kernel,
        [block],
        [ya, yb, xnear, xother, xfar, xfar2, spread],
        [(TILES, 96, LANES), (4, 120, LANES), (48, CELLS // 2), block],
        sems=4,
        outs=HBM,
    )
    return out.reshape(fields.shape)


def solution(mesh):
    return jax.shard_map(
        functools.partial(local, mesh.shape["stream"], mesh.shape["span"]),
        mesh=mesh,
        in_specs=(P(None, "stream", "span", None),),
        out_specs=P(None, "stream", "span", None),
        check_vma=False,
    )
```

time: 35.5 us -> 36.1 us (1.017); the launches traced: 35.5 us -> 35.6 us
  Pallas kernels: 3.36 us -> 4.89 us
  waiting for transfers between devices: 14.3 us -> 13.1 us
  starting transfers between devices: 15 us -> 14.5 us
    unnamed x7 -> x10, local copies, waits for them, and re-layouts: 1.26 us -> 3.02 us
    pallas_call x4, Pallas kernels: 3.36 us -> 4.89 us  [call(): pl.pallas_call(kernel, out_shape=[jax.ShapeDtypeStruct(s, jnp.float32) fo...]
    reshape x1 -> x0, local copies, waits for them, and re-layouts: 1.42 us -> none  [local(): return out.reshape(fields.shape)]
    ppermute x7, waiting for transfers between devices: 14.3 us -> 13.1 us  [send(): return lax.ppermute(rows, ('stream', 'span'), pairs)]
    ppermute x7, starting transfers between devices: 15 us -> 14.5 us  [send(): return lax.ppermute(rows, ('stream', 'span'), pairs)]
where the time goes in v3:
time: 36.1 us; the launch traced here: 35.6 us
  starting transfers between devices  14.5 us (40%)
  waiting for transfers between devices  13.1 us (36%)
  Pallas kernels  4.89 us (14%)
  local copies, waits for them, and re-layouts  3.02 us (8%)
    ppermute x7, starting transfers between devices, send(): return lax.ppermute(rows, ('stream', 'span'), pairs)  14.5 us
    ppermute x7, waiting for transfers between devices, send(): return lax.ppermute(rows, ('stream', 'span'), pairs)  13.1 us
    pallas_call x4, Pallas kernels, call(): pl.pallas_call(kernel, out_shape=[jax.ShapeDtypeStruct(s, jnp.float32) fo...  4.89 us
    unnamed x10, local copies, waits for them, and re-layouts  3.02 us
  transfers between devices with their start and end apart: 7, of which 4 were waited for; matrix products, arithmetic and copies ran while one was open for 0% of the time, Pallas kernels for 0%

profile of v3, /device:TPU:4, one launch (start us, length us, event | category | flops | bytes accessed | tf_op | source)
XLA Modules:
  0.0 35.6 jit_solution(14104986621176483407)
XLA Ops:
  0.0 0.0 copy-start
  0.0 1.0 %copy-done = bf16[768,256]{1,0:T(8,128)(2,1)S(1)} copy-done((bf16[768,256]{1,0:T(8,128)(2,1)S(1)}, bf16[768,256]{1,0:T(8,128)(2,1)}, u32[]{:S(2)}) %copy-start) | copy-done | bytes 393240
  1.0 0.0 copy-start.2
  1.0 1.1 %copy-done.2 = f32[1,12,12,1024]{3,0,2,1:T(1,128)S(1)} copy-done((f32[1,12,12,1024]{3,0,2,1:T(1,128)S(1)}, f32[1,12,12,1024]{3,0,2,1:T(1,128)}, u32[]{:S(2)}) %copy-start.2) | copy-done | bytes 589848
  2.1 0.0 copy-start.3
  2.1 0.9 %copy-done.3 = bf16[512,256]{1,0:T(8,128)(2,1)S(1)} copy-done((bf16[512,256]{1,0:T(8,128)(2,1)S(1)}, bf16[512,256]{1,0:T(8,128)(2,1)}, u32[]{:S(2)}) %copy-start.3) | copy-done | bytes 262168
  3.0 2.0 %shard_map.46 = (f32[8,144,128]{2,1,0:T(8,128)S(1)}, f32[8,72,128]{2,1,0:T(8,128)S(1)}, f32[528,128]{1,0:T(8,128)S(1)}, f32[432,128]{1,0:T(8,128)S(1)}, f32[96,128]{1,0:T(8,128)S(1)}) custom-call(f32[1152,128]{1,0:T(8,128)S(1)} %bitcast.2, bf16[512,256]{1,0:T(8,128)(2,1)S(1)} %copy-done.3, bf16[768,256]{1,0:T(8,128)(2,1)S(1)} %copy-done), custom_call_target="tpu_custom_call" | custom-call | tf_op jit(solution)/shard_map/pallas_call | solution.py:298
  5.1 0.0 copy-start.1
  5.1 0.1 collective-permute-start
  5.2 1.5 %collective-permute-done.near_ref = f32[528,128]{1,0:T(8,128)S(1)} collective-permute-done((f32[528,128]{1,0:T(8,128)S(1)}, f32[528,128]{1,0:T(8,128)S(1)}, u32[]{:S(2)}, u32[]{:S(2)}) %collective-permute-start) | collective-permute-done | bytes 270368 | tf_op jit(solution)/shard_map/ppermute | solution.py:315
  6.7 8.6 %collective-permute-start.1 = (f32[432,128]{1,0:T(8,128)S(1)}, f32[432,128]{1,0:T(8,128)S(1)}, u32[]{:S(2)}, u32[]{:S(2)}) collective-permute-start(f32[432,128]{1,0:T(8,128)S(1)} %shard_map.47), channel_id=1, source_target_pairs={{0,31},{1,2},{2,1},{3,4},{4,3},{5,6},{6,5},{7,8},{8,7},{9,10},{10,... | collective-permute-start | bytes 663560 | tf_op jit(solution)/shard_map/ppermute | solution.py:315
  15.3 0.7 %collective-permute-start.2 = (f32[96,128]{1,0:T(8,128)S(1)}, f32[96,128]{1,0:T(8,128)S(1)}, u32[]{:S(2)}, u32[]{:S(2)}) collective-permute-start(f32[96,128]{1,0:T(8,128)S(1)} %get-tuple-element.20), channel_id=1, source_target_pairs={{0,30},{1,3},{2,0},{3,5},{4,2},{5,7},{6,4},{7,9},{8,6},{9,11},{10,... | collective-permute-start | bytes 147464 | tf_op jit(solution)/shard_map/ppermute | solution.py:315
  16.1 6.2 %collective-permute-done.2.far_ref = f32[96,128]{1,0:T(8,128)S(1)} collective-permute-done((f32[96,128]{1,0:T(8,128)S(1)}, f32[96,128]{1,0:T(8,128)S(1)}, u32[]{:S(2)}, u32[]{:S(2)}) %collective-permute-start.2) | collective-permute-done | bytes 49184 | tf_op jit(solution)/shard_map/ppermute | solution.py:315
  22.2 0.0 collective-permute-done.1.other_ref
  22.2 0.0 copy-done.1
  22.2 0.0 copy-start.4
  22.2 1.4 %shard_map.48 = (f32[8,192,128]{2,1,0:T(8,128)S(1)}, f32[8,48,128]{2,1,0:T(8,128)S(1)}, f32[432,128]{1,0:T(8,128)S(1)}, f32[432,128]{1,0:T(8,128)S(1)}, f32[48,128]{1,0:T(8,128)S(1)}, /*index=5*/f32[48,128]{1,0:T(8,128)S(1)}) custom-call(f32[8,144,128]{2,1,0:T(8,128)S(1)} %get-tuple-element.16.a_ref, f32[8,72,128]{2,1,0:T(8,128)S(1)} %get-tuple-element.17.b_ref, ...), custom_call_target="tpu_custom_call" | custom-call | tf_op jit(solution)/shard_map/pallas_call | solution.py:298
  23.7 1.3 %collective-permute-start.3 = (f32[432,128]{1,0:T(8,128)S(1)}, f32[432,128]{1,0:T(8,128)S(1)}, u32[]{:S(2)}, u32[]{:S(2)}) collective-permute-start(f32[432,128]{1,0:T(8,128)S(1)} %get-tuple-element.23), channel_id=1, source_target_pairs={{0,32},{1,33},{2,34},{3,35},{4,36},{5,37},{6,38},{7,39},{8,40},{9,... | collective-permute-start | bytes 663560 | tf_op jit(solution)/shard_map/ppermute | solution.py:315
  25.0 0.0 collective-permute-start.4
  25.0 3.0 %collective-permute-start.5 = (f32[48,128]{1,0:T(8,128)S(1)}, f32[48,128]{1,0:T(8,128)S(1)}, u32[]{:S(2)}, u32[]{:S(2)}) collective-permute-start(f32[48,128]{1,0:T(8,128)S(1)} %get-tuple-element.25), channel_id=1, source_target_pairs={{0,64},{1,65},{2,66},{3,67},{4,68},{5,69},{6,70},{7,71},{8,72},{9,... | collective-permute-start | bytes 73736 | tf_op jit(solution)/shard_map/ppermute | solution.py:315
  27.9 0.8 %collective-permute-start.6 = (f32[48,128]{1,0:T(8,128)S(1)}, f32[48,128]{1,0:T(8,128)S(1)}, u32[]{:S(2)}, u32[]{:S(2)}) collective-permute-start(f32[48,128]{1,0:T(8,128)S(1)} %get-tuple-element.26), channel_id=1, source_target_pairs={{0,192},{1,193},{2,194},{3,195},{4,196},{5,197},{6,198},{7,199},{8... | collective-permute-start | bytes 73736 | tf_op jit(solution)/shard_map/ppermute | solution.py:315
  28.8 1.6 %collective-permute-done.5.xfar_ref = f32[48,128]{1,0:T(8,128)S(1)} collective-permute-done((f32[48,128]{1,0:T(8,128)S(1)}, f32[48,128]{1,0:T(8,128)S(1)}, u32[]{:S(2)}, u32[]{:S(2)}) %collective-permute-start.5) | collective-permute-done | bytes 24608 | tf_op jit(solution)/shard_map/ppermute | solution.py:315
  30.4 3.8 %collective-permute-done.6.xfar2_ref = f32[48,128]{1,0:T(8,128)S(1)} collective-permute-done((f32[48,128]{1,0:T(8,128)S(1)}, f32[48,128]{1,0:T(8,128)S(1)}, u32[]{:S(2)}, u32[]{:S(2)}) %collective-permute-start.6) | collective-permute-done | bytes 24608 | tf_op jit(solution)/shard_map/ppermute | solution.py:315
  34.2 0.0 collective-permute-done.3.xnear_ref
  34.2 0.0 collective-permute-done.4.xother_ref
  34.2 0.0 copy-done.4
  34.2 1.4 %shard_map.49 = f32[1152,128]{1,0:T(8,128)} custom-call(f32[8,192,128]{2,1,0:T(8,128)S(1)} %get-tuple-element.21.ya_ref, f32[8,48,128]{2,1,0:T(8,128)S(1)} %get-tuple-element.22.yb_ref, f32[432,128]{1,0:T(8,128)S(1)} %collective-permute-done.3.xnear_ref, f32[432,128]{1,0:T(8,128)S(1)} %collective-permute-done.4.xother_ref, ...), custom_call_target="tpu_custom_call" | custom-call | tf_op jit(solution)/shard_map/pallas_call | solution.py:298
  (1 shorter events, 0.0 us)
Async XLA Ops:
  0.0 1.0 %copy-start = (bf16[768,256]{1,0:T(8,128)(2,1)S(1)}, bf16[768,256]{1,0:T(8,128)(2,1)}, u32[]{:S(2)}) copy-start(bf16[768,256]{1,0:T(8,128)(2,1)} %constant.7.clone.low_ref) | copy-start | bytes 1179652
  1.0 1.1 %copy-start.2 = (f32[1,12,12,1024]{3,0,2,1:T(1,128)S(1)}, f32[1,12,12,1024]{3,0,2,1:T(1,128)}, u32[]{:S(2)}) copy-start(f32[1,12,12,1024]{3,0,2,1:T(1,128)} %param.4) | copy-start | bytes 1769476
  2.1 0.9 %copy-start.3 = (bf16[512,256]{1,0:T(8,128)(2,1)S(1)}, bf16[512,256]{1,0:T(8,128)(2,1)}, u32[]{:S(2)}) copy-start(bf16[512,256]{1,0:T(8,128)(2,1)} %constant.6.clone.fine_ref) | copy-start | bytes 786436
  5.1 17.2 %copy-start.1 = (bf16[768,256]{1,0:T(8,128)(2,1)S(1)}, bf16[768,256]{1,0:T(8,128)(2,1)}, u32[]{:S(2)}) copy-start(bf16[768,256]{1,0:T(8,128)(2,1)} %constant.7.clone.low_ref) | copy-start | bytes 1179652
  5.1 1.6 %collective-permute-start = (f32[528,128]{1,0:T(8,128)S(1)}, f32[528,128]{1,0:T(8,128)S(1)}, u32[]{:S(2)}, u32[]{:S(2)}) collective-permute-start(f32[528,128]{1,0:T(8,128)S(1)} %get-tuple-element.18), channel_id=1, source_target_pairs={{0,1},{1,0},{2,3},{3,2},{4,5},{5,4},{6,7},{7,6},{8,9},{9,8},{10,11... | collective-permute-start | bytes 811016 | tf_op jit(solution)/shard_map/ppermute | solution.py:315
  6.7 15.5 %collective-permute-start.1 = (f32[432,128]{1,0:T(8,128)S(1)}, f32[432,128]{1,0:T(8,128)S(1)}, u32[]{:S(2)}, u32[]{:S(2)}) collective-permute-start(f32[432,128]{1,0:T(8,128)S(1)} %shard_map.47), channel_id=1, source_target_pairs={{0,31},{1,2},{2,1},{3,4},{4,3},{5,6},{6,5},{7,8},{8,7},{9,10},{10,... | collective-permute-start | bytes 663560 | tf_op jit(solution)/shard_map/ppermute | solution.py:315
  15.3 6.9 %collective-permute-start.2 = (f32[96,128]{1,0:T(8,128)S(1)}, f32[96,128]{1,0:T(8,128)S(1)}, u32[]{:S(2)}, u32[]{:S(2)}) collective-permute-start(f32[96,128]{1,0:T(8,128)S(1)} %get-tuple-element.20), channel_id=1, source_target_pairs={{0,30},{1,3},{2,0},{3,5},{4,2},{5,7},{6,4},{7,9},{8,6},{9,11},{10,... | collective-permute-start | bytes 147464 | tf_op jit(solution)/shard_map/ppermute | solution.py:315
  22.2 11.9 %copy-start.4 = (bf16[128,256]{1,0:T(8,128)(2,1)S(1)}, bf16[128,256]{1,0:T(8,128)(2,1)}, u32[]{:S(2)}) copy-start(bf16[128,256]{1,0:T(8,128)(2,1)} %constant.8.clone.spread_ref) | copy-start | bytes 196612
  23.7 10.5 %collective-permute-start.3 = (f32[432,128]{1,0:T(8,128)S(1)}, f32[432,128]{1,0:T(8,128)S(1)}, u32[]{:S(2)}, u32[]{:S(2)}) collective-permute-start(f32[432,128]{1,0:T(8,128)S(1)} %get-tuple-element.23), channel_id=1, source_target_pairs={{0,32},{1,33},{2,34},{3,35},{4,36},{5,37},{6,38},{7,39},{8,40},{9,... | collective-permute-start | bytes 663560 | tf_op jit(solution)/shard_map/ppermute | solution.py:315
  25.0 9.2 %collective-permute-start.4 = (f32[432,128]{1,0:T(8,128)S(1)}, f32[432,128]{1,0:T(8,128)S(1)}, u32[]{:S(2)}, u32[]{:S(2)}) collective-permute-start(f32[432,128]{1,0:T(8,128)S(1)} %get-tuple-element.24), channel_id=1, source_target_pairs={{0,224},{1,225},{2,226},{3,227},{4,228},{5,229},{6,230},{7,231},{8... | collective-permute-start | bytes 663560 | tf_op jit(solution)/shard_map/ppermute | solution.py:315
  25.0 5.4 %collective-permute-start.5 = (f32[48,128]{1,0:T(8,128)S(1)}, f32[48,128]{1,0:T(8,128)S(1)}, u32[]{:S(2)}, u32[]{:S(2)}) collective-permute-start(f32[48,128]{1,0:T(8,128)S(1)} %get-tuple-element.25), channel_id=1, source_target_pairs={{0,64},{1,65},{2,66},{3,67},{4,68},{5,69},{6,70},{7,71},{8,72},{9,... | collective-permute-start | bytes 73736 | tf_op jit(solution)/shard_map/ppermute | solution.py:315
  27.9 6.2 %collective-permute-start.6 = (f32[48,128]{1,0:T(8,128)S(1)}, f32[48,128]{1,0:T(8,128)S(1)}, u32[]{:S(2)}, u32[]{:S(2)}) collective-permute-start(f32[48,128]{1,0:T(8,128)S(1)} %get-tuple-element.26), channel_id=1, source_target_pairs={{0,192},{1,193},{2,194},{3,195},{4,196},{5,197},{6,198},{7,199},{8... | collective-permute-start | bytes 73736 | tf_op jit(solution)/shard_map/ppermute | solution.py:315

commit v4 on v3

--- a/solution.py
+++ b/solution.py
@@ -78,18 +78,39 @@
     return lax.broadcasted_iota(jnp.int32, shape, len(shape) - 1)
 
 
-def band(size, step, first, count):
-    v = np.eye(size)
-    r = lambda k: np.roll(v, k * step, axis=1)
-    at = np.arange(size) % (2 * step)
-    d = v - (NEAR_D * (r(1) + r(-1)) - FAR_D * (r(3) + r(-3)))
-    v = np.where(at == step, d, v)
-    s = v + (NEAR_S * (r(1) + r(-1)) - FAR_S * (r(3) + r(-3)))
-    v = np.where(at == 0, s, v)
-    m = v[:, first:first + step * count:step]
-    held = m.astype(ml_dtypes.bfloat16)
-    assert (held.astype(np.float64) == m).all()
-    return held
+def cut(t):
+    return pl.ds(t * LANES, LANES)
+
+
+def taps():
+    v = np.eye(32)
+    at = np.arange(32) % 2
+    r = lambda k: np.roll(v, k, axis=1)
+    v = np.where(at == 1, v - (NEAR_D * (r(1) + r(-1)) - FAR_D * (r(3) + r(-3))), v)
+    v = np.where(at == 0, v + (NEAR_S * (r(1) + r(-1)) - FAR_S * (r(3) + r(-3))), v)
+    assert (v == v.astype(ml_dtypes.bfloat16).astype(np.float64)).all()
+    found = {k: (float(v[16 + k, 16]), float(v[17 + k, 17])) for k in range(-8, 9)}
+    return {k: pair for k, pair in found.items() if any(pair)}
+
+
+def table_kernel(fine_ref, low_ref):
+    i, j = (lax.broadcasted_iota(jnp.int32, (LANES, LANES), axis) for axis in (0, 1))
+    smooth = (j & 1) == 0
+    value = {k: jnp.where(smooth, *pair) for k, pair in taps().items()}
+
+    def block(step, tile):
+        offset = i + tile * LANES - step * j
+        out = jnp.zeros((LANES, LANES), jnp.float32)
+        for k, v in value.items():
+            out = jnp.where(offset == step * k, v, out)
+        return out.astype(jnp.bfloat16)
+
+    for ref, step in ((fine_ref, 1), (low_ref, 2)):
+        ref[...] = jnp.zeros(ref.shape, jnp.bfloat16)
+        for n in range(step + 2):
+            one = block(step, n - 1)
+            for column in (0, 1):
+                ref[pl.ds((n + step * column) * LANES, LANES), cut(column)] = one
 
 
 def parts(v):
@@ -104,10 +125,6 @@
     return sum(
         jnp.dot(jnp.concatenate(p, axis=1), m, preferred_element_type=jnp.float32) for p in zip(*chosen)
     )
-
-
-def cut(t):
-    return pl.ds(t * LANES, LANES)
 
 
 NEAR, EDGE, Y_FAR, X_FAR = 66, 54, 12, 6
@@ -140,16 +157,9 @@
     return [jnp.where(odd, x, y) for x, y in zip(a, b)]
 
 
-def first_kernel(f_ref, fine_ref, low_ref, a_ref, b_ref, near_ref, other_ref, far_ref, in_ref, v_ref, sems):
+def first_kernel(f_ref, fine_ref, low_ref, a_ref, b_ref, near_ref, other_ref, far_ref, v_ref):
     odd_core = lax.axis_index("span") % 2 == 1
-    copies = []
-    for g in range(4):
-        rows = pl.ds(3 * g * ROWS * TILES, 3 * ROWS * TILES)
-        copies.append(pltpu.make_async_copy(f_ref.at[rows], in_ref.at[rows], sems.at[g]))
-        copies[-1].start()
-    for copy in copies:
-        copy.wait()
-    tiles = [parts(in_ref[pl.ds(t, PLANES * ROWS, stride=TILES), :]) for t in range(TILES)]
+    tiles = [parts(f_ref[pl.ds(t, PLANES * ROWS, stride=TILES), :]) for t in range(TILES)]
     for q in range(4):
         block = banded(tiles, fine_ref[...], 2 * q - 1, 4)
         for t in range(2):
@@ -241,10 +251,29 @@
     return [yb_ref[t + 4 * odd, pl.ds(8 * k, 8), :] for k in range(PAIRS) for odd in (0, 1)]
 
 
-def last_kernel(ya_ref, yb_ref, xnear_ref, xother_ref, xfar_ref, xfar2_ref, spread_ref, out_ref, la_ref, lb_ref, c_ref, o_ref, sems):
+def last_kernel(ya_ref, yb_ref, xnear_ref, xother_ref, xfar_ref, xfar2_ref, out_ref, la_ref, lb_ref, c_ref, o_ref, sems):
     odd_x = lax.axis_index("stream") % 2 == 1
     odd_pair = lax.axis_index("stream") // 2 % 2 == 1
-    even = (lane((8, LANES)) & 1) == 0
+
+    def rows_of(x, y, t):
+        return pl.ds((x * ROWS + y) * TILES + t, PAIRS, stride=2 * TILES)
+
+    def leave(x):
+        rows = pl.ds(x * ROWS * TILES, ROWS * TILES)
+        copy = pltpu.make_async_copy(o_ref.at[rows], out_ref.at[rows], sems.at[x])
+        copy.start()
+        return copy
+
+    for t in range(TILES):
+        near, other = (get_rows(ref, 0, 6, 6, t) for ref in (xnear_ref, xother_ref))
+        for j, row in enumerate(choose(odd_x, near, other) + choose(odd_x, other, near)):
+            la_ref[t, pl.ds(8 * j, 6), :] = row
+        a = stream_planes(ya_ref, t)
+        halo = [la_ref[t, pl.ds(16 * j, 16), :] for j in range(6)]
+        for x, plane in enumerate(interleaved(*lift(halo[:3], a, halo[3:]))):
+            o_ref[rows_of(x, 0, t), :] = plane[0:6]
+            o_ref[rows_of(x, 1, t), :] = plane[8:14]
+    copies = [leave(x) for x in range(1, PLANES, 2)]
     for t in range(4):
         b = low_planes(yb_ref, t)
         near, other = (get_rows(ref, 36, 6, 3, t) + get_rows(ref, 36, 6, 3, t + 4) for ref in (xnear_ref, xother_ref))
@@ -260,32 +289,20 @@
         right = plus(plus(halo[9:12], edge_left(to_right)), [None, halo[14], None])
         for k, plane in enumerate(interleaved(*lift(left, smooth, right))):
             c_ref[pl.ds(8 * k, 8), cut(t)] = plane
+    i, j = (lax.broadcasted_iota(jnp.int32, (LANES, 2 * LANES), axis) for axis in (0, 1))
+    spread = jnp.where(j == 2 * i, 1.0, 0.0).astype(jnp.bfloat16)
+    even = (lane((6, LANES)) & 1) == 0
     split = parts(c_ref[...])
-    for t in range(TILES):
-        near, other = (get_rows(ref, 0, 6, 6, t) for ref in (xnear_ref, xother_ref))
-        for j, row in enumerate(choose(odd_x, near, other) + choose(odd_x, other, near)):
-            la_ref[t, pl.ds(8 * j, 6), :] = row
-        if t % 2 == 0:
-            spread = sum(
-                jnp.dot(p[:, t * 64:t * 64 + LANES], spread_ref[...], preferred_element_type=jnp.float32) for p in split
-            )
-        coarse = spread[:, (t % 2) * LANES:(t % 2 + 1) * LANES]
-        a = stream_planes(ya_ref, t)
-        halo = [la_ref[t, pl.ds(16 * j, 16), :] for j in range(6)]
-        a_smooth, a_detail = lift(halo[:3], a, halo[3:])
-        for k in range(PAIRS):
-            for x, plane in ((2 * k, a_smooth[k]), (2 * k + 1, a_detail[k])):
-                low, high = plane[0:8], plane[8:16]
-                if x % 2 == 0:
-                    low = jnp.where(even, coarse[8 * k:8 * k + 8], low)
-                row = x * ROWS * TILES + t
-                o_ref[pl.ds(row, PAIRS, stride=2 * TILES), :] = low[0:6]
-                o_ref[pl.ds(row + TILES, PAIRS, stride=2 * TILES), :] = high[0:6]
-    copies = []
-    for g in range(4):
-        rows = pl.ds(3 * g * ROWS * TILES, 3 * ROWS * TILES)
-        copies.append(pltpu.make_async_copy(o_ref.at[rows], out_ref.at[rows], sems.at[g]))
-        copies[-1].start()
+    for t in range(0, TILES, 2):
+        wide = sum(
+            jnp.dot(p[:, t * 64:t * 64 + LANES], spread, preferred_element_type=jnp.float32) for p in split
+        )
+        for half in (0, 1):
+            for k in range(PAIRS):
+                rows = rows_of(2 * k, 0, t + half)
+                coarse = wide[8 * k:8 * k + 6, half * LANES:(half + 1) * LANES]
+                o_ref[rows, :] = jnp.where(even, coarse, o_ref[rows, :])
+    copies += [leave(x) for x in range(0, PLANES, 2)]
     for copy in copies:
         copy.wait()
 
@@ -294,14 +311,15 @@
 HBM = pl.BlockSpec(memory_space=pltpu.HBM)
 
 
-def call(kernel, shapes, args, scratch=(), sems=0, ins=VMEM, outs=VMEM):
+def call(kernel, shapes, args, scratch=(), sems=0, out=VMEM, kind=jnp.float32, cost=None):
     return pl.pallas_call(
         kernel,
-        out_shape=[jax.ShapeDtypeStruct(s, jnp.float32) for s in shapes],
-        in_specs=[ins] + [VMEM] * (len(args) - 1),
-        out_specs=[outs] + [VMEM] * (len(shapes) - 1),
+        out_shape=[jax.ShapeDtypeStruct(s, kind) for s in shapes],
+        in_specs=[VMEM] * len(args),
+        out_specs=[out] + [VMEM] * (len(shapes) - 1),
         scratch_shapes=[pltpu.VMEM(s, jnp.float32) for s in scratch] + [pltpu.SemaphoreType.DMA((sems,))] * (sems > 0),
         compiler_params=pltpu.CompilerParams(vmem_limit_bytes=16 << 20),
+        cost_estimate=cost,
     )(*args)
 
 
@@ -314,16 +332,14 @@
         pairs = [(s * spans + y, (lambda q: q[0] % streams * spans + q[1] % spans)(target(s, y))) for s in range(streams) for y in range(spans)]
         return lax.ppermute(rows, ("stream", "span"), pairs)
 
-    fine, low = jnp.asarray(band(512, 1, 128, 256)), jnp.asarray(band(768, 2, 128, 256))
-    spread = jnp.asarray(np.repeat(np.eye(LANES), 2, axis=1) * (np.arange(2 * LANES) % 2 == 0), jnp.bfloat16)
+    cost = pl.CostEstimate(flops=10**9, bytes_accessed=10**6, transcendentals=0)
+    fine, low = call(table_kernel, [(4 * LANES, 2 * LANES), (6 * LANES, 2 * LANES)], [], kind=jnp.bfloat16, cost=cost)
     block = (PLANES * ROWS * TILES, LANES)
     a, b, near, other, far = call(
         first_kernel,
         [(TILES, PLANES * ROWS, LANES), (TILES, PAIRS * ROWS, LANES), message(NEAR), message(EDGE), message(Y_FAR)],
         [fields.reshape(block), fine, low],
-        [block, (PLANES * ROWS, CELLS)],
-        sems=4,
-        ins=HBM,
+        [(PLANES * ROWS, CELLS // 2)],
     )
     near = send(near, lambda s, y: (s, y ^ 1))
     far = send(far, lambda s, y: (s, y + (2 if y % 2 else -2)))
@@ -342,10 +358,10 @@
     (out,) = call(
         last_kernel,
         [block],
-        [ya, yb, xnear, xother, xfar, xfar2, spread],
+        [ya, yb, xnear, xother, xfar, xfar2],
         [(TILES, 96, LANES), (4, 120, LANES), (48, CELLS // 2), block],
-        sems=4,
-        outs=HBM,
+        sems=PLANES,
+        out=HBM,
     )
     return out.reshape(fields.shape)
 

time: 36.1 us -> 33.3 us (0.922)
  local copies, waits for them, and re-layouts: 3.02 us -> 0.75 us
  Pallas kernels: 4.89 us -> 4.43 us
    unnamed x10 -> x2, local copies, waits for them, and re-layouts: 3.02 us -> 0.75 us
    pallas_call x4 -> x5, Pallas kernels: 4.89 us -> 4.43 us  [call(): pl.pallas_call(kernel, out_shape=[jax.ShapeDtypeStruct(s, kind) for s in...]
where the time goes in v4:
time: 33.3 us; the launch traced here: 32.8 us
  starting transfers between devices  14.5 us (44%)
  waiting for transfers between devices  13.1 us (39%)
  Pallas kernels  4.43 us (13%)
  local copies, waits for them, and re-layouts  0.75 us (2%)
    ppermute x7, starting transfers between devices, send(): return lax.ppermute(rows, ('stream', 'span'), pairs)  14.5 us
    ppermute x7, waiting for transfers between devices, send(): return lax.ppermute(rows, ('stream', 'span'), pairs)  13.1 us
    pallas_call x5, Pallas kernels, call(): pl.pallas_call(kernel, out_shape=[jax.ShapeDtypeStruct(s, kind) for s in...  4.43 us
    unnamed x2, local copies, waits for them, and re-layouts  0.75 us
  transfers between devices with their start and end apart: 7, of which 4 were waited for; matrix products, arithmetic and copies ran while one was open for 0% of the time, Pallas kernels for 0%

profile of v4, /device:TPU:4, one launch (start us, length us, event | category | flops | bytes accessed | tf_op | source)
XLA Modules:
  0.0 32.8 jit_solution(9422928830569573521)
XLA Ops:
  0.0 0.0 copy-start
  0.0 0.3 shard_map.17
  0.3 0.8 %copy-done = f32[1,12,12,1024]{3,0,2,1:T(1,128)S(1)} copy-done((f32[1,12,12,1024]{3,0,2,1:T(1,128)S(1)}, f32[1,12,12,1024]{3,0,2,1:T(1,128)}, u32[]{:S(2)}) %copy-start) | copy-done | bytes 589848
  1.1 1.3 %shard_map.18 = (f32[8,144,128]{2,1,0:T(8,128)S(1)}, f32[8,72,128]{2,1,0:T(8,128)S(1)}, f32[528,128]{1,0:T(8,128)S(1)}, f32[432,128]{1,0:T(8,128)S(1)}, f32[96,128]{1,0:T(8,128)S(1)}) custom-call(f32[1152,128]{1,0:T(8,128)S(1)} %bitcast.2, bf16[512,256]{1,0:T(8,128)(2,1)S(1)} %get-tuple-element.18.fine_ref, bf16[768,256]{1,0:T(8,128)(2,1)S(1)} %get-tuple-element.19.low_ref), custom_call_target="tpu_custom_call" | custom-call | tf_op jit(solution)/shard_map/pallas_call | solution.py:315
  2.3 0.1 collective-permute-start
  2.4 1.5 %collective-permute-done.near_ref = f32[528,128]{1,0:T(8,128)S(1)} collective-permute-done((f32[528,128]{1,0:T(8,128)S(1)}, f32[528,128]{1,0:T(8,128)S(1)}, u32[]{:S(2)}, u32[]{:S(2)}) %collective-permute-start) | collective-permute-done | bytes 270368 | tf_op jit(solution)/shard_map/ppermute | solution.py:333
  4.0 8.6 %collective-permute-start.1 = (f32[432,128]{1,0:T(8,128)S(1)}, f32[432,128]{1,0:T(8,128)S(1)}, u32[]{:S(2)}, u32[]{:S(2)}) collective-permute-start(f32[432,128]{1,0:T(8,128)S(1)} %shard_map.19), channel_id=1, source_target_pairs={{0,31},{1,2},{2,1},{3,4},{4,3},{5,6},{6,5},{7,8},{8,7},{9,10},{10,... | collective-permute-start | bytes 663560 | tf_op jit(solution)/shard_map/ppermute | solution.py:333
  12.6 0.7 %collective-permute-start.2 = (f32[96,128]{1,0:T(8,128)S(1)}, f32[96,128]{1,0:T(8,128)S(1)}, u32[]{:S(2)}, u32[]{:S(2)}) collective-permute-start(f32[96,128]{1,0:T(8,128)S(1)} %get-tuple-element.24), channel_id=1, source_target_pairs={{0,30},{1,3},{2,0},{3,5},{4,2},{5,7},{6,4},{7,9},{8,6},{9,11},{10,... | collective-permute-start | bytes 147464 | tf_op jit(solution)/shard_map/ppermute | solution.py:333
  13.3 6.2 %collective-permute-done.2.far_ref = f32[96,128]{1,0:T(8,128)S(1)} collective-permute-done((f32[96,128]{1,0:T(8,128)S(1)}, f32[96,128]{1,0:T(8,128)S(1)}, u32[]{:S(2)}, u32[]{:S(2)}) %collective-permute-start.2) | collective-permute-done | bytes 49184 | tf_op jit(solution)/shard_map/ppermute | solution.py:333
  19.5 0.0 collective-permute-done.1.other_ref
  19.5 1.4 %shard_map.20 = (f32[8,192,128]{2,1,0:T(8,128)S(1)}, f32[8,48,128]{2,1,0:T(8,128)S(1)}, f32[432,128]{1,0:T(8,128)S(1)}, f32[432,128]{1,0:T(8,128)S(1)}, f32[48,128]{1,0:T(8,128)S(1)}, /*index=5*/f32[48,128]{1,0:T(8,128)S(1)}) custom-call(f32[8,144,128]{2,1,0:T(8,128)S(1)} %get-tuple-element.20.a_ref, f32[8,72,128]{2,1,0:T(8,128)S(1)} %get-tuple-element.21.b_ref, ...), custom_call_target="tpu_custom_call" | custom-call | tf_op jit(solution)/shard_map/pallas_call | solution.py:315
  21.0 1.3 %collective-permute-start.3 = (f32[432,128]{1,0:T(8,128)S(1)}, f32[432,128]{1,0:T(8,128)S(1)}, u32[]{:S(2)}, u32[]{:S(2)}) collective-permute-start(f32[432,128]{1,0:T(8,128)S(1)} %get-tuple-element.27), channel_id=1, source_target_pairs={{0,32},{1,33},{2,34},{3,35},{4,36},{5,37},{6,38},{7,39},{8,40},{9,... | collective-permute-start | bytes 663560 | tf_op jit(solution)/shard_map/ppermute | solution.py:333
  22.2 0.0 collective-permute-start.4
  22.2 3.0 %collective-permute-start.5 = (f32[48,128]{1,0:T(8,128)S(1)}, f32[48,128]{1,0:T(8,128)S(1)}, u32[]{:S(2)}, u32[]{:S(2)}) collective-permute-start(f32[48,128]{1,0:T(8,128)S(1)} %get-tuple-element.29), channel_id=1, source_target_pairs={{0,64},{1,65},{2,66},{3,67},{4,68},{5,69},{6,70},{7,71},{8,72},{9,... | collective-permute-start | bytes 73736 | tf_op jit(solution)/shard_map/ppermute | solution.py:333
  25.2 0.8 %collective-permute-start.6 = (f32[48,128]{1,0:T(8,128)S(1)}, f32[48,128]{1,0:T(8,128)S(1)}, u32[]{:S(2)}, u32[]{:S(2)}) collective-permute-start(f32[48,128]{1,0:T(8,128)S(1)} %get-tuple-element.30), channel_id=1, source_target_pairs={{0,192},{1,193},{2,194},{3,195},{4,196},{5,197},{6,198},{7,199},{8... | collective-permute-start | bytes 73736 | tf_op jit(solution)/shard_map/ppermute | solution.py:333
  26.0 1.6 %collective-permute-done.5.xfar_ref = f32[48,128]{1,0:T(8,128)S(1)} collective-permute-done((f32[48,128]{1,0:T(8,128)S(1)}, f32[48,128]{1,0:T(8,128)S(1)}, u32[]{:S(2)}, u32[]{:S(2)}) %collective-permute-start.5) | collective-permute-done | bytes 24608 | tf_op jit(solution)/shard_map/ppermute | solution.py:333
  27.7 3.7 %collective-permute-done.6.xfar2_ref = f32[48,128]{1,0:T(8,128)S(1)} collective-permute-done((f32[48,128]{1,0:T(8,128)S(1)}, f32[48,128]{1,0:T(8,128)S(1)}, u32[]{:S(2)}, u32[]{:S(2)}) %collective-permute-start.6) | collective-permute-done | bytes 24608 | tf_op jit(solution)/shard_map/ppermute | solution.py:333
  31.4 0.0 collective-permute-done.3.xnear_ref
  31.4 0.0 collective-permute-done.4.xother_ref
  31.4 1.4 %shard_map.21 = f32[1152,128]{1,0:T(8,128)} custom-call(f32[8,192,128]{2,1,0:T(8,128)S(1)} %get-tuple-element.25.ya_ref, f32[8,48,128]{2,1,0:T(8,128)S(1)} %get-tuple-element.26.yb_ref, f32[432,128]{1,0:T(8,128)S(1)} %collective-permute-done.3.xnear_ref, f32[432,128]{1,0:T(8,128)S(1)} %collective-permute-done.4.xother_ref, ...), custom_call_target="tpu_custom_call" | custom-call | tf_op jit(solution)/shard_map/pallas_call | solution.py:315
  (1 shorter events, 0.0 us)
Async XLA Ops:
  0.0 1.1 %copy-start = (f32[1,12,12,1024]{3,0,2,1:T(1,128)S(1)}, f32[1,12,12,1024]{3,0,2,1:T(1,128)}, u32[]{:S(2)}) copy-start(f32[1,12,12,1024]{3,0,2,1:T(1,128)} %param.1) | copy-start | bytes 1769476
  2.3 1.6 %collective-permute-start = (f32[528,128]{1,0:T(8,128)S(1)}, f32[528,128]{1,0:T(8,128)S(1)}, u32[]{:S(2)}, u32[]{:S(2)}) collective-permute-start(f32[528,128]{1,0:T(8,128)S(1)} %get-tuple-element.22), channel_id=1, source_target_pairs={{0,1},{1,0},{2,3},{3,2},{4,5},{5,4},{6,7},{7,6},{8,9},{9,8},{10,11... | collective-permute-start | bytes 811016 | tf_op jit(solution)/shard_map/ppermute | solution.py:333
  4.0 15.5 %collective-permute-start.1 = (f32[432,128]{1,0:T(8,128)S(1)}, f32[432,128]{1,0:T(8,128)S(1)}, u32[]{:S(2)}, u32[]{:S(2)}) collective-permute-start(f32[432,128]{1,0:T(8,128)S(1)} %shard_map.19), channel_id=1, source_target_pairs={{0,31},{1,2},{2,1},{3,4},{4,3},{5,6},{6,5},{7,8},{8,7},{9,10},{10,... | collective-permute-start | bytes 663560 | tf_op jit(solution)/shard_map/ppermute | solution.py:333
  12.6 6.9 %collective-permute-start.2 = (f32[96,128]{1,0:T(8,128)S(1)}, f32[96,128]{1,0:T(8,128)S(1)}, u32[]{:S(2)}, u32[]{:S(2)}) collective-permute-start(f32[96,128]{1,0:T(8,128)S(1)} %get-tuple-element.24), channel_id=1, source_target_pairs={{0,30},{1,3},{2,0},{3,5},{4,2},{5,7},{6,4},{7,9},{8,6},{9,11},{10,... | collective-permute-start | bytes 147464 | tf_op jit(solution)/shard_map/ppermute | solution.py:333
  21.0 10.5 %collective-permute-start.3 = (f32[432,128]{1,0:T(8,128)S(1)}, f32[432,128]{1,0:T(8,128)S(1)}, u32[]{:S(2)}, u32[]{:S(2)}) collective-permute-start(f32[432,128]{1,0:T(8,128)S(1)} %get-tuple-element.27), channel_id=1, source_target_pairs={{0,32},{1,33},{2,34},{3,35},{4,36},{5,37},{6,38},{7,39},{8,40},{9,... | collective-permute-start | bytes 663560 | tf_op jit(solution)/shard_map/ppermute | solution.py:333
  22.2 9.2 %collective-permute-start.4 = (f32[432,128]{1,0:T(8,128)S(1)}, f32[432,128]{1,0:T(8,128)S(1)}, u32[]{:S(2)}, u32[]{:S(2)}) collective-permute-start(f32[432,128]{1,0:T(8,128)S(1)} %get-tuple-element.28), channel_id=1, source_target_pairs={{0,224},{1,225},{2,226},{3,227},{4,228},{5,229},{6,230},{7,231},{8... | collective-permute-start | bytes 663560 | tf_op jit(solution)/shard_map/ppermute | solution.py:333
  22.2 5.4 %collective-permute-start.5 = (f32[48,128]{1,0:T(8,128)S(1)}, f32[48,128]{1,0:T(8,128)S(1)}, u32[]{:S(2)}, u32[]{:S(2)}) collective-permute-start(f32[48,128]{1,0:T(8,128)S(1)} %get-tuple-element.29), channel_id=1, source_target_pairs={{0,64},{1,65},{2,66},{3,67},{4,68},{5,69},{6,70},{7,71},{8,72},{9,... | collective-permute-start | bytes 73736 | tf_op jit(solution)/shard_map/ppermute | solution.py:333
  25.2 6.2 %collective-permute-start.6 = (f32[48,128]{1,0:T(8,128)S(1)}, f32[48,128]{1,0:T(8,128)S(1)}, u32[]{:S(2)}, u32[]{:S(2)}) collective-permute-start(f32[48,128]{1,0:T(8,128)S(1)} %get-tuple-element.30), channel_id=1, source_target_pairs={{0,192},{1,193},{2,194},{3,195},{4,196},{5,197},{6,198},{7,199},{8... | collective-permute-start | bytes 73736 | tf_op jit(solution)/shard_map/ppermute | solution.py:333

commit v5 on v4

--- a/solution.py
+++ b/solution.py
@@ -120,11 +120,19 @@
     return high, mid, (rest - mid.astype(jnp.float32)).astype(jnp.bfloat16)
 
 
-def banded(tiles, m, start, count):
-    chosen = [tiles[(start + i) % TILES] for i in range(count)]
-    return sum(
-        jnp.dot(jnp.concatenate(p, axis=1), m, preferred_element_type=jnp.float32) for p in zip(*chosen)
-    )
+def banded(tiles, m, starts, count):
+    rows = tiles[0][0].shape[0]
+    stacked = jnp.concatenate(
+        [
+            jnp.concatenate([tiles[(start + i) % TILES][part] for i in range(count)], axis=1)
+            for part in range(3)
+            for start in starts
+        ],
+        axis=0,
+    )
+    out = jnp.dot(stacked, m, preferred_element_type=jnp.float32)
+    at_part = lambda part, n: out[(part * len(starts) + n) * rows:(part * len(starts) + n + 1) * rows]
+    return [at_part(0, n) + (at_part(1, n) + at_part(2, n)) for n in range(len(starts))]
 
 
 NEAR, EDGE, Y_FAR, X_FAR = 66, 54, 12, 6
@@ -160,13 +168,12 @@
 def first_kernel(f_ref, fine_ref, low_ref, a_ref, b_ref, near_ref, other_ref, far_ref, v_ref):
     odd_core = lax.axis_index("span") % 2 == 1
     tiles = [parts(f_ref[pl.ds(t, PLANES * ROWS, stride=TILES), :]) for t in range(TILES)]
-    for q in range(4):
-        block = banded(tiles, fine_ref[...], 2 * q - 1, 4)
+    for q, block in enumerate([banded(tiles, fine_ref[...], (start,), 4)[0] for start in (-1, 1, 3, 5)]):
         for t in range(2):
             a_ref[2 * q + t] = block[:, t * LANES:(t + 1) * LANES]
     tiles = [parts(a_ref[t]) for t in range(TILES)]
-    for q in range(2):
-        v_ref[:, pl.ds(256 * q, 256)] = banded(tiles, low_ref[...], 4 * q - 1, 6)
+    for q, block in enumerate([banded(tiles, low_ref[...], (start,), 6)[0] for start in (-1, 3)]):
+        v_ref[:, pl.ds(256 * q, 256)] = block
     for t in range(TILES):
         for k in range(PAIRS):
             b_ref[t, pl.ds(k * ROWS, ROWS), :] = v_ref[pl.ds((2 * k + t // 4) * ROWS, ROWS), cut(t % 4)]
@@ -193,34 +200,66 @@
         put_rows(out_ref, 36, plus(get_rows(other_ref, 36, PAIRS, 3, t), terms), t)
 
 
-def middle_kernel(a_ref, b_ref, near_ref, other_ref, far_ref, low_ref, ya_ref, yb_ref, xnear_ref, xother_ref, xfar_ref, xfar2_ref, halo_ref):
+def low_rows(ref, low_ref, halo_ref):
+    tiles = [parts(get_rows(ref, 0, 48, 1, t)[0]) for t in range(TILES)]
+    for q, low in enumerate(banded(tiles, low_ref[...], (-1, 3), 6)):
+        for t in range(2):
+            halo_ref[2 * q + t] = low[:, t * LANES:(t + 1) * LANES]
+
+
+def low_halo(halo_ref, t):
+    return [halo_ref[t % 4, pl.ds(PLANES * j + t // 4, PAIRS, stride=2), :] for j in range(3)]
+
+
+def one_side(odd, rows):
+    zeros = [jnp.zeros_like(row) for row in rows]
+    return choose(odd, rows, zeros), choose(odd, zeros, rows)
+
+
+def near_kernel(a_ref, b_ref, near_ref, low_ref, ya_ref, s_ref, halo_ref):
+    odd_core = lax.axis_index("span") % 2 == 1
+    low_rows(near_ref, low_ref, halo_ref)
+    for t in range(TILES):
+        a, b = span_edges(a_ref, b_ref, t)
+        left, right = one_side(odd_core, get_rows(near_ref, 0, PLANES, 3, t))
+        smooth, detail = lift(left, a, right)
+        for c in range(PAIRS):
+            ya_ref[t, pl.ds(c, PLANES, stride=16), :] = smooth[c]
+            ya_ref[t, pl.ds(8 + c, PLANES, stride=16), :] = detail[c]
+        left, right = one_side(odd_core, low_halo(halo_ref, t))
+        smooth, _ = lift(left, b, right)
+        left, right = one_side(odd_core, get_rows(near_ref, 36, PAIRS, 3, t))
+        to_right, to_left = coarse_terms(b)
+        rows = smooth + plus(left, edge_right(to_left)) + plus(right, edge_left(to_right))
+        for j, row in enumerate(rows):
+            s_ref[t, pl.ds(8 * j, PAIRS), :] = row
+
+
+def middle_kernel(near_ya_ref, s_ref, other_ref, far_ref, low_ref, ya_ref, yb_ref, xnear_ref, xother_ref, xfar_ref, xfar2_ref, halo_ref):
     odd_core = lax.axis_index("span") % 2 == 1
     odd_x = lax.axis_index("stream") % 2 == 1
     odd_pair = lax.axis_index("stream") // 2 % 2 == 1
-    for side, ref in ((0, near_ref), (1, other_ref)):
-        tiles = [parts(get_rows(ref, 0, 48, 1, t)[0]) for t in range(TILES)]
-        for q in range(2):
-            low = banded(tiles, low_ref[...], 4 * q - 1, 6)
-            for t in range(2):
-                halo_ref[2 * q + t, pl.ds(side * 48, 48), :] = low[:, t * LANES:(t + 1) * LANES]
-    for t in range(TILES):
-        a, b = span_edges(a_ref, b_ref, t)
-        near, other = (get_rows(ref, 0, PLANES, 3, t) for ref in (near_ref, other_ref))
-        smooth, detail = lift(choose(odd_core, near, other), a, choose(odd_core, other, near))
-        for c in range(PAIRS):
-            ya_ref[t, pl.ds(c, PLANES, stride=16), :] = smooth[c]
-            ya_ref[t, pl.ds(8 + c, PLANES, stride=16), :] = detail[c]
-        near, other = (
-            [halo_ref[t % 4, pl.ds(48 * side + PLANES * j + t // 4, PAIRS, stride=2), :] for j in range(3)] for side in (0, 1)
-        )
-        smooth, _ = lift(choose(odd_core, near, other), b, choose(odd_core, other, near))
-        to_right, to_left = coarse_terms(b)
-        near, other = (get_rows(ref, 36, PAIRS, 3, t) for ref in (near_ref, other_ref))
+    low_rows(other_ref, low_ref, halo_ref)
+    for t in range(TILES):
+        right, left = one_side(odd_core, get_rows(other_ref, 0, PLANES, 3, t))
+        smooth, detail = lift(left, [None] * ROWS, right)
+        for start, terms in ((0, smooth), (8, detail)):
+            for c, term in enumerate(terms):
+                rows = pl.ds(start + c, PLANES, stride=16)
+                if term is not None:
+                    ya_ref[t, rows, :] = near_ya_ref[t, rows, :] + term
+                else:
+                    ya_ref[t, rows, :] = near_ya_ref[t, rows, :]
+        held = [s_ref[t, pl.ds(8 * j, PAIRS), :] for j in range(12)]
+        right, left = one_side(odd_core, low_halo(halo_ref, t))
+        terms, _ = lift(left, [None] * ROWS, right)
+        smooth = plus(held[:6], terms)
+        right, left = one_side(odd_core, get_rows(other_ref, 36, PAIRS, 3, t))
         one, two = get_rows(far_ref, 0, PAIRS, 2, t)
         zero = jnp.zeros_like(one)
-        left = plus(choose(odd_core, near, other), choose(odd_core, [one, zero, two], [zero, zero, zero]))
-        right = plus(choose(odd_core, other, near), choose(odd_core, [zero, zero, zero], [zero, one, zero]))
-        smooth, detail = lift(plus(left, edge_right(to_left)), smooth, plus(right, edge_left(to_right)))
+        left = plus(plus(left, held[6:9]), choose(odd_core, [one, zero, two], [zero, zero, zero]))
+        right = plus(plus(right, held[9:12]), choose(odd_core, [zero, zero, zero], [zero, one, zero]))
+        smooth, detail = lift(left, smooth, right)
         for c, row in enumerate(interleaved(smooth, detail)):
             yb_ref[t, pl.ds(c, PAIRS, stride=8), :] = row
     for t in range(TILES):
@@ -345,11 +384,18 @@
     far = send(far, lambda s, y: (s, y + (2 if y % 2 else -2)))
     (other,) = call(fold_kernel, [message(EDGE)], [other, near])
     other = send(other, lambda s, y: (s, y + (1 if y % 2 else -1)))
+    ya, smooth = call(
+        near_kernel,
+        [(TILES, PLANES * 16, LANES), (TILES, 96, LANES)],
+        [a, b, near, low],
+        [(4, 48, LANES)],
+        cost=cost,
+    )
     ya, yb, xnear, xother, xfar, xfar2 = call(
         middle_kernel,
         [(TILES, PLANES * 16, LANES), (TILES, PAIRS * 8, LANES), message(EDGE), message(EDGE), message(X_FAR), message(X_FAR)],
-        [a, b, near, other, far, low],
-        [(4, 96, LANES)],
+        [ya, smooth, other, far, low],
+        [(4, 48, LANES)],
     )
     xnear = send(xnear, lambda s, y: (s ^ 1, y))
     xother = send(xother, lambda s, y: (s + (1 if s % 2 else -1), y))

time: 33.3 us -> 32.7 us (0.982)
  waiting for transfers between devices: 13.1 us -> 12.4 us
    ppermute x7, waiting for transfers between devices: 13.1 us -> 12.4 us  [send(): return lax.ppermute(rows, ('stream', 'span'), pairs)]
    pallas_call x5 -> x6, Pallas kernels: 4.43 us -> 4.47 us  [call(): pl.pallas_call(kernel, out_shape=[jax.ShapeDtypeStruct(s, kind) for s in...]
  transfers between devices with their start and end apart: 7 -> 7, of which waited for: 4 -> 4; matrix products, arithmetic and copies ran while one was open for 0% -> 0% of each run, Pallas kernels for 0% -> 2%
where the time goes in v5:
time: 32.7 us; the launch traced here: 32.2 us
  starting transfers between devices  14.5 us (44%)
  waiting for transfers between devices  12.4 us (38%)
  Pallas kernels  4.47 us (14%)
  local copies, waits for them, and re-layouts  0.75 us (2%)
    ppermute x7, starting transfers between devices, send(): return lax.ppermute(rows, ('stream', 'span'), pairs)  14.5 us
    ppermute x7, waiting for transfers between devices, send(): return lax.ppermute(rows, ('stream', 'span'), pairs)  12.4 us
    pallas_call x6, Pallas kernels, call(): pl.pallas_call(kernel, out_shape=[jax.ShapeDtypeStruct(s, kind) for s in...  4.47 us
    unnamed x2, local copies, waits for them, and re-layouts  0.75 us
  transfers between devices with their start and end apart: 7, of which 4 were waited for; matrix products, arithmetic and copies ran while one was open for 0% of the time, Pallas kernels for 2%

profile of v5, /device:TPU:4, one launch (start us, length us, event | category | flops | bytes accessed | tf_op | source)
XLA Modules:
  0.0 32.2 jit_solution(5760824867648062629)
XLA Ops:
  0.0 0.0 copy-start
  0.0 0.3 shard_map.17
  0.3 0.8 %copy-done = f32[1,12,12,1024]{3,0,2,1:T(1,128)S(1)} copy-done((f32[1,12,12,1024]{3,0,2,1:T(1,128)S(1)}, f32[1,12,12,1024]{3,0,2,1:T(1,128)}, u32[]{:S(2)}) %copy-start) | copy-done | bytes 589848
  1.1 1.3 %shard_map.18 = (f32[8,144,128]{2,1,0:T(8,128)S(1)}, f32[8,72,128]{2,1,0:T(8,128)S(1)}, f32[528,128]{1,0:T(8,128)S(1)}, f32[432,128]{1,0:T(8,128)S(1)}, f32[96,128]{1,0:T(8,128)S(1)}) custom-call(f32[1152,128]{1,0:T(8,128)S(1)} %bitcast.2, bf16[512,256]{1,0:T(8,128)(2,1)S(1)} %get-tuple-element.20.fine_ref, bf16[768,256]{1,0:T(8,128)(2,1)S(1)} %get-tuple-element.21.low_ref), custom_call_target="tpu_custom_call" | custom-call | tf_op jit(solution)/shard_map/pallas_call | solution.py:354
  2.3 0.1 collective-permute-start
  2.4 1.5 %collective-permute-done.near_ref = f32[528,128]{1,0:T(8,128)S(1)} collective-permute-done((f32[528,128]{1,0:T(8,128)S(1)}, f32[528,128]{1,0:T(8,128)S(1)}, u32[]{:S(2)}, u32[]{:S(2)}) %collective-permute-start) | collective-permute-done | bytes 270368 | tf_op jit(solution)/shard_map/ppermute | solution.py:372
  4.0 8.6 %collective-permute-start.1 = (f32[432,128]{1,0:T(8,128)S(1)}, f32[432,128]{1,0:T(8,128)S(1)}, u32[]{:S(2)}, u32[]{:S(2)}) collective-permute-start(f32[432,128]{1,0:T(8,128)S(1)} %shard_map.20), channel_id=1, source_target_pairs={{0,31},{1,2},{2,1},{3,4},{4,3},{5,6},{6,5},{7,8},{8,7},{9,10},{10,... | collective-permute-start | bytes 663560 | tf_op jit(solution)/shard_map/ppermute | solution.py:372
  12.6 0.7 %collective-permute-start.2 = (f32[96,128]{1,0:T(8,128)S(1)}, f32[96,128]{1,0:T(8,128)S(1)}, u32[]{:S(2)}, u32[]{:S(2)}) collective-permute-start(f32[96,128]{1,0:T(8,128)S(1)} %get-tuple-element.28), channel_id=1, source_target_pairs={{0,30},{1,3},{2,0},{3,5},{4,2},{5,7},{6,4},{7,9},{8,6},{9,11},{10,... | collective-permute-start | bytes 147464 | tf_op jit(solution)/shard_map/ppermute | solution.py:372
  13.3 0.7 %shard_map.19 = (f32[8,192,128]{2,1,0:T(8,128)S(1)}, f32[8,96,128]{2,1,0:T(8,128)S(1)}) custom-call(f32[8,144,128]{2,1,0:T(8,128)S(1)} %get-tuple-element.22.a_ref, f32[8,72,128]{2,1,0:T(8,128)S(1)} %get-tuple-element.23.b_ref, f32[528,128]{1,0:T(8,128)S(1)} %collective-permute-done.near_ref, bf16[768,256]{1,0:T(8,128)(2,1)S(1)} %get-tuple-element.21.low_ref), custom_call_target="tpu_custom_call" | custom-call | flops 1000000000 | bytes 1000000 | tf_op jit(solution)/shard_map/pallas_call | solution.py:354
  14.0 5.5 %collective-permute-done.2.far_ref = f32[96,128]{1,0:T(8,128)S(1)} collective-permute-done((f32[96,128]{1,0:T(8,128)S(1)}, f32[96,128]{1,0:T(8,128)S(1)}, u32[]{:S(2)}, u32[]{:S(2)}) %collective-permute-start.2) | collective-permute-done | bytes 49184 | tf_op jit(solution)/shard_map/ppermute | solution.py:372
  19.5 0.0 collective-permute-done.1.other_ref
  19.5 0.8 %shard_map.21 = (f32[8,192,128]{2,1,0:T(8,128)S(1)}, f32[8,48,128]{2,1,0:T(8,128)S(1)}, f32[432,128]{1,0:T(8,128)S(1)}, f32[432,128]{1,0:T(8,128)S(1)}, f32[48,128]{1,0:T(8,128)S(1)}, /*index=5*/f32[48,128]{1,0:T(8,128)S(1)}) custom-call(f32[8,192,128]{2,1,0:T(8,128)S(1)} %get-tuple-element.25.near_ya_ref, f32[8,96,128]{2,1,0:T(8,128)S(1)} %get-tuple-element.26.s_ref, ...), custom_call_target="tpu_custom_call" | custom-call | tf_op jit(solution)/shard_map/pallas_call | solution.py:354
  20.3 1.3 %collective-permute-start.3 = (f32[432,128]{1,0:T(8,128)S(1)}, f32[432,128]{1,0:T(8,128)S(1)}, u32[]{:S(2)}, u32[]{:S(2)}) collective-permute-start(f32[432,128]{1,0:T(8,128)S(1)} %get-tuple-element.31), channel_id=1, source_target_pairs={{0,32},{1,33},{2,34},{3,35},{4,36},{5,37},{6,38},{7,39},{8,40},{9,... | collective-permute-start | bytes 663560 | tf_op jit(solution)/shard_map/ppermute | solution.py:372
  21.6 0.0 collective-permute-start.4
  21.6 3.0 %collective-permute-start.5 = (f32[48,128]{1,0:T(8,128)S(1)}, f32[48,128]{1,0:T(8,128)S(1)}, u32[]{:S(2)}, u32[]{:S(2)}) collective-permute-start(f32[48,128]{1,0:T(8,128)S(1)} %get-tuple-element.33), channel_id=1, source_target_pairs={{0,64},{1,65},{2,66},{3,67},{4,68},{5,69},{6,70},{7,71},{8,72},{9,... | collective-permute-start | bytes 73736 | tf_op jit(solution)/shard_map/ppermute | solution.py:372
  24.6 0.8 %collective-permute-start.6 = (f32[48,128]{1,0:T(8,128)S(1)}, f32[48,128]{1,0:T(8,128)S(1)}, u32[]{:S(2)}, u32[]{:S(2)}) collective-permute-start(f32[48,128]{1,0:T(8,128)S(1)} %get-tuple-element.34), channel_id=1, source_target_pairs={{0,192},{1,193},{2,194},{3,195},{4,196},{5,197},{6,198},{7,199},{8... | collective-permute-start | bytes 73736 | tf_op jit(solution)/shard_map/ppermute | solution.py:372
  25.4 1.6 %collective-permute-done.5.xfar_ref = f32[48,128]{1,0:T(8,128)S(1)} collective-permute-done((f32[48,128]{1,0:T(8,128)S(1)}, f32[48,128]{1,0:T(8,128)S(1)}, u32[]{:S(2)}, u32[]{:S(2)}) %collective-permute-start.5) | collective-permute-done | bytes 24608 | tf_op jit(solution)/shard_map/ppermute | solution.py:372
  27.1 3.7 %collective-permute-done.6.xfar2_ref = f32[48,128]{1,0:T(8,128)S(1)} collective-permute-done((f32[48,128]{1,0:T(8,128)S(1)}, f32[48,128]{1,0:T(8,128)S(1)}, u32[]{:S(2)}, u32[]{:S(2)}) %collective-permute-start.6) | collective-permute-done | bytes 24608 | tf_op jit(solution)/shard_map/ppermute | solution.py:372
  30.8 0.0 collective-permute-done.3.xnear_ref
  30.8 0.0 collective-permute-done.4.xother_ref
  30.8 1.4 %shard_map.22 = f32[1152,128]{1,0:T(8,128)} custom-call(f32[8,192,128]{2,1,0:T(8,128)S(1)} %get-tuple-element.29.ya_ref, f32[8,48,128]{2,1,0:T(8,128)S(1)} %get-tuple-element.30.yb_ref, f32[432,128]{1,0:T(8,128)S(1)} %collective-permute-done.3.xnear_ref, f32[432,128]{1,0:T(8,128)S(1)} %collective-permute-done.4.xother_ref, ...), custom_call_target="tpu_custom_call" | custom-call | tf_op jit(solution)/shard_map/pallas_call | solution.py:354
  (1 shorter events, 0.0 us)
Async XLA Ops:
  0.0 1.1 %copy-start = (f32[1,12,12,1024]{3,0,2,1:T(1,128)S(1)}, f32[1,12,12,1024]{3,0,2,1:T(1,128)}, u32[]{:S(2)}) copy-start(f32[1,12,12,1024]{3,0,2,1:T(1,128)} %param.1) | copy-start | bytes 1769476
  2.3 1.6 %collective-permute-start = (f32[528,128]{1,0:T(8,128)S(1)}, f32[528,128]{1,0:T(8,128)S(1)}, u32[]{:S(2)}, u32[]{:S(2)}) collective-permute-start(f32[528,128]{1,0:T(8,128)S(1)} %get-tuple-element.24), channel_id=1, source_target_pairs={{0,1},{1,0},{2,3},{3,2},{4,5},{5,4},{6,7},{7,6},{8,9},{9,8},{10,11... | collective-permute-start | bytes 811016 | tf_op jit(solution)/shard_map/ppermute | solution.py:372
  4.0 15.5 %collective-permute-start.1 = (f32[432,128]{1,0:T(8,128)S(1)}, f32[432,128]{1,0:T(8,128)S(1)}, u32[]{:S(2)}, u32[]{:S(2)}) collective-permute-start(f32[432,128]{1,0:T(8,128)S(1)} %shard_map.20), channel_id=1, source_target_pairs={{0,31},{1,2},{2,1},{3,4},{4,3},{5,6},{6,5},{7,8},{8,7},{9,10},{10,... | collective-permute-start | bytes 663560 | tf_op jit(solution)/shard_map/ppermute | solution.py:372
  12.6 6.9 %collective-permute-start.2 = (f32[96,128]{1,0:T(8,128)S(1)}, f32[96,128]{1,0:T(8,128)S(1)}, u32[]{:S(2)}, u32[]{:S(2)}) collective-permute-start(f32[96,128]{1,0:T(8,128)S(1)} %get-tuple-element.28), channel_id=1, source_target_pairs={{0,30},{1,3},{2,0},{3,5},{4,2},{5,7},{6,4},{7,9},{8,6},{9,11},{10,... | collective-permute-start | bytes 147464 | tf_op jit(solution)/shard_map/ppermute | solution.py:372
  20.3 10.5 %collective-permute-start.3 = (f32[432,128]{1,0:T(8,128)S(1)}, f32[432,128]{1,0:T(8,128)S(1)}, u32[]{:S(2)}, u32[]{:S(2)}) collective-permute-start(f32[432,128]{1,0:T(8,128)S(1)} %get-tuple-element.31), channel_id=1, source_target_pairs={{0,32},{1,33},{2,34},{3,35},{4,36},{5,37},{6,38},{7,39},{8,40},{9,... | collective-permute-start | bytes 663560 | tf_op jit(solution)/shard_map/ppermute | solution.py:372
  21.6 9.2 %collective-permute-start.4 = (f32[432,128]{1,0:T(8,128)S(1)}, f32[432,128]{1,0:T(8,128)S(1)}, u32[]{:S(2)}, u32[]{:S(2)}) collective-permute-start(f32[432,128]{1,0:T(8,128)S(1)} %get-tuple-element.32), channel_id=1, source_target_pairs={{0,224},{1,225},{2,226},{3,227},{4,228},{5,229},{6,230},{7,231},{8... | collective-permute-start | bytes 663560 | tf_op jit(solution)/shard_map/ppermute | solution.py:372
  21.6 5.4 %collective-permute-start.5 = (f32[48,128]{1,0:T(8,128)S(1)}, f32[48,128]{1,0:T(8,128)S(1)}, u32[]{:S(2)}, u32[]{:S(2)}) collective-permute-start(f32[48,128]{1,0:T(8,128)S(1)} %get-tuple-element.33), channel_id=1, source_target_pairs={{0,64},{1,65},{2,66},{3,67},{4,68},{5,69},{6,70},{7,71},{8,72},{9,... | collective-permute-start | bytes 73736 | tf_op jit(solution)/shard_map/ppermute | solution.py:372
  24.6 6.2 %collective-permute-start.6 = (f32[48,128]{1,0:T(8,128)S(1)}, f32[48,128]{1,0:T(8,128)S(1)}, u32[]{:S(2)}, u32[]{:S(2)}) collective-permute-start(f32[48,128]{1,0:T(8,128)S(1)} %get-tuple-element.34), channel_id=1, source_target_pairs={{0,192},{1,193},{2,194},{3,195},{4,196},{5,197},{6,198},{7,199},{8... | collective-permute-start | bytes 73736 | tf_op jit(solution)/shard_map/ppermute | solution.py:372

commit v6 on v5

--- a/solution.py
+++ b/solution.py
@@ -290,44 +290,57 @@
     return [yb_ref[t + 4 * odd, pl.ds(8 * k, 8), :] for k in range(PAIRS) for odd in (0, 1)]
 
 
-def last_kernel(ya_ref, yb_ref, xnear_ref, xother_ref, xfar_ref, xfar2_ref, out_ref, la_ref, lb_ref, c_ref, o_ref, sems):
+def rows_of(x, y, t):
+    return pl.ds((x * ROWS + y) * TILES + t, PAIRS, stride=2 * TILES)
+
+
+def own_kernel(ya_ref, yb_ref, part_ref, s_ref):
+    for t in range(TILES):
+        for x, plane in enumerate(interleaved(*lift(None, stream_planes(ya_ref, t), None))):
+            part_ref[rows_of(x, 0, t), :] = plane[0:6]
+            part_ref[rows_of(x, 1, t), :] = plane[8:14]
+    for t in range(4):
+        b = low_planes(yb_ref, t)
+        smooth, _ = lift(None, b, None)
+        to_right, to_left = coarse_terms(b)
+        for j, row in enumerate(smooth + edge_right(to_left) + edge_left(to_right)):
+            s_ref[t, pl.ds(8 * j, 8), :] = row
+
+
+def last_kernel(part_ref, s_ref, xnear_ref, xother_ref, xfar_ref, xfar2_ref, out_ref, c_ref, o_ref, sems):
     odd_x = lax.axis_index("stream") % 2 == 1
     odd_pair = lax.axis_index("stream") // 2 % 2 == 1
 
-    def rows_of(x, y, t):
-        return pl.ds((x * ROWS + y) * TILES + t, PAIRS, stride=2 * TILES)
-
-    def leave(x):
+    def leave(ref, x):
         rows = pl.ds(x * ROWS * TILES, ROWS * TILES)
-        copy = pltpu.make_async_copy(o_ref.at[rows], out_ref.at[rows], sems.at[x])
+        copy = pltpu.make_async_copy(ref.at[rows], out_ref.at[rows], sems.at[x])
         copy.start()
         return copy
 
+    apart = (3, 5, 7)
+    copies = [leave(part_ref, x) for x in apart]
     for t in range(TILES):
         near, other = (get_rows(ref, 0, 6, 6, t) for ref in (xnear_ref, xother_ref))
-        for j, row in enumerate(choose(odd_x, near, other) + choose(odd_x, other, near)):
-            la_ref[t, pl.ds(8 * j, 6), :] = row
-        a = stream_planes(ya_ref, t)
-        halo = [la_ref[t, pl.ds(16 * j, 16), :] for j in range(6)]
-        for x, plane in enumerate(interleaved(*lift(halo[:3], a, halo[3:]))):
-            o_ref[rows_of(x, 0, t), :] = plane[0:6]
-            o_ref[rows_of(x, 1, t), :] = plane[8:14]
-    copies = [leave(x) for x in range(1, PLANES, 2)]
+        left, right = choose(odd_x, near, other), choose(odd_x, other, near)
+        for y in (0, 1):
+            terms = interleaved(*lift(left[y::2], [None] * PLANES, right[y::2]))
+            for x, term in enumerate(terms):
+                if x not in apart:
+                    rows = rows_of(x, y, t)
+                    o_ref[rows, :] = total(part_ref[rows, :], term)
+    copies += [leave(o_ref, x) for x in range(1, PLANES, 2) if x not in apart]
     for t in range(4):
-        b = low_planes(yb_ref, t)
         near, other = (get_rows(ref, 36, 6, 3, t) + get_rows(ref, 36, 6, 3, t + 4) for ref in (xnear_ref, xother_ref))
         far, far2 = (get_rows(ref, 0, 6, 1, t) + get_rows(ref, 0, 6, 1, t + 4) for ref in (xfar_ref, xfar2_ref))
-        rows = choose(odd_x, near, other) + choose(odd_x, other, near)
-        rows += choose(odd_pair, far, far2) + choose(odd_pair, far2, far)[:1]
-        for j, row in enumerate(rows):
-            lb_ref[t, pl.ds(8 * j, 6), :] = row
-        halo = [lb_ref[t, pl.ds(8 * j, 8), :] for j in range(15)]
-        smooth, _ = lift(halo[0:3], b, halo[6:9])
-        to_right, to_left = coarse_terms(b)
-        left = plus(plus(halo[3:6], edge_right(to_left)), [halo[12], None, halo[13]])
-        right = plus(plus(halo[9:12], edge_left(to_right)), [None, halo[14], None])
+        left, right = choose(odd_x, near, other), choose(odd_x, other, near)
+        far_left, far_right = choose(odd_pair, far, far2), choose(odd_pair, far2, far)
+        held = [s_ref[t, pl.ds(8 * j, 6), :] for j in range(12)]
+        terms, _ = lift(left[:3], [None] * PLANES, right[:3])
+        smooth = plus(held[:6], terms)
+        left = plus(plus(left[3:], held[6:9]), [far_left[0], None, far_left[1]])
+        right = plus(plus(right[3:], held[9:12]), [None, far_right[0], None])
         for k, plane in enumerate(interleaved(*lift(left, smooth, right))):
-            c_ref[pl.ds(8 * k, 8), cut(t)] = plane
+            c_ref[pl.ds(8 * k, 6), cut(t)] = plane
     i, j = (lax.broadcasted_iota(jnp.int32, (LANES, 2 * LANES), axis) for axis in (0, 1))
     spread = jnp.where(j == 2 * i, 1.0, 0.0).astype(jnp.bfloat16)
     even = (lane((6, LANES)) & 1) == 0
@@ -341,7 +354,7 @@
                 rows = rows_of(2 * k, 0, t + half)
                 coarse = wide[8 * k:8 * k + 6, half * LANES:(half + 1) * LANES]
                 o_ref[rows, :] = jnp.where(even, coarse, o_ref[rows, :])
-    copies += [leave(x) for x in range(0, PLANES, 2)]
+    copies += [leave(o_ref, x) for x in range(0, PLANES, 2)]
     for copy in copies:
         copy.wait()
 
@@ -401,11 +414,12 @@
     xother = send(xother, lambda s, y: (s + (1 if s % 2 else -1), y))
     xfar = send(xfar, lambda s, y: (s + (-2 if s // 2 % 2 else 2), y))
     xfar2 = send(xfar2, lambda s, y: (s + (2 if s // 2 % 2 else -2), y))
+    part, smooth = call(own_kernel, [block, (4, 96, LANES)], [ya, yb], cost=cost)
     (out,) = call(
         last_kernel,
         [block],
-        [ya, yb, xnear, xother, xfar, xfar2],
-        [(TILES, 96, LANES), (4, 120, LANES), (48, CELLS // 2), block],
+        [part, smooth, xnear, xother, xfar, xfar2],
+        [(48, CELLS // 2), block],
         sems=PLANES,
         out=HBM,
     )

time: 32.7 us -> 32.6 us (level)
    pallas_call x6 -> x7, Pallas kernels: 4.47 us -> 4.69 us  [call(): pl.pallas_call(kernel, out_shape=[jax.ShapeDtypeStruct(s, kind) for s in...]
  transfers between devices with their start and end apart: 7 -> 7, of which waited for: 4 -> 4; matrix products, arithmetic and copies ran while one was open for 0% -> 0% of each run, Pallas kernels for 2% -> 3%
where the time goes in v6:
time: 32.6 us; the launch traced here: 32.1 us
  starting transfers between devices  14.5 us (44%)
  waiting for transfers between devices  12.1 us (37%)
  Pallas kernels  4.69 us (14%)
  local copies, waits for them, and re-layouts  0.75 us (2%)
    ppermute x7, starting transfers between devices, send(): return lax.ppermute(rows, ('stream', 'span'), pairs)  14.5 us
    ppermute x7, waiting for transfers between devices, send(): return lax.ppermute(rows, ('stream', 'span'), pairs)  12.1 us
    pallas_call x7, Pallas kernels, call(): pl.pallas_call(kernel, out_shape=[jax.ShapeDtypeStruct(s, kind) for s in...  4.69 us
    unnamed x2, local copies, waits for them, and re-layouts  0.75 us
  transfers between devices with their start and end apart: 7, of which 4 were waited for; matrix products, arithmetic and copies ran while one was open for 0% of the time, Pallas kernels for 3%

profile of v6, /device:TPU:4, one launch (start us, length us, event | category | flops | bytes accessed | tf_op | source)
XLA Modules:
  0.0 32.1 jit_solution(13867689097089634917)
XLA Ops:
  0.0 0.0 copy-start
  0.0 0.3 shard_map.17
  0.3 0.8 %copy-done = f32[1,12,12,1024]{3,0,2,1:T(1,128)S(1)} copy-done((f32[1,12,12,1024]{3,0,2,1:T(1,128)S(1)}, f32[1,12,12,1024]{3,0,2,1:T(1,128)}, u32[]{:S(2)}) %copy-start) | copy-done | bytes 589848
  1.1 1.3 %shard_map.18 = (f32[8,144,128]{2,1,0:T(8,128)S(1)}, f32[8,72,128]{2,1,0:T(8,128)S(1)}, f32[528,128]{1,0:T(8,128)S(1)}, f32[432,128]{1,0:T(8,128)S(1)}, f32[96,128]{1,0:T(8,128)S(1)}) custom-call(f32[1152,128]{1,0:T(8,128)S(1)} %bitcast.2, bf16[512,256]{1,0:T(8,128)(2,1)S(1)} %get-tuple-element.22.fine_ref, bf16[768,256]{1,0:T(8,128)(2,1)S(1)} %get-tuple-element.23.low_ref), custom_call_target="tpu_custom_call" | custom-call | tf_op jit(solution)/shard_map/pallas_call | solution.py:367
  2.3 0.1 collective-permute-start
  2.4 1.5 %collective-permute-done.near_ref = f32[528,128]{1,0:T(8,128)S(1)} collective-permute-done((f32[528,128]{1,0:T(8,128)S(1)}, f32[528,128]{1,0:T(8,128)S(1)}, u32[]{:S(2)}, u32[]{:S(2)}) %collective-permute-start) | collective-permute-done | bytes 270368 | tf_op jit(solution)/shard_map/ppermute | solution.py:385
  4.0 8.6 %collective-permute-start.1 = (f32[432,128]{1,0:T(8,128)S(1)}, f32[432,128]{1,0:T(8,128)S(1)}, u32[]{:S(2)}, u32[]{:S(2)}) collective-permute-start(f32[432,128]{1,0:T(8,128)S(1)} %shard_map.20), channel_id=1, source_target_pairs={{0,31},{1,2},{2,1},{3,4},{4,3},{5,6},{6,5},{7,8},{8,7},{9,10},{10,... | collective-permute-start | bytes 663560 | tf_op jit(solution)/shard_map/ppermute | solution.py:385
  12.6 0.7 %collective-permute-start.2 = (f32[96,128]{1,0:T(8,128)S(1)}, f32[96,128]{1,0:T(8,128)S(1)}, u32[]{:S(2)}, u32[]{:S(2)}) collective-permute-start(f32[96,128]{1,0:T(8,128)S(1)} %get-tuple-element.30), channel_id=1, source_target_pairs={{0,30},{1,3},{2,0},{3,5},{4,2},{5,7},{6,4},{7,9},{8,6},{9,11},{10,... | collective-permute-start | bytes 147464 | tf_op jit(solution)/shard_map/ppermute | solution.py:385
  13.3 0.7 %shard_map.19 = (f32[8,192,128]{2,1,0:T(8,128)S(1)}, f32[8,96,128]{2,1,0:T(8,128)S(1)}) custom-call(f32[8,144,128]{2,1,0:T(8,128)S(1)} %get-tuple-element.24.a_ref, f32[8,72,128]{2,1,0:T(8,128)S(1)} %get-tuple-element.25.b_ref, f32[528,128]{1,0:T(8,128)S(1)} %collective-permute-done.near_ref, bf16[768,256]{1,0:T(8,128)(2,1)S(1)} %get-tuple-element.23.low_ref), custom_call_target="tpu_custom_call" | custom-call | flops 1000000000 | bytes 1000000 | tf_op jit(solution)/shard_map/pallas_call | solution.py:367
  14.0 5.5 %collective-permute-done.2.far_ref = f32[96,128]{1,0:T(8,128)S(1)} collective-permute-done((f32[96,128]{1,0:T(8,128)S(1)}, f32[96,128]{1,0:T(8,128)S(1)}, u32[]{:S(2)}, u32[]{:S(2)}) %collective-permute-start.2) | collective-permute-done | bytes 49184 | tf_op jit(solution)/shard_map/ppermute | solution.py:385
  19.5 0.0 collective-permute-done.1.other_ref
  19.5 0.8 %shard_map.21 = (f32[8,192,128]{2,1,0:T(8,128)S(1)}, f32[8,48,128]{2,1,0:T(8,128)S(1)}, f32[432,128]{1,0:T(8,128)S(1)}, f32[432,128]{1,0:T(8,128)S(1)}, f32[48,128]{1,0:T(8,128)S(1)}, /*index=5*/f32[48,128]{1,0:T(8,128)S(1)}) custom-call(f32[8,192,128]{2,1,0:T(8,128)S(1)} %get-tuple-element.27.near_ya_ref, f32[8,96,128]{2,1,0:T(8,128)S(1)} %get-tuple-element.28.s_ref, ...), custom_call_target="tpu_custom_call" | custom-call | tf_op jit(solution)/shard_map/pallas_call | solution.py:367
  20.3 1.3 %collective-permute-start.3 = (f32[432,128]{1,0:T(8,128)S(1)}, f32[432,128]{1,0:T(8,128)S(1)}, u32[]{:S(2)}, u32[]{:S(2)}) collective-permute-start(f32[432,128]{1,0:T(8,128)S(1)} %get-tuple-element.35), channel_id=1, source_target_pairs={{0,32},{1,33},{2,34},{3,35},{4,36},{5,37},{6,38},{7,39},{8,40},{9,... | collective-permute-start | bytes 663560 | tf_op jit(solution)/shard_map/ppermute | solution.py:385
  21.6 0.0 collective-permute-start.4
  21.6 3.0 %collective-permute-start.5 = (f32[48,128]{1,0:T(8,128)S(1)}, f32[48,128]{1,0:T(8,128)S(1)}, u32[]{:S(2)}, u32[]{:S(2)}) collective-permute-start(f32[48,128]{1,0:T(8,128)S(1)} %get-tuple-element.37), channel_id=1, source_target_pairs={{0,64},{1,65},{2,66},{3,67},{4,68},{5,69},{6,70},{7,71},{8,72},{9,... | collective-permute-start | bytes 73736 | tf_op jit(solution)/shard_map/ppermute | solution.py:385
  24.6 0.8 %collective-permute-start.6 = (f32[48,128]{1,0:T(8,128)S(1)}, f32[48,128]{1,0:T(8,128)S(1)}, u32[]{:S(2)}, u32[]{:S(2)}) collective-permute-start(f32[48,128]{1,0:T(8,128)S(1)} %get-tuple-element.38), channel_id=1, source_target_pairs={{0,192},{1,193},{2,194},{3,195},{4,196},{5,197},{6,198},{7,199},{8... | collective-permute-start | bytes 73736 | tf_op jit(solution)/shard_map/ppermute | solution.py:385
  25.4 0.3 shard_map.22
  25.7 1.3 %collective-permute-done.5.xfar_ref = f32[48,128]{1,0:T(8,128)S(1)} collective-permute-done((f32[48,128]{1,0:T(8,128)S(1)}, f32[48,128]{1,0:T(8,128)S(1)}, u32[]{:S(2)}, u32[]{:S(2)}) %collective-permute-start.5) | collective-permute-done | bytes 24608 | tf_op jit(solution)/shard_map/ppermute | solution.py:385
  27.1 3.7 %collective-permute-done.6.xfar2_ref = f32[48,128]{1,0:T(8,128)S(1)} collective-permute-done((f32[48,128]{1,0:T(8,128)S(1)}, f32[48,128]{1,0:T(8,128)S(1)}, u32[]{:S(2)}, u32[]{:S(2)}) %collective-permute-start.6) | collective-permute-done | bytes 24608 | tf_op jit(solution)/shard_map/ppermute | solution.py:385
  30.8 0.0 collective-permute-done.3.xnear_ref
  30.8 0.0 collective-permute-done.4.xother_ref
  30.8 1.3 %shard_map.23 = f32[1152,128]{1,0:T(8,128)} custom-call(f32[1152,128]{1,0:T(8,128)S(1)} %get-tuple-element.33.part_ref, f32[4,96,128]{2,1,0:T(8,128)S(1)} %get-tuple-element.34.s_ref, f32[432,128]{1,0:T(8,128)S(1)} %collective-permute-done.3.xnear_ref, f32[432,128]{1,0:T(8,128)S(1)} %collective-permute-done.4.xother_ref, ...), custom_call_target="tpu_custom_call" | custom-call | tf_op jit(solution)/shard_map/pallas_call | solution.py:367
  (1 shorter events, 0.0 us)
Async XLA Ops:
  0.0 1.1 %copy-start = (f32[1,12,12,1024]{3,0,2,1:T(1,128)S(1)}, f32[1,12,12,1024]{3,0,2,1:T(1,128)}, u32[]{:S(2)}) copy-start(f32[1,12,12,1024]{3,0,2,1:T(1,128)} %param.1) | copy-start | bytes 1769476
  2.3 1.6 %collective-permute-start = (f32[528,128]{1,0:T(8,128)S(1)}, f32[528,128]{1,0:T(8,128)S(1)}, u32[]{:S(2)}, u32[]{:S(2)}) collective-permute-start(f32[528,128]{1,0:T(8,128)S(1)} %get-tuple-element.26), channel_id=1, source_target_pairs={{0,1},{1,0},{2,3},{3,2},{4,5},{5,4},{6,7},{7,6},{8,9},{9,8},{10,11... | collective-permute-start | bytes 811016 | tf_op jit(solution)/shard_map/ppermute | solution.py:385
  4.0 15.5 %collective-permute-start.1 = (f32[432,128]{1,0:T(8,128)S(1)}, f32[432,128]{1,0:T(8,128)S(1)}, u32[]{:S(2)}, u32[]{:S(2)}) collective-permute-start(f32[432,128]{1,0:T(8,128)S(1)} %shard_map.20), channel_id=1, source_target_pairs={{0,31},{1,2},{2,1},{3,4},{4,3},{5,6},{6,5},{7,8},{8,7},{9,10},{10,... | collective-permute-start | bytes 663560 | tf_op jit(solution)/shard_map/ppermute | solution.py:385
  12.6 6.9 %collective-permute-start.2 = (f32[96,128]{1,0:T(8,128)S(1)}, f32[96,128]{1,0:T(8,128)S(1)}, u32[]{:S(2)}, u32[]{:S(2)}) collective-permute-start(f32[96,128]{1,0:T(8,128)S(1)} %get-tuple-element.30), channel_id=1, source_target_pairs={{0,30},{1,3},{2,0},{3,5},{4,2},{5,7},{6,4},{7,9},{8,6},{9,11},{10,... | collective-permute-start | bytes 147464 | tf_op jit(solution)/shard_map/ppermute | solution.py:385
  20.3 10.5 %collective-permute-start.3 = (f32[432,128]{1,0:T(8,128)S(1)}, f32[432,128]{1,0:T(8,128)S(1)}, u32[]{:S(2)}, u32[]{:S(2)}) collective-permute-start(f32[432,128]{1,0:T(8,128)S(1)} %get-tuple-element.35), channel_id=1, source_target_pairs={{0,32},{1,33},{2,34},{3,35},{4,36},{5,37},{6,38},{7,39},{8,40},{9,... | collective-permute-start | bytes 663560 | tf_op jit(solution)/shard_map/ppermute | solution.py:385
  21.6 9.2 %collective-permute-start.4 = (f32[432,128]{1,0:T(8,128)S(1)}, f32[432,128]{1,0:T(8,128)S(1)}, u32[]{:S(2)}, u32[]{:S(2)}) collective-permute-start(f32[432,128]{1,0:T(8,128)S(1)} %get-tuple-element.36), channel_id=1, source_target_pairs={{0,224},{1,225},{2,226},{3,227},{4,228},{5,229},{6,230},{7,231},{8... | collective-permute-start | bytes 663560 | tf_op jit(solution)/shard_map/ppermute | solution.py:385
  21.6 5.4 %collective-permute-start.5 = (f32[48,128]{1,0:T(8,128)S(1)}, f32[48,128]{1,0:T(8,128)S(1)}, u32[]{:S(2)}, u32[]{:S(2)}) collective-permute-start(f32[48,128]{1,0:T(8,128)S(1)} %get-tuple-element.37), channel_id=1, source_target_pairs={{0,64},{1,65},{2,66},{3,67},{4,68},{5,69},{6,70},{7,71},{8,72},{9,... | collective-permute-start | bytes 73736 | tf_op jit(solution)/shard_map/ppermute | solution.py:385
  24.6 6.2 %collective-permute-start.6 = (f32[48,128]{1,0:T(8,128)S(1)}, f32[48,128]{1,0:T(8,128)S(1)}, u32[]{:S(2)}, u32[]{:S(2)}) collective-permute-start(f32[48,128]{1,0:T(8,128)S(1)} %get-tuple-element.38), channel_id=1, source_target_pairs={{0,192},{1,193},{2,194},{3,195},{4,196},{5,197},{6,198},{7,199},{8... | collective-permute-start | bytes 73736 | tf_op jit(solution)/shard_map/ppermute | solution.py:385

commit v7 on v6

--- a/solution.py
+++ b/solution.py
@@ -135,17 +135,24 @@
     return [at_part(0, n) + (at_part(1, n) + at_part(2, n)) for n in range(len(starts))]
 
 
-NEAR, EDGE, Y_FAR, X_FAR = 66, 54, 12, 6
+EDGE, Y_FAR, X_FAR = 54, 12, 6
+FIRST, SECOND = (0, 1, 2, 6, 8, 9, 10, 11), (3, 4, 5, 7)
 
 
 def at(count, t, start, size):
     return pl.ds(t * count + start, size)
 
 
-def span_edges(a_ref, b_ref, t):
-    a = [a_ref[t, pl.ds(y, PLANES, stride=ROWS), :] for y in range(ROWS)]
-    b = [b_ref[t, pl.ds(y, PAIRS, stride=ROWS), :] for y in range(ROWS)]
-    return a, b
+def fine_rows(refs, t):
+    found = {y: ref[t, pl.ds(PLANES * n, PLANES), :] for ref, ys in refs for n, y in enumerate(ys)}
+    return [found.get(y) for y in range(ROWS)]
+
+
+def deep_rows(refs, t):
+    found = {
+        y: ref[t % 4, pl.ds(PLANES * n + t // 4, PAIRS, stride=2), :] for ref, ys in refs for n, y in enumerate(ys)
+    }
+    return [found.get(y) for y in range(ROWS)]
 
 
 def put_rows(ref, start, rows, t):
@@ -165,36 +172,51 @@
     return [jnp.where(odd, x, y) for x, y in zip(a, b)]
 
 
-def first_kernel(f_ref, fine_ref, low_ref, a_ref, b_ref, near_ref, other_ref, far_ref, v_ref):
-    odd_core = lax.axis_index("span") % 2 == 1
-    tiles = [parts(f_ref[pl.ds(t, PLANES * ROWS, stride=TILES), :]) for t in range(TILES)]
-    for q, block in enumerate([banded(tiles, fine_ref[...], (start,), 4)[0] for start in (-1, 1, 3, 5)]):
+def lift_cells(f_ref, fine_ref, low_ref, ys, a_ref, b_ref):
+    for t in range(TILES):
+        for n, y in enumerate(ys):
+            a_ref[t, pl.ds(PLANES * n, PLANES), :] = f_ref[pl.ds(y * TILES + t, PLANES, stride=ROWS * TILES), :]
+    tiles = [parts(a_ref[t]) for t in range(TILES)]
+    for q, start in enumerate((-1, 1, 3, 5)):
+        (block,) = banded(tiles, fine_ref[...], (start,), 4)
         for t in range(2):
             a_ref[2 * q + t] = block[:, t * LANES:(t + 1) * LANES]
     tiles = [parts(a_ref[t]) for t in range(TILES)]
-    for q, block in enumerate([banded(tiles, low_ref[...], (start,), 6)[0] for start in (-1, 3)]):
-        v_ref[:, pl.ds(256 * q, 256)] = block
-    for t in range(TILES):
-        for k in range(PAIRS):
-            b_ref[t, pl.ds(k * ROWS, ROWS), :] = v_ref[pl.ds((2 * k + t // 4) * ROWS, ROWS), cut(t % 4)]
-    for t in range(TILES):
-        a, b = span_edges(a_ref, b_ref, t)
-        smooth, _ = lift(None, b, None)
-        to_right, to_left = coarse_terms(b)
+    for q, start in enumerate((-1, 3)):
+        (block,) = banded(tiles, low_ref[...], (start,), 6)
+        for t in range(2):
+            b_ref[2 * q + t] = block[:, t * LANES:(t + 1) * LANES]
+
+
+def first_kernel(f_ref, fine_ref, low_ref, a_ref, b_ref, behind_ref, far_ref):
+    odd_core = lax.axis_index("span") % 2 == 1
+    lift_cells(f_ref, fine_ref, low_ref, FIRST, a_ref, b_ref)
+    for t in range(TILES):
+        to_right, to_left = coarse_terms(deep_rows([(b_ref, FIRST)], t))
         far_right, far_left = edge_right(to_right), edge_left(to_left)
         far_right, far_left = [far_right[0], far_right[2]], [far_left[1], jnp.zeros_like(far_left[1])]
+        put_rows(behind_ref, 0, choose(odd_core, far_left, far_right), t)
+        put_rows(far_ref, 0, choose(odd_core, far_right, far_left), t)
+
+
+def second_kernel(f_ref, fine_ref, low_ref, a_ref, b_ref, a2_ref, b2_ref, near_ref, other_ref):
+    odd_core = lax.axis_index("span") % 2 == 1
+    lift_cells(f_ref, fine_ref, low_ref, SECOND, a2_ref, b2_ref)
+    for t in range(TILES):
+        a = fine_rows([(a_ref, FIRST), (a2_ref, SECOND)], t)
+        smooth, _ = lift(None, deep_rows([(b_ref, FIRST), (b2_ref, SECOND)], t), None)
         right = edge_right(a) + edge_right(smooth)
         left = edge_left(a) + edge_left(smooth)
-        put_rows(near_ref, 0, choose(odd_core, left + far_left, right + far_right), t)
+        put_rows(near_ref, 0, choose(odd_core, left, right), t)
         put_rows(other_ref, 0, choose(odd_core, right, left), t)
-        put_rows(far_ref, 0, choose(odd_core, far_right, far_left), t)
-
-
-def fold_kernel(other_ref, near_ref, out_ref):
+
+
+def fold_kernel(other_ref, behind_ref, near_ref, out_ref, near_out_ref):
     odd_core = lax.axis_index("span") % 2 == 1
     out_ref[...] = other_ref[...]
-    for t in range(TILES):
-        one, two = get_rows(near_ref, EDGE, PAIRS, 2, t)
+    near_out_ref[...] = near_ref[...]
+    for t in range(TILES):
+        one, two = get_rows(behind_ref, 0, PAIRS, 2, t)
         zero = jnp.zeros_like(one)
         terms = choose(odd_core, [one, zero, two], [zero, one, zero])
         put_rows(out_ref, 36, plus(get_rows(other_ref, 36, PAIRS, 3, t), terms), t)
@@ -216,11 +238,12 @@
     return choose(odd, rows, zeros), choose(odd, zeros, rows)
 
 
-def near_kernel(a_ref, b_ref, near_ref, low_ref, ya_ref, s_ref, halo_ref):
+def near_kernel(a_ref, b_ref, a2_ref, b2_ref, near_ref, low_ref, ya_ref, s_ref, halo_ref):
     odd_core = lax.axis_index("span") % 2 == 1
     low_rows(near_ref, low_ref, halo_ref)
     for t in range(TILES):
-        a, b = span_edges(a_ref, b_ref, t)
+        a = fine_rows([(a_ref, FIRST), (a2_ref, SECOND)], t)
+        b = deep_rows([(b_ref, FIRST), (b2_ref, SECOND)], t)
         left, right = one_side(odd_core, get_rows(near_ref, 0, PLANES, 3, t))
         smooth, detail = lift(left, a, right)
         for c in range(PAIRS):
@@ -380,6 +403,8 @@
 
 
 def local(streams, spans, fields):
+    shape = fields.shape
+
     def send(rows, target):
         pairs = [(s * spans + y, (lambda q: q[0] % streams * spans + q[1] % spans)(target(s, y))) for s in range(streams) for y in range(spans)]
         return lax.ppermute(rows, ("stream", "span"), pairs)
@@ -387,20 +412,21 @@
     cost = pl.CostEstimate(flops=10**9, bytes_accessed=10**6, transcendentals=0)
     fine, low = call(table_kernel, [(4 * LANES, 2 * LANES), (6 * LANES, 2 * LANES)], [], kind=jnp.bfloat16, cost=cost)
     block = (PLANES * ROWS * TILES, LANES)
-    a, b, near, other, far = call(
-        first_kernel,
-        [(TILES, PLANES * ROWS, LANES), (TILES, PAIRS * ROWS, LANES), message(NEAR), message(EDGE), message(Y_FAR)],
-        [fields.reshape(block), fine, low],
-        [(PLANES * ROWS, CELLS // 2)],
-    )
+    fields = fields.reshape(block)
+    shapes = lambda ys: [(TILES, PLANES * len(ys), LANES), (TILES // 2, PLANES * len(ys), LANES)]
+    a, b, behind, far = call(first_kernel, shapes(FIRST) + [message(Y_FAR)] * 2, [fields, fine, low])
+    behind = send(behind, lambda s, y: (s, y ^ 1))
+    far = send(far, lambda s, y: (s, y + (2 if y % 2 else -2)))
+    a2, b2, near, other = call(
+        second_kernel, shapes(SECOND) + [message(EDGE)] * 2, [fields, fine, low, a, b], cost=cost
+    )
+    other, near = call(fold_kernel, [message(EDGE)] * 2, [other, behind, near])
     near = send(near, lambda s, y: (s, y ^ 1))
-    far = send(far, lambda s, y: (s, y + (2 if y % 2 else -2)))
-    (other,) = call(fold_kernel, [message(EDGE)], [other, near])
     other = send(other, lambda s, y: (s, y + (1 if y % 2 else -1)))
     ya, smooth = call(
         near_kernel,
         [(TILES, PLANES * 16, LANES), (TILES, 96, LANES)],
-        [a, b, near, low],
+        [a, b, a2, b2, near, low],
         [(4, 48, LANES)],
         cost=cost,
     )
@@ -423,7 +449,7 @@
         sems=PLANES,
         out=HBM,
     )
-    return out.reshape(fields.shape)
+    return out.reshape(shape)
 
 
 def solution(mesh):

time: 32.6 us -> 32.4 us (level)
  waiting for transfers between devices: 12.1 us -> 11.1 us
  starting transfers between devices: 14.5 us -> 14.9 us
  Pallas kernels: 4.69 us -> 5.08 us
    ppermute x7 -> x8, waiting for transfers between devices: 12.1 us -> 11.1 us  [send(): return lax.ppermute(rows, ('stream', 'span'), pairs)]
    pallas_call x7 -> x8, Pallas kernels: 4.69 us -> 5.08 us  [call(): pl.pallas_call(kernel, out_shape=[jax.ShapeDtypeStruct(s, kind) for s in...]
    ppermute x7 -> x8, starting transfers between devices: 14.5 us -> 14.9 us  [send(): return lax.ppermute(rows, ('stream', 'span'), pairs)]
  transfers between devices with their start and end apart: 7 -> 8, of which waited for: 4 -> 4; matrix products, arithmetic and copies ran while one was open for 0% -> 0% of each run, Pallas kernels for 3% -> 5%
where the time goes in v7:
time: 32.4 us; the launch traced here: 31.9 us
  starting transfers between devices  14.9 us (46%)
  waiting for transfers between devices  11.1 us (34%)
  Pallas kernels  5.08 us (16%)
  local copies, waits for them, and re-layouts  0.75 us (2%)
    ppermute x8, starting transfers between devices, send(): return lax.ppermute(rows, ('stream', 'span'), pairs)  14.9 us
    ppermute x8, waiting for transfers between devices, send(): return lax.ppermute(rows, ('stream', 'span'), pairs)  11.1 us
    pallas_call x8, Pallas kernels, call(): pl.pallas_call(kernel, out_shape=[jax.ShapeDtypeStruct(s, kind) for s in...  5.08 us
    unnamed x2, local copies, waits for them, and re-layouts  0.75 us
  transfers between devices with their start and end apart: 8, of which 4 were waited for; matrix products, arithmetic and copies ran while one was open for 0% of the time, Pallas kernels for 5%

profile of v7, /device:TPU:4, one launch (start us, length us, event | category | flops | bytes accessed | tf_op | source)
XLA Modules:
  0.0 31.9 jit_solution(13357801574708208562)
XLA Ops:
  0.0 0.0 copy-start
  0.0 0.3 shard_map.17
  0.3 0.8 %copy-done = f32[1,12,12,1024]{3,0,2,1:T(1,128)S(1)} copy-done((f32[1,12,12,1024]{3,0,2,1:T(1,128)S(1)}, f32[1,12,12,1024]{3,0,2,1:T(1,128)}, u32[]{:S(2)}) %copy-start) | copy-done | bytes 589848
  1.1 1.0 %shard_map.18 = (f32[8,96,128]{2,1,0:T(8,128)S(1)}, f32[4,96,128]{2,1,0:T(8,128)S(1)}, f32[96,128]{1,0:T(8,128)S(1)}, f32[96,128]{1,0:T(8,128)S(1)}) custom-call(f32[1152,128]{1,0:T(8,128)S(1)} %bitcast.2, bf16[512,256]{1,0:T(8,128)(2,1)S(1)} %get-tuple-element.27.fine_ref, bf16[768,256]{1,0:T(8,128)(2,1)S(1)} %get-tuple-element.28.low_ref), custom_call_target="tpu_custom_call" | custom-call | tf_op jit(solution)/shard_map/pallas_call | solution.py:390
  2.0 0.1 collective-permute-start
  2.1 0.7 %shard_map.19 = (f32[8,48,128]{2,1,0:T(8,128)S(1)}, f32[4,48,128]{2,1,0:T(8,128)S(1)}, f32[432,128]{1,0:T(8,128)S(1)}, f32[432,128]{1,0:T(8,128)S(1)}) custom-call(f32[1152,128]{1,0:T(8,128)S(1)} %bitcast.3, bf16[512,256]{1,0:T(8,128)(2,1)S(1)} %get-tuple-element.27.fine_ref, bf16[768,256]{1,0:T(8,128)(2,1)S(1)} %get-tuple-element.28.low_ref, ...), custom_call_target="tpu_custom_call" | custom-call | flops 1000000000 | bytes 1000000 | tf_op jit(solution)/shard_map/pallas_call | solution.py:390
  2.9 0.5 %collective-permute-done.behind_ref = f32[96,128]{1,0:T(8,128)S(1)} collective-permute-done((f32[96,128]{1,0:T(8,128)S(1)}, f32[96,128]{1,0:T(8,128)S(1)}, u32[]{:S(2)}, u32[]{:S(2)}) %collective-permute-start) | collective-permute-done | bytes 49184 | tf_op jit(solution)/shard_map/ppermute | solution.py:410
  3.4 0.2 collective-permute-start.1
  3.7 8.7 %collective-permute-start.2 = (f32[432,128]{1,0:T(8,128)S(1)}, f32[432,128]{1,0:T(8,128)S(1)}, u32[]{:S(2)}, u32[]{:S(2)}) collective-permute-start(f32[432,128]{1,0:T(8,128)S(1)} %get-tuple-element.39), channel_id=1, source_target_pairs={{0,31},{1,2},{2,1},{3,4},{4,3},{5,6},{6,5},{7,8},{8,7},{9,10},{10,... | collective-permute-start | bytes 663560 | tf_op jit(solution)/shard_map/ppermute | solution.py:410
  12.4 0.7 %collective-permute-start.3 = (f32[96,128]{1,0:T(8,128)S(1)}, f32[96,128]{1,0:T(8,128)S(1)}, u32[]{:S(2)}, u32[]{:S(2)}) collective-permute-start(f32[96,128]{1,0:T(8,128)S(1)} %get-tuple-element.40), channel_id=1, source_target_pairs={{0,30},{1,3},{2,0},{3,5},{4,2},{5,7},{6,4},{7,9},{8,6},{9,11},{10,... | collective-permute-start | bytes 147464 | tf_op jit(solution)/shard_map/ppermute | solution.py:410
  13.1 0.0 collective-permute-done.1.near_ref
  13.1 0.6 %shard_map.21 = (f32[8,192,128]{2,1,0:T(8,128)S(1)}, f32[8,96,128]{2,1,0:T(8,128)S(1)}) custom-call(f32[8,96,128]{2,1,0:T(8,128)S(1)} %get-tuple-element.29.a_ref, f32[4,96,128]{2,1,0:T(8,128)S(1)} %get-tuple-element.30.b_ref, f32[8,48,128]{2,1,0:T(8,128)S(1)} %get-tuple-element.31.a2_ref, f32[4,48,128]{2,1,0:T(8,128)S(1)} %get-tuple-element.32.b2_ref, ...), custom_call_target="tpu_custom_call" | custom-call | flops 1000000000 | bytes 1000000 | tf_op jit(solution)/shard_map/pallas_call | solution.py:390
  13.8 5.5 %collective-permute-done.3.far_ref = f32[96,128]{1,0:T(8,128)S(1)} collective-permute-done((f32[96,128]{1,0:T(8,128)S(1)}, f32[96,128]{1,0:T(8,128)S(1)}, u32[]{:S(2)}, u32[]{:S(2)}) %collective-permute-start.3) | collective-permute-done | bytes 49184 | tf_op jit(solution)/shard_map/ppermute | solution.py:410
  19.3 0.0 collective-permute-done.2.other_ref
  19.3 0.8 %shard_map.22 = (f32[8,192,128]{2,1,0:T(8,128)S(1)}, f32[8,48,128]{2,1,0:T(8,128)S(1)}, f32[432,128]{1,0:T(8,128)S(1)}, f32[432,128]{1,0:T(8,128)S(1)}, f32[48,128]{1,0:T(8,128)S(1)}, /*index=5*/f32[48,128]{1,0:T(8,128)S(1)}) custom-call(f32[8,192,128]{2,1,0:T(8,128)S(1)} %get-tuple-element.37.near_ya_ref, f32[8,96,128]{2,1,0:T(8,128)S(1)} %get-tuple-element.38.s_ref, ...), custom_call_target="tpu_custom_call" | custom-call | tf_op jit(solution)/shard_map/pallas_call | solution.py:390
  20.1 1.3 %collective-permute-start.4 = (f32[432,128]{1,0:T(8,128)S(1)}, f32[432,128]{1,0:T(8,128)S(1)}, u32[]{:S(2)}, u32[]{:S(2)}) collective-permute-start(f32[432,128]{1,0:T(8,128)S(1)} %get-tuple-element.45), channel_id=1, source_target_pairs={{0,32},{1,33},{2,34},{3,35},{4,36},{5,37},{6,38},{7,39},{8,40},{9,... | collective-permute-start | bytes 663560 | tf_op jit(solution)/shard_map/ppermute | solution.py:410
  21.4 0.0 collective-permute-start.5
  21.4 3.0 %collective-permute-start.6 = (f32[48,128]{1,0:T(8,128)S(1)}, f32[48,128]{1,0:T(8,128)S(1)}, u32[]{:S(2)}, u32[]{:S(2)}) collective-permute-start(f32[48,128]{1,0:T(8,128)S(1)} %get-tuple-element.47), channel_id=1, source_target_pairs={{0,64},{1,65},{2,66},{3,67},{4,68},{5,69},{6,70},{7,71},{8,72},{9,... | collective-permute-start | bytes 73736 | tf_op jit(solution)/shard_map/ppermute | solution.py:410
  24.3 0.8 %collective-permute-start.7 = (f32[48,128]{1,0:T(8,128)S(1)}, f32[48,128]{1,0:T(8,128)S(1)}, u32[]{:S(2)}, u32[]{:S(2)}) collective-permute-start(f32[48,128]{1,0:T(8,128)S(1)} %get-tuple-element.48), channel_id=1, source_target_pairs={{0,192},{1,193},{2,194},{3,195},{4,196},{5,197},{6,198},{7,199},{8... | collective-permute-start | bytes 73736 | tf_op jit(solution)/shard_map/ppermute | solution.py:410
  25.2 0.3 shard_map.23
  25.5 1.3 %collective-permute-done.6.xfar_ref = f32[48,128]{1,0:T(8,128)S(1)} collective-permute-done((f32[48,128]{1,0:T(8,128)S(1)}, f32[48,128]{1,0:T(8,128)S(1)}, u32[]{:S(2)}, u32[]{:S(2)}) %collective-permute-start.6) | collective-permute-done | bytes 24608 | tf_op jit(solution)/shard_map/ppermute | solution.py:410
  26.8 3.7 %collective-permute-done.7.xfar2_ref = f32[48,128]{1,0:T(8,128)S(1)} collective-permute-done((f32[48,128]{1,0:T(8,128)S(1)}, f32[48,128]{1,0:T(8,128)S(1)}, u32[]{:S(2)}, u32[]{:S(2)}) %collective-permute-start.7) | collective-permute-done | bytes 24608 | tf_op jit(solution)/shard_map/ppermute | solution.py:410
  30.6 0.0 collective-permute-done.4.xnear_ref
  30.6 0.0 collective-permute-done.5.xother_ref
  30.6 1.3 %shard_map.24 = f32[1152,128]{1,0:T(8,128)} custom-call(f32[1152,128]{1,0:T(8,128)S(1)} %get-tuple-element.43.part_ref, f32[4,96,128]{2,1,0:T(8,128)S(1)} %get-tuple-element.44.s_ref, f32[432,128]{1,0:T(8,128)S(1)} %collective-permute-done.4.xnear_ref, f32[432,128]{1,0:T(8,128)S(1)} %collective-permute-done.5.xother_ref, ...), custom_call_target="tpu_custom_call" | custom-call | tf_op jit(solution)/shard_map/pallas_call | solution.py:390
  (1 shorter events, 0.0 us)
Async XLA Ops:
  0.0 1.1 %copy-start = (f32[1,12,12,1024]{3,0,2,1:T(1,128)S(1)}, f32[1,12,12,1024]{3,0,2,1:T(1,128)}, u32[]{:S(2)}) copy-start(f32[1,12,12,1024]{3,0,2,1:T(1,128)} %param.1) | copy-start | bytes 1769476
  2.0 1.3 %collective-permute-start = (f32[96,128]{1,0:T(8,128)S(1)}, f32[96,128]{1,0:T(8,128)S(1)}, u32[]{:S(2)}, u32[]{:S(2)}) collective-permute-start(f32[96,128]{1,0:T(8,128)S(1)} %get-tuple-element.34), channel_id=1, source_target_pairs={{0,1},{1,0},{2,3},{3,2},{4,5},{5,4},{6,7},{7,6},{8,9},{9,8},{10,11... | collective-permute-start | bytes 147464 | tf_op jit(solution)/shard_map/ppermute | solution.py:410
  3.4 9.7 %collective-permute-start.1 = (f32[432,128]{1,0:T(8,128)S(1)}, f32[432,128]{1,0:T(8,128)S(1)}, u32[]{:S(2)}, u32[]{:S(2)}) collective-permute-start(f32[432,128]{1,0:T(8,128)S(1)} %get-tuple-element.36), channel_id=1, source_target_pairs={{0,1},{1,0},{2,3},{3,2},{4,5},{5,4},{6,7},{7,6},{8,9},{9,8},{10,11... | collective-permute-start | bytes 663560 | tf_op jit(solution)/shard_map/ppermute | solution.py:410
  3.7 15.6 %collective-permute-start.2 = (f32[432,128]{1,0:T(8,128)S(1)}, f32[432,128]{1,0:T(8,128)S(1)}, u32[]{:S(2)}, u32[]{:S(2)}) collective-permute-start(f32[432,128]{1,0:T(8,128)S(1)} %get-tuple-element.39), channel_id=1, source_target_pairs={{0,31},{1,2},{2,1},{3,4},{4,3},{5,6},{6,5},{7,8},{8,7},{9,10},{10,... | collective-permute-start | bytes 663560 | tf_op jit(solution)/shard_map/ppermute | solution.py:410
  12.4 6.9 %collective-permute-start.3 = (f32[96,128]{1,0:T(8,128)S(1)}, f32[96,128]{1,0:T(8,128)S(1)}, u32[]{:S(2)}, u32[]{:S(2)}) collective-permute-start(f32[96,128]{1,0:T(8,128)S(1)} %get-tuple-element.40), channel_id=1, source_target_pairs={{0,30},{1,3},{2,0},{3,5},{4,2},{5,7},{6,4},{7,9},{8,6},{9,11},{10,... | collective-permute-start | bytes 147464 | tf_op jit(solution)/shard_map/ppermute | solution.py:410
  20.1 10.5 %collective-permute-start.4 = (f32[432,128]{1,0:T(8,128)S(1)}, f32[432,128]{1,0:T(8,128)S(1)}, u32[]{:S(2)}, u32[]{:S(2)}) collective-permute-start(f32[432,128]{1,0:T(8,128)S(1)} %get-tuple-element.45), channel_id=1, source_target_pairs={{0,32},{1,33},{2,34},{3,35},{4,36},{5,37},{6,38},{7,39},{8,40},{9,... | collective-permute-start | bytes 663560 | tf_op jit(solution)/shard_map/ppermute | solution.py:410
  21.4 9.2 %collective-permute-start.5 = (f32[432,128]{1,0:T(8,128)S(1)}, f32[432,128]{1,0:T(8,128)S(1)}, u32[]{:S(2)}, u32[]{:S(2)}) collective-permute-start(f32[432,128]{1,0:T(8,128)S(1)} %get-tuple-element.46), channel_id=1, source_target_pairs={{0,224},{1,225},{2,226},{3,227},{4,228},{5,229},{6,230},{7,231},{8... | collective-permute-start | bytes 663560 | tf_op jit(solution)/shard_map/ppermute | solution.py:410
  21.4 5.4 %collective-permute-start.6 = (f32[48,128]{1,0:T(8,128)S(1)}, f32[48,128]{1,0:T(8,128)S(1)}, u32[]{:S(2)}, u32[]{:S(2)}) collective-permute-start(f32[48,128]{1,0:T(8,128)S(1)} %get-tuple-element.47), channel_id=1, source_target_pairs={{0,64},{1,65},{2,66},{3,67},{4,68},{5,69},{6,70},{7,71},{8,72},{9,... | collective-permute-start | bytes 73736 | tf_op jit(solution)/shard_map/ppermute | solution.py:410
  24.3 6.2 %collective-permute-start.7 = (f32[48,128]{1,0:T(8,128)S(1)}, f32[48,128]{1,0:T(8,128)S(1)}, u32[]{:S(2)}, u32[]{:S(2)}) collective-permute-start(f32[48,128]{1,0:T(8,128)S(1)} %get-tuple-element.48), channel_id=1, source_target_pairs={{0,192},{1,193},{2,194},{3,195},{4,196},{5,197},{6,198},{7,199},{8... | collective-permute-start | bytes 73736 | tf_op jit(solution)/shard_map/ppermute | solution.py:410
